TPU v7x, 128 devices: a whole 4x4x4 slice. The times are simulated.
128 devices in a mesh: dp: 16 (over x, z_hi, core), seq: 8 (over z_lo, y).
Axes of the slice: x: 4, y: 4, z: 4 (z_hi: 2, z_lo: 2; z = z_hi * 2 + z_lo), core: 2. Of those that a mesh axis runs over, the one named last changes fastest.
Arguments:
- queries: bfloat16 [16, 1024, 4096], P('dp', 'seq'), may hold values from -6 to 6
- key_input: bfloat16 [16, 1024, 4096], P('dp', 'seq'), may hold values from -6 to 6
- value_input: bfloat16 [16, 1024, 4096], P('dp', 'seq'), may hold values from -6 to 6
- cotangent: bfloat16 [16, 1024, 4096], P('dp', 'seq'), may hold values from -6 to 6
- out_weight: bfloat16 [4096, 4096], P('dp', 'seq'), may hold values from -0.09375 to 0.09375
- filters: bfloat16 [256, 128], replicated, may hold values from -0.5 to 0.5
- skip_gain: float32 [4096], replicated, may hold values from -1 to 1
Outputs:
- grad_queries: bfloat16 [16, 1024, 4096], P('dp', 'seq')
- grad_keys: bfloat16 [16, 1024, 4096], P('dp', 'seq')
- grad_values: bfloat16 [16, 1024, 4096], P('dp', 'seq')
- grad_weight: float32 [4096, 4096], P('dp', 'seq')
- grad_filters: float32 [256, 128], P('seq')
- grad_gain: float32 [4096], P('seq')
All inputs are finite; a program needn't handle non-finite values.
Results may differ from a plain program's by a relative error of at most 0.0095.
Values may be sent and summed in bfloat16 or wider, within the bound.
No kernel may reach another device: no remote copies, remote signals or barrier semaphores. Data moves between devices by JAX's collectives and lax.ppermute only.
A program may use at most 192 MiB of HBM per device.

v0:
```python
import math

import jax
import jax.numpy as jnp
from jax import lax
from jax.sharding import PartitionSpec as P

GROUP = 16
TAPS = 128


def band_table(taps_rows, forward):
    groups = taps_rows.shape[0]
    if forward:
        base = jnp.concatenate(
            [
                jnp.zeros((groups, 1), taps_rows.dtype),
                taps_rows[:, ::-1],
                jnp.zeros((groups, TAPS), taps_rows.dtype),
            ],
            1,
        )
    else:
        base = jnp.concatenate([taps_rows, jnp.zeros((groups, TAPS + 1), taps_rows.dtype)], 1)
    repeated = jnp.tile(base, (1, TAPS))
    flat = repeated[:, : TAPS * 2 * TAPS]
    return flat.reshape(groups, TAPS, 2 * TAPS)


def block_windows(current, extra, before):
    width = current.shape[1]
    block_count = current.shape[0] // TAPS
    blocks = current.reshape(block_count, TAPS, width)
    if before:
        other = jnp.concatenate([extra[None], blocks[:-1]], 0)
        window = jnp.concatenate([other, blocks], 1)
    else:
        other = jnp.concatenate([blocks[1:], extra[None]], 0)
        window = jnp.concatenate([blocks, other], 1)
    return window.reshape(block_count, 2 * TAPS, width // GROUP, GROUP)


def conv_forward(product, before_rows, taps_rows):
    window = block_windows(product, before_rows, True)
    table = band_table(taps_rows, True)
    mixed = jnp.einsum("gts,bsgc->btgc", table, window, preferred_element_type=jnp.float32)
    return (mixed.reshape(product.shape), window)


def conv_backward(gradient, after_rows, taps_rows):
    window = block_windows(gradient, after_rows, False)
    table = band_table(taps_rows, False)
    result = jnp.einsum("gst,btgc->bsgc", table, window, preferred_element_type=jnp.float32)
    return result.reshape(gradient.shape)


def filter_terms(gradient, window):
    block_count, span, groups, members = window.shape
    grad_blocks = gradient.reshape(block_count, TAPS, groups, members)
    pairs = jnp.einsum("btgc,bsgc->gts", grad_blocks, window, preferred_element_type=jnp.float32)
    flat = pairs.reshape(groups, TAPS * 2 * TAPS)
    flat = jnp.pad(flat, ((0, 0), (0, TAPS)))
    skewed = flat.reshape(groups, TAPS, 2 * TAPS + 1)
    summed = jnp.sum(skewed[:, :, 1 : TAPS + 1], axis=1)
    return summed[:, ::-1]


def shards(queries, key_input, value_input, cotangent, out_weight, filters, skip_gain):
    seq_count = lax.axis_size("seq")
    data_count = lax.axis_size("dp")
    query_rows = queries[0]
    key_rows = key_input[0]
    value_rows = value_input[0]
    tok_rows, width = query_rows.shape
    length = tok_rows * seq_count
    scale = 1.0 / math.sqrt(data_count * length)
    panel = width // seq_count
    position = lax.axis_index("seq")
    grad_all = lax.all_gather(cotangent[0], "seq", axis=0, tiled=True)
    group_rows = panel // GROUP
    taps_panel = lax.dynamic_slice_in_dim(filters, position * group_rows, group_rows, 0)
    gain_panel = lax.dynamic_slice_in_dim(skip_gain, position * panel, panel, 0)
    query_c, key_c, value_c = (
        lax.all_to_all(query_rows, "seq", split_axis=1, concat_axis=0, tiled=True),
        lax.all_to_all(key_rows, "seq", split_axis=1, concat_axis=0, tiled=True),
        lax.all_to_all(value_rows, "seq", split_axis=1, concat_axis=0, tiled=True),
    )
    product = (key_c.astype(jnp.float32) * value_c.astype(jnp.float32)).astype(jnp.bfloat16)
    product_f = product.astype(jnp.float32)
    zero_rows = jnp.zeros((TAPS, panel), jnp.bfloat16)
    convolved, window = conv_forward(product, zero_rows, taps_panel)
    mixed = convolved + gain_panel * product_f
    gated = (query_c.astype(jnp.float32) * mixed).astype(jnp.bfloat16)
    columns = grad_all
    grad_gated = jnp.dot(
        columns,
        lax.all_gather(out_weight, "dp", axis=0, tiled=True),
        preferred_element_type=jnp.float32,
    )
    columns = grad_all
    grad_weight = lax.psum_scatter(
        lax.dot_general(
            columns, gated, (((0,), (0,)), ((), ())), preferred_element_type=jnp.float32
        )
        * scale,
        "dp",
        scatter_dimension=0,
        tiled=True,
    )
    grad_query = (grad_gated * mixed).astype(jnp.bfloat16)
    grad_mixed = (grad_gated * query_c.astype(jnp.float32)).astype(jnp.bfloat16)
    grad_mixed_f = grad_mixed.astype(jnp.float32)
    grad_product = conv_backward(grad_mixed, zero_rows, taps_panel) + gain_panel * grad_mixed_f
    grad_key = (grad_product * value_c.astype(jnp.float32)).astype(jnp.bfloat16)
    grad_value = (grad_product * key_c.astype(jnp.float32)).astype(jnp.bfloat16)
    filter_part = filter_terms(grad_mixed, window) * scale
    gain_part = jnp.sum(grad_mixed_f * product_f, 0) * scale
    grad_query, grad_key, grad_value = (
        lax.all_to_all(grad_query, "seq", split_axis=0, concat_axis=1, tiled=True),
        lax.all_to_all(grad_key, "seq", split_axis=0, concat_axis=1, tiled=True),
        lax.all_to_all(grad_value, "seq", split_axis=0, concat_axis=1, tiled=True),
    )
    grad_filters, grad_gain = lax.psum((filter_part, gain_part), "dp")
    return (
        grad_query[None],
        grad_key[None],
        grad_value[None],
        grad_weight,
        grad_filters,
        grad_gain,
    )


def solution(mesh):
    placed = (
        P("dp", "seq", None),
        P("dp", "seq", None),
        P("dp", "seq", None),
        P("dp", "seq", None),
        P("dp", "seq"),
        P(),
        P(),
    )
    return jax.shard_map(
        shards,
        mesh=mesh,
        in_specs=placed,
        out_specs=(
            P("dp", "seq", None),
            P("dp", "seq", None),
            P("dp", "seq", None),
            P("dp", "seq"),
            P("seq", None),
            P("seq"),
        ),
        check_vma=False,
    )
```

profile of v0, /device:TPU:8, one launch (start us, length us, event | category | flops | bytes accessed | tf_op | source)
XLA Modules:
  0.0 379.2 jit_solution(10522545832901023129)
XLA Ops:
  11.0 6.3 %all-to-all-start.1 = ((bf16[128,8,512]{0,2,1:T(8,128)(2,1)}), bf16[128,8,512]{0,2,1:T(8,128)(2,1)S(1)}, u32[]{:S(2)}, u32[]{:S(2)}) async-start(bf16[128,8,512]{0,2,1:T(8,128)(2,1)} %bitcast.4), calls=%async_computation.1 | async-start | bytes 2097152 | tf_op jit(solution)/shard_map/all_to_all | solution.py:86
  18.6 13.2 %all-to-all-done.1 = bf16[128,8,512]{0,2,1:T(8,128)(2,1)S(1)} async-done(((bf16[128,8,512]{0,2,1:T(8,128)(2,1)}), bf16[128,8,512]{0,2,1:T(8,128)(2,1)S(1)}, u32[]{:S(2)}, u32[]{:S(2)}) %all-to-all-start.1) | async-done | bytes 1048608 | tf_op jit(solution)/shard_map/all_to_all | solution.py:86
  31.8 5.9 %all-to-all-start = ((bf16[128,8,512]{0,2,1:T(8,128)(2,1)}), bf16[128,8,512]{0,2,1:T(8,128)(2,1)S(1)}, u32[]{:S(2)}, u32[]{:S(2)}) async-start(bf16[128,8,512]{0,2,1:T(8,128)(2,1)} %bitcast.1), calls=%async_computation | async-start | bytes 2097152 | tf_op jit(solution)/shard_map/all_to_all | solution.py:85
  39.6 12.9 %all-to-all-done = bf16[128,8,512]{0,2,1:T(8,128)(2,1)S(1)} async-done(((bf16[128,8,512]{0,2,1:T(8,128)(2,1)}), bf16[128,8,512]{0,2,1:T(8,128)(2,1)S(1)}, u32[]{:S(2)}, u32[]{:S(2)}) %all-to-all-start) | async-done | bytes 1048608 | tf_op jit(solution)/shard_map/all_to_all | solution.py:85
  52.4 5.3 %all-to-all-start.3 = ((bf16[128,8,512]{2,0,1:T(8,128)(2,1)}), bf16[128,8,512]{2,0,1:T(8,128)(2,1)}, u32[]{:S(2)}, u32[]{:S(2)}) async-start(bf16[128,8,512]{2,0,1:T(8,128)(2,1)} %copy.34), calls=%async_computation.3 | async-start | bytes 2097152 | tf_op jit(solution)/shard_map/all_to_all | solution.py:84
  58.1 4.5 %tile.9 = bf16[32,32896]{1,0:T(8,128)(2,1)} reshape(bf16[32,128,257]{2,1,0:T(8,128)(2,1)S(1)} %tile.8) | data formatting | bytes 4210688 | tf_op jit(solution)/shard_map/tile | solution.py:25
  66.3 4.5 %tile.21 = bf16[32,32896]{1,0:T(8,128)(2,1)} reshape(bf16[32,128,257]{2,1,0:T(8,128)(2,1)S(1)} %tile.20) | data formatting | bytes 4210688 | tf_op jit(solution)/shard_map/tile | solution.py:25
  76.4 3.0 copy.27
  80.8 2.9 copy.25
  86.3 88.4 %all-gather.6.cloned.1.call-done = bf16[1,1024,4096]{2,1,0:T(8,128)(2,1)} async-done(((bf16[1,128,4096]{2,1,0:T(8,128)(2,1)}), bf16[1,1024,4096]{2,1,0:T(8,128)(2,1)}) %all-gather.6.cloned.1.call-update) | async-done | bytes 8388624 | tf_op jit(solution)/shard_map/all_gather | solution.py:79
  174.7 12.1 %fusion.8 = (f32[512]{0:T(512)S(1)}, bf16[1024,512]{1,0:T(8,128)(2,1)S(1)}, bf16[1024,512]{1,0:T(8,128)(2,1)S(1)}, f32[1024,512]{1,0:T(8,128)}) fusion(bf16[128,8,512]{2,0,1:T(8,128)(2,1)} %all-to-all-done.3, f32[8,128,512]{2,1,0:T(8,128)} %copy.27, f32[8,128,512]{2,1,0:T(8,128)} %copy.25, bf16[4096,512]{1,0:T(8,128)(2,1)} %all-gather.4.cloned.1.call-done, ...), kind=kOutput, calls=%fused_computation.13 | convolution fusion | flops 4299685376 | bytes 22022144 | tf_op jit(solution)/shard_map/dot_general | solution.py:95
  191.9 2.7 fusion.25
  197.3 3.0 copy.32
  204.4 2.6 fusion.30
  209.7 2.9 copy.40
  212.6 7.7 %fusion.17 = (bf16[1024,512]{1,0:T(8,128)(2,1)S(1)}, bf16[1024,512]{1,0:T(8,128)(2,1)S(1)}, bf16[1024,512]{1,0:T(8,128)(2,1)}, bf16[1024,512]{1,0:T(8,128)(2,1)}) fusion(bf16[128,8,512]{2,0,1:T(8,128)(2,1)} %all-to-all-done.3, f32[1024,512]{1,0:T(8,128)} %copy.32, bf16[1024,512]{1,0:T(8,128)(2,1)} %copy-done.10, f32[512]{0:T(512)S(1)} %dynamic_slice.7, ...), kind=kLoop, calls=%fused_computation.28 | loop fusion | flops 7864320 | bytes 17827840 | tf_op jit(solution)/shard_map/convert_element_type | solution.py:93
  220.3 10.1 %multiply_bitcast_fusion = f32[4096,512]{0,1:T(8,128)} fusion(bf16[1024,512]{1,0:T(8,128)(2,1)S(1)} %get-tuple-element.23, bf16[1,1024,4096]{2,1,0:T(8,128)(2,1)} %all-gather.6.cloned.1.call-done), kind=kOutput, calls=%fused_computation.4 | convolution fusion | flops 4297064448 | bytes 17825792 | tf_op jit(solution)/shard_map/dot_general | solution.py:102
  230.5 20.8 %all_to_all.87 = bf16[8,128,512]{2,1,0:T(8,128)(2,1)} all-to-all(bf16[8,128,512]{2,1,0:T(8,128)(2,1)S(1)} %bitcast.117), channel_id=1, replica_groups=mesh['dp'=16,'seq'=8] {'seq'}, dimensions={0} | all-to-all | bytes 2097152 | tf_op jit(solution)/shard_map/all_to_all | solution.py:119
  251.2 5.3 %all-to-all-start.4 = ((bf16[8,128,512]{2,1,0:T(8,128)(2,1)}), bf16[8,128,512]{2,1,0:T(8,128)(2,1)}, u32[]{:S(2)}, u32[]{:S(2)}) async-start(bf16[8,128,512]{2,1,0:T(8,128)(2,1)} %bitcast.21), calls=%async_computation.4 | async-start | bytes 2097152 | tf_op jit(solution)/shard_map/all_to_all | solution.py:120
  258.4 12.1 %all-to-all-done.4 = bf16[8,128,512]{2,1,0:T(8,128)(2,1)} async-done(((bf16[8,128,512]{2,1,0:T(8,128)(2,1)}), bf16[8,128,512]{2,1,0:T(8,128)(2,1)}, u32[]{:S(2)}, u32[]{:S(2)}) %all-to-all-start.4) | async-done | bytes 1048608 | tf_op jit(solution)/shard_map/all_to_all | solution.py:120
  270.6 5.3 %all-to-all-start.5 = ((bf16[8,128,512]{2,1,0:T(8,128)(2,1)}), bf16[8,128,512]{2,1,0:T(8,128)(2,1)}, u32[]{:S(2)}, u32[]{:S(2)}) async-start(bf16[8,128,512]{2,1,0:T(8,128)(2,1)} %bitcast.116), calls=%async_computation.5 | async-start | bytes 2097152 | tf_op jit(solution)/shard_map/all_to_all | solution.py:121
  282.1 8.0 %reshape.86 = f32[32,128,257]{2,1,0:T(8,128)} reshape(f32[32,32896]{1,0:T(8,128)} %pad.7) | data formatting | bytes 8421376 | tf_op jit(solution)/shard_map/reshape | solution.py:63
  290.2 2.9 slice_reduce_fusion
  293.1 69.3 %all-reduce.4 = (f32[32,128]{1,0:T(8,128)}, f32[512]{0:T(512)}) all-reduce(f32[32,128]{1,0:T(8,128)S(1)} %broadcast_multiply_fusion, f32[512]{0:T(512)S(1)} %broadcast_multiply_fusion.1), channel_id=1, replica_groups=mesh['dp'=16,'seq'=8] {'dp'}, use_global_device_ids=true, to_apply=%region_2.3 | all-reduce | flops 4608 | bytes 36864 | tf_op jit(solution)/shard_map/psum | solution.py:123
  (88 shorter events, 53.7 us)
Async XLA Ops:
  7.2 32.2 %copy-start = (bf16[256,128]{1,0:T(8,128)(2,1)S(1)}, bf16[256,128]{1,0:T(8,128)(2,1)}, u32[]{:S(2)}) copy-start(bf16[256,128]{1,0:T(8,128)(2,1)} %param.12) | copy-start | bytes 196612
  7.2 79.1 %all-gather.4.cloned.1.call-start = ((), (), s32[]{:S(2)}) async-start(), calls=%async_computation.7 | async-start | bytes 4456448 | tf_op jit(solution)/shard_map/all_gather | solution.py:97
  7.9 166.8 %all-gather.6.cloned.1.call-start = ((), (), s32[]{:S(2)}) async-start(), calls=%async_computation.9 | async-start | bytes 9437184 | tf_op jit(solution)/shard_map/all_gather | solution.py:79
  8.7 8.6 %copy-start.12 = (bf16[1,128,4096]{2,1,0:T(8,128)(2,1)S(1)}, bf16[1,128,4096]{2,1,0:T(8,128)(2,1)}, u32[]{:S(2)}) copy-start(bf16[1,128,4096]{2,1,0:T(8,128)(2,1)} %param.8) | copy-start | bytes 3145732
  11.0 20.8 %all-to-all-start.1 = ((bf16[128,8,512]{0,2,1:T(8,128)(2,1)}), bf16[128,8,512]{0,2,1:T(8,128)(2,1)S(1)}, u32[]{:S(2)}, u32[]{:S(2)}) async-start(bf16[128,8,512]{0,2,1:T(8,128)(2,1)} %bitcast.4), calls=%async_computation.1 | async-start | bytes 2097152 | tf_op jit(solution)/shard_map/all_to_all | solution.py:86
  17.3 20.4 %copy-start.13 = (bf16[1,128,4096]{2,1,0:T(8,128)(2,1)S(1)}, bf16[1,128,4096]{2,1,0:T(8,128)(2,1)}, u32[]{:S(2)}) copy-start(bf16[1,128,4096]{2,1,0:T(8,128)(2,1)} %param.7) | copy-start | bytes 3145732
  31.8 6.3 %copy-start.2 = (bf16[128,8,512]{0,2,1:T(8,128)(2,1)}, bf16[128,8,512]{0,2,1:T(8,128)(2,1)S(1)}, u32[]{:S(2)}) copy-start(bf16[128,8,512]{0,2,1:T(8,128)(2,1)S(1)} %all-to-all-done.1) | copy-start | bytes 3145732
  31.8 20.6 %all-to-all-start = ((bf16[128,8,512]{0,2,1:T(8,128)(2,1)}), bf16[128,8,512]{0,2,1:T(8,128)(2,1)S(1)}, u32[]{:S(2)}, u32[]{:S(2)}) async-start(bf16[128,8,512]{0,2,1:T(8,128)(2,1)} %bitcast.1), calls=%async_computation | async-start | bytes 2097152 | tf_op jit(solution)/shard_map/all_to_all | solution.py:85
  52.4 5.4 %copy-start.4 = (bf16[128,8,512]{0,2,1:T(8,128)(2,1)}, bf16[128,8,512]{0,2,1:T(8,128)(2,1)S(1)}, u32[]{:S(2)}) copy-start(bf16[128,8,512]{0,2,1:T(8,128)(2,1)S(1)} %all-to-all-done) | copy-start | bytes 3145732
  52.4 31.6 %all-to-all-start.3 = ((bf16[128,8,512]{2,0,1:T(8,128)(2,1)}), bf16[128,8,512]{2,0,1:T(8,128)(2,1)}, u32[]{:S(2)}, u32[]{:S(2)}) async-start(bf16[128,8,512]{2,0,1:T(8,128)(2,1)} %copy.34), calls=%async_computation.3 | async-start | bytes 2097152 | tf_op jit(solution)/shard_map/all_to_all | solution.py:84
  57.7 312.9 %reduce-scatter.2.cloned.1.call-start = ((), (), s32[]{:S(2)}) async-start(), calls=%async_computation.8 | async-start | bytes 8912896 | tf_op jit(solution)/shard_map/reduce_scatter | solution.py:101
  62.6 1.6 slice-start
  70.7 1.6 slice-start.1
  72.3 2.6 copy-start.3
  76.4 3.0 copy-start.5
  84.0 107.9 %copy-start.6 = (bf16[128,8,512]{0,2,1:T(8,128)(2,1)}, bf16[128,8,512]{0,2,1:T(8,128)(2,1)S(1)}, u32[]{:S(2)}) copy-start(bf16[128,8,512]{0,2,1:T(8,128)(2,1)S(1)} %fusion.9) | copy-start | bytes 3145732
  186.8 3.5 copy-start.10
  191.9 2.7 copy-start.9
  197.3 3.0 copy-start.8
  200.6 1.2 copy-start.11
  251.2 19.3 %all-to-all-start.4 = ((bf16[8,128,512]{2,1,0:T(8,128)(2,1)}), bf16[8,128,512]{2,1,0:T(8,128)(2,1)}, u32[]{:S(2)}, u32[]{:S(2)}) async-start(bf16[8,128,512]{2,1,0:T(8,128)(2,1)} %bitcast.21), calls=%async_computation.4 | async-start | bytes 2097152 | tf_op jit(solution)/shard_map/all_to_all | solution.py:120
  270.6 96.9 %all-to-all-start.5 = ((bf16[8,128,512]{2,1,0:T(8,128)(2,1)}), bf16[8,128,512]{2,1,0:T(8,128)(2,1)}, u32[]{:S(2)}, u32[]{:S(2)}) async-start(bf16[8,128,512]{2,1,0:T(8,128)(2,1)} %bitcast.116), calls=%async_computation.5 | async-start | bytes 2097152 | tf_op jit(solution)/shard_map/all_to_all | solution.py:121
  290.2 72.3 %copy-start.7 = (bf16[8,128,512]{2,1,0:T(8,128)(2,1)S(1)}, bf16[8,128,512]{2,1,0:T(8,128)(2,1)}, u32[]{:S(2)}) copy-start(bf16[8,128,512]{2,1,0:T(8,128)(2,1)} %all_to_all.87) | copy-start | bytes 3145732
  367.5 5.2 %copy-start.1 = (bf16[256,128]{1,0:T(8,128)(2,1)S(1)}, bf16[256,128]{1,0:T(8,128)(2,1)}, u32[]{:S(2)}) copy-start(bf16[256,128]{1,0:T(8,128)(2,1)} %param.12) | copy-start | bytes 196612
Sparse Core Ops, SparseCore 0:
  10.4 75.8 all-gather.3
  87.9 86.6 all-gather.5
  230.6 115.1 reduce-scatter.1
where the time goes:
time: 381 us; the launch traced here: 379 us
  waiting for transfers between devices  130 us (34%)
  blocking collectives  90.1 us (24%)
  local copies, waits for them, and re-layouts  71.8 us (19%)
  matrix products  29.2 us (8%)
  starting transfers between devices  28.1 us (7%)
  other arithmetic  15.7 us (4%)
  between operations  13.9 us (4%)
    all_gather x1, waiting for transfers between devices, shards(): grad_all = lax.all_gather(cotangent[0], 'seq', axis=0, tiled=True)  88.4 us
    psum x1, blocking collectives, shards(): grad_filters, grad_gain = lax.psum((filter_part, gain_part), 'dp')  69.3 us
    all_to_all x1, blocking collectives, shards(): lax.all_to_all(grad_query, 'seq', split_axis=0, concat_axis=1, tiled=True)  20.8 us
    unnamed x38, local copies, waits for them, and re-layouts  16.1 us
    all_to_all x1, waiting for transfers between devices, shards(): lax.all_to_all(value_rows, 'seq', split_axis=1, concat_axis=0, tiled=True)  13.2 us
    all_to_all x1, waiting for transfers between devices, shards(): lax.all_to_all(key_rows, 'seq', split_axis=1, concat_axis=0, tiled=True)  12.9 us
    all_to_all x1, waiting for transfers between devices, shards(): lax.all_to_all(grad_key, 'seq', split_axis=0, concat_axis=1, tiled=True)  12.1 us
    dot_general x1, matrix products, shards(): jnp.dot(columns, lax.all_gather(out_weight, 'dp', axis=0, tiled=True), pr...  12.1 us
  transfers between devices with their start and end apart: 8, of which 5 were waited for; matrix products, arithmetic and copies ran while one was open for 15% of the time, Pallas kernels for 0%

commit v1 on v0

v1 whole, which is shorter than its diff:
```python
import functools
import math

import jax
import jax.numpy as jnp
from jax import lax
from jax.experimental import pallas as pl
from jax.experimental.pallas import tpu as pltpu
from jax.sharding import Mesh
from jax.sharding import PartitionSpec as P

GROUP = 16
TAPS = 128
BLOCKS = 8
BF = jnp.bfloat16
F32 = jnp.float32
MIB = 1024 * 1024
DP = ("x", "zh", "core")
SEQ = ("zl", "y")

ANY = pl.BlockSpec(memory_space=pl.ANY)
SMEM = pl.BlockSpec(memory_space=pltpu.SMEM)
VMEM = pl.BlockSpec(memory_space=pltpu.VMEM)


def call(body, out_shape, in_specs, out_specs, scratch=(), flops=0, moved=0, limit=40):
    return pl.pallas_call(
        body,
        out_shape=out_shape,
        in_specs=in_specs,
        out_specs=out_specs,
        scratch_shapes=list(scratch),
        compiler_params=pltpu.CompilerParams(vmem_limit_bytes=limit * MIB),
        cost_estimate=pl.CostEstimate(flops=flops, bytes_accessed=moved, transcendentals=0),
    )


def shape(dims, dtype=BF):
    return jax.ShapeDtypeStruct(dims, dtype)


def transpose_kernel(w_ref, out_ref):
    out_ref[...] = w_ref[...].astype(F32).T.astype(BF)


def table_kernel(panel_ref, filters_ref, gain_ref, table_ref, gain_out_ref):
    groups = table_ref.shape[0]
    panel = panel_ref[0]
    row = lax.broadcasted_iota(jnp.int32, (8, 2 * TAPS), 0)
    first = pl.multiple_of(panel * groups, groups)
    taps_all = filters_ref[pl.ds(first, groups), :].astype(F32)
    for g in range(groups):
        taps = jnp.broadcast_to(taps_all[g : g + 1, :], (8, TAPS))
        rows = jnp.concatenate([taps, jnp.zeros((8, TAPS), F32)], 1)
        for bit in (1, 2, 4):
            rows = jnp.where((row & bit) != 0, pltpu.roll(rows, bit, 1), rows)
        count = 8
        while count < TAPS:
            rows = jnp.concatenate([rows, pltpu.roll(rows, count, 1)], 0)
            count *= 2
        table_ref[g] = rows.astype(BF)
    gain_rows = gain_ref[panel]
    for i in range(gain_rows.shape[0]):
        gain_out_ref[TAPS * i : TAPS * (i + 1), :] = jnp.broadcast_to(
            gain_rows[i : i + 1, :], (TAPS, TAPS)
        ).T


def prepare_kernel(channels_ref, q_ref, k_ref, v_ref, *outs):
    width = outs[0].shape[1]
    for j in range(BLOCKS):
        cols = pl.ds(pl.multiple_of(channels_ref[j] * width, width), width)
        product = k_ref[:, cols].astype(F32) * v_ref[:, cols].astype(F32)
        outs[j][0] = product.T.astype(BF)
        outs[j][1] = q_ref[:, cols].astype(F32).T.astype(BF)


def tiles(rows):
    return [rows[:, TAPS * b : TAPS * (b + 1)] for b in range(BLOCKS)]


def forward_kernel(place_ref, *refs):
    slots = refs[:BLOCKS]
    table_ref, gain_ref, p_ref, q_ref, mixed_ref, gated_ref, sems = refs[BLOCKS:]
    copies = []
    for j in range(BLOCKS):
        lanes = pl.ds(pl.multiple_of(place_ref[j] * TAPS, TAPS), TAPS)
        for i, dst in ((0, p_ref), (1, q_ref)):
            copies.append(pltpu.make_async_copy(slots[j].at[i], dst.at[:, lanes], sems.at[2 * j + i]))
    for c in copies:
        c.start()
    for c in copies:
        c.wait()

    def one_group(g, carry):
        rows = pl.ds(pl.multiple_of(g * GROUP, GROUP), GROUP)
        x = tiles(p_ref[rows, :])
        q = tiles(q_ref[rows, :])
        zero = jnp.zeros((GROUP, TAPS), BF)
        lhs = jnp.concatenate(
            [jnp.concatenate(x, 0), jnp.concatenate([zero] + x[:-1], 0)], 1
        )
        table = table_ref[g]
        rhs = jnp.concatenate([table[:, :TAPS], table[:, TAPS:]], 0)
        conv = jnp.dot(lhs, rhs, preferred_element_type=F32)
        gain = gain_ref[rows, :]
        for b in range(BLOCKS):
            mixed = conv[GROUP * b : GROUP * (b + 1)] + gain * x[b].astype(F32)
            mixed_ref[rows, TAPS * b : TAPS * (b + 1)] = mixed
            gated_ref[rows, TAPS * b : TAPS * (b + 1)] = (q[b].astype(F32) * mixed).astype(BF)
        return carry

    lax.fori_loop(0, table_ref.shape[0], one_group, 0, unroll=4)


def cot_copies(place_ref, refs, held, sems):
    copies = []
    half = TAPS // 2
    for core in range(2):
        own, up, down, far_a, far_b = refs[5 * core : 5 * core + 5]
        for piece, (ref, k, first, count) in enumerate(
            ((own, 0, 0, TAPS), (up, 1, 0, TAPS), (down, 3, 0, TAPS), (far_a, 2, 0, half), (far_b, 2, half, half))
        ):
            start = pl.multiple_of(place_ref[4 * core + k] * TAPS + first, half)
            copies.append(
                pltpu.make_async_copy(ref, held.at[pl.ds(start, count), :], sems.at[5 * core + piece])
            )
    return copies


def weight_kernel(place_ref, at_ref, *refs):
    cot = refs[:10]
    gated_ref = refs[10]
    out_x = refs[11:15]
    out_z = refs[15:19]
    held, sems = refs[19:]
    copies = cot_copies(place_ref, cot, held, sems)
    for c in copies:
        c.start()
    for c in copies:
        c.wait()
    half = gated_ref.shape[0] // 2
    width = out_x[0].shape[2]
    x, z = at_ref[0], at_ref[1]
    for k in range(4):
        xk = lax.rem(x + k, 4)
        zk = lax.rem(z + k, 4)

        def part(i, carry, xk=xk, zk=zk, k=k):
            cols = pl.ds(pl.multiple_of((xk * 4 + i) * width, width), width)
            out_x[k][i] = jnp.dot(
                gated_ref[:half, :], held[:, cols], preferred_element_type=F32
            ).astype(BF)
            cols = pl.ds(pl.multiple_of((i * 4 + zk) * width, width), width)
            out_z[k][i] = jnp.dot(
                gated_ref[half:, :], held[:, cols], preferred_element_type=F32
            ).astype(BF)
            return carry

        lax.fori_loop(0, 4, part, 0)


def gradient_kernel(place_ref, *refs):
    cot = refs[:10]
    w_ref, mixed_ref, q_ref = refs[10:13]
    gm_ref = refs[13]
    outs = refs[14:22]
    held, w_held, gq, sems, w_sems, out_sems = refs[22:]
    copies = cot_copies(place_ref, cot, held, sems)
    blocks, channels, width = w_ref.shape
    for d in range(blocks):
        copies.append(
            pltpu.make_async_copy(w_ref.at[d], w_held.at[:, width * d : width * (d + 1)], w_sems.at[d])
        )
    for c in copies:
        c.start()
    for c in copies:
        c.wait()
    span = 2 * TAPS

    def part(n, carry):
        toks = pl.ds(pl.multiple_of(n * span, span), span)
        grad = lax.dot_general(
            w_held[...], held[toks, :], (((1,), (1,)), ((), ())), preferred_element_type=F32
        )
        gq[:, toks] = (grad * mixed_ref[:, toks]).astype(BF)
        gm_ref[:, toks] = (grad * q_ref[:, toks].astype(F32)).astype(BF)
        return carry

    lax.fori_loop(0, held.shape[0] // span, part, 0)
    backs = []
    for j in range(BLOCKS):
        lanes = pl.ds(pl.multiple_of(place_ref[j] * TAPS, TAPS), TAPS)
        backs.append(pltpu.make_async_copy(gq.at[:, lanes], outs[j], out_sems.at[j]))
    for c in backs:
        c.start()
    for c in backs:
        c.wait()


def backward_kernel(place_ref, gm_ref, table_ref, gain_ref, *refs):
    outs = refs[:BLOCKS]
    gp, out_sems = refs[BLOCKS:]

    def one_group(g, carry):
        rows = pl.ds(pl.multiple_of(g * GROUP, GROUP), GROUP)
        x = tiles(gm_ref[rows, :])
        zero = jnp.zeros((GROUP, TAPS), BF)
        lhs = jnp.concatenate(
            [jnp.concatenate(x, 0), jnp.concatenate(x[1:] + [zero], 0)], 1
        )
        conv = lax.dot_general(
            lhs, table_ref[g], (((1,), (1,)), ((), ())), preferred_element_type=F32
        )
        gain = gain_ref[rows, :]
        for b in range(BLOCKS):
            total = conv[GROUP * b : GROUP * (b + 1)] + gain * x[b].astype(F32)
            gp[rows, TAPS * b : TAPS * (b + 1)] = total.astype(BF)
        return carry

    lax.fori_loop(0, table_ref.shape[0], one_group, 0, unroll=4)
    backs = []
    for j in range(BLOCKS):
        lanes = pl.ds(pl.multiple_of(place_ref[j] * TAPS, TAPS), TAPS)
        backs.append(pltpu.make_async_copy(gp.at[:, lanes], outs[j], out_sems.at[j]))
    for c in backs:
        c.start()
    for c in backs:
        c.wait()


def filter_kernel(gm_ref, p_ref, out_ref):
    groups = gm_ref.shape[0] // GROUP
    span = 2 * TAPS
    row = lax.broadcasted_iota(jnp.int32, (8, span), 0)

    def one_group(g, carry):
        rows = pl.ds(pl.multiple_of(g * GROUP, GROUP), GROUP)
        x = jnp.concatenate(tiles(p_ref[rows, :]), 0)
        y = tiles(gm_ref[rows, :])
        zero = jnp.zeros((GROUP, TAPS), BF)
        window = jnp.concatenate(
            [jnp.concatenate(y, 0), jnp.concatenate(y[1:] + [zero], 0)], 1
        )
        pairs = lax.dot_general(x, window, (((0,), (0,)), ((), ())), preferred_element_type=F32)
        count = TAPS
        while count > 8:
            count //= 2
            pairs = pairs[:count] + pltpu.roll(pairs[count:], span - count, 1)
        for bit in (4, 2, 1):
            pairs = jnp.where((row & bit) != 0, pltpu.roll(pairs, span - bit, 1), pairs)
        out_ref[pl.ds(g, 1), :] = jnp.sum(pairs, 0, keepdims=True)[:, :TAPS]
        return carry

    lax.fori_loop(0, groups, one_group, 0, unroll=2)
    channels = gm_ref.shape[0]
    for i in range(channels // TAPS):
        rows = slice(TAPS * i, TAPS * (i + 1))
        total = jnp.zeros((TAPS, TAPS), F32)
        for b in range(BLOCKS):
            lanes = slice(TAPS * b, TAPS * (b + 1))
            total += gm_ref[rows, lanes].astype(F32) * p_ref[rows, lanes].astype(F32)
        out_ref[groups + i : groups + i + 1, :] = jnp.sum(total.T, 0, keepdims=True)
    first = groups + channels // TAPS
    out_ref[first:, :] = jnp.zeros((out_ref.shape[0] - first, TAPS), F32)


def partial_kernel(at_ref, *refs):
    pieces, outs = refs[:4], refs[4:]
    for k in range(4):
        i = lax.rem(at_ref[0] + k, 4)
        total = pieces[0][i].astype(F32)
        for piece in pieces[1:]:
            total += piece[i].astype(F32)
        outs[k][...] = total.astype(BF)


def total_kernel(scale, *refs):
    out_ref = refs[8]
    for h in range(2):
        total = refs[4 * h][...].astype(F32)
        for ref in refs[4 * h + 1 : 4 * h + 4]:
            total += ref[...].astype(F32)
        half = total.shape[0]
        out_ref[:, half * h : half * (h + 1)] = (total * scale).T


def finish_kernel(channels_ref, k_ref, v_ref, *refs):
    gqs, gps = refs[:BLOCKS], refs[BLOCKS : 2 * BLOCKS]
    gq_ref, gk_ref, gv_ref = refs[2 * BLOCKS :]
    width = gqs[0].shape[0]
    for j in range(BLOCKS):
        cols = pl.ds(pl.multiple_of(channels_ref[j] * width, width), width)
        gq_ref[:, cols] = gqs[j][...].astype(F32).T.astype(BF)
        gp = gps[j][...].astype(F32).T
        gk_ref[:, cols] = (gp * v_ref[:, cols].astype(F32)).astype(BF)
        gv_ref[:, cols] = (gp * k_ref[:, cols].astype(F32)).astype(BF)


SWAP = [(0, 0), (1, 2), (2, 1), (3, 3)]
SLOTS = [(d, k) for d in range(2) for k in range(4)]


def ring(n, k):
    return [(i, (i + k) % n) for i in range(n)]


def stream_pairs(d, k):
    pairs = []
    for core in range(2):
        for zl in range(2):
            for y in range(4):
                pairs.append(((core * 2 + zl) * 4 + y, ((zl ^ d) * 2 + core) * 4 + (y + k) % 4))
    return pairs


def z_pairs(k):
    pairs = []
    for zh in range(2):
        for core in range(2):
            for zl in range(2):
                z = (zh * 2 + zl + k) % 4
                pairs.append(((zh * 2 + core) * 2 + zl, z * 2 + core))
    return pairs


def x_pairs(k):
    pairs = []
    for x in range(4):
        for core in range(2):
            for zl in range(2):
                pairs.append(((x * 2 + core) * 2 + zl, (((x + k) % 4) * 2 + zl) * 2 + core))
    return pairs


def ring_z(k):
    return [(z, (z + k) % 4) for z in range(4)]


def shards(queries, key_input, value_input, cotangent, out_weight, filters, skip_gain):
    q, k, v, cot = queries[0], key_input[0], value_input[0], cotangent[0]
    rows, width = q.shape
    panel = width // 8
    outs_here = out_weight.shape[0]
    length = rows * 8
    groups = panel // GROUP
    scale = 1.0 / math.sqrt(16 * length)
    x, zh, core, zl, y = (lax.axis_index(n) for n in ("x", "zh", "core", "zl", "y"))
    z = zh * 2 + zl
    channels = jnp.stack([(zl ^ d) * 4 + (y + i) % 4 for d, i in SLOTS]).astype(jnp.int32)
    place = jnp.stack([(core ^ d) * 4 + (y - i) % 4 for d, i in SLOTS]).astype(jnp.int32)
    own_panel = (core * 4 + y).astype(jnp.int32).reshape(1)
    at = jnp.stack([x, z]).astype(jnp.int32)
    at_x, at_z = x.astype(jnp.int32).reshape(1), z.astype(jnp.int32).reshape(1)

    w_t = call(transpose_kernel, shape((panel, outs_here)), [VMEM], VMEM, moved=2 * outs_here * panel * 2)(out_weight)
    w_t = lax.ppermute(w_t, ("core", "zl"), SWAP)
    w_all = lax.all_gather(w_t, ("x", "zh", "zl"), axis=0)

    own = lax.ppermute(cot, ("core", "zl"), SWAP)
    up = lax.ppermute(own, "y", ring(4, 1))
    down = lax.ppermute(own, "y", ring(4, -1))
    far_a = lax.ppermute(up[: rows // 2], "y", ring(4, 1))
    far_b = lax.ppermute(down[rows // 2 :], "y", ring(4, -1))
    cots = [own, up, down, far_a, far_b]
    cots = cots + [lax.ppermute(c, "core", ring(2, 1)) for c in cots]

    chunks = call(
        prepare_kernel,
        [shape((2, panel, rows))] * BLOCKS,
        [SMEM, VMEM, VMEM, VMEM],
        [VMEM] * BLOCKS,
        flops=8 * rows * width,
        moved=10 * rows * width,
    )(channels, q, k, v)
    slots = [
        lax.ppermute(c, ("core", "zl", "y"), stream_pairs(d, i)) for c, (d, i) in zip(chunks, SLOTS)
    ]
    table, gain = call(
        table_kernel,
        [shape((groups, TAPS, 2 * TAPS)), shape((panel, TAPS), F32)],
        [SMEM, VMEM, VMEM],
        [VMEM, VMEM],
        flops=groups * TAPS * 2 * TAPS * 4,
        moved=3 * MIB,
    )(own_panel, filters, skip_gain.reshape(8, panel // TAPS, TAPS))
    p_t, q_t, mixed, gated = call(
        forward_kernel,
        [shape((panel, length)), shape((panel, length)), shape((panel, length), F32), shape((panel, length))],
        [SMEM] + [ANY] * BLOCKS + [VMEM, VMEM],
        [VMEM] * 4,
        scratch=[pltpu.SemaphoreType.DMA((2 * BLOCKS,))],
        flops=2 * groups * TAPS * TAPS * 2 * TAPS,
        moved=12 * MIB,
    )(place, *slots, table, gain)

    cot_held = pltpu.VMEM((length, width), BF)
    ten = pltpu.SemaphoreType.DMA((10,))
    parts = call(
        weight_kernel,
        [shape((4, panel // 2, outs_here))] * 8,
        [SMEM, SMEM] + [ANY] * 10 + [VMEM],
        [VMEM] * 8,
        scratch=[cot_held, ten],
        flops=2 * length * width * panel,
        moved=13 * MIB,
    )(place, at, *cots, gated)
    by_x, by_z = parts[:4], parts[4:]
    by_x = [by_x[0]] + [lax.ppermute(by_x[i], "x", ring(4, i)) for i in (1, 2, 3)]
    by_z = [by_z[0]] + [lax.ppermute(by_z[i], ("zh", "zl"), ring_z(i)) for i in (1, 2, 3)]
    partial = call(
        partial_kernel,
        [shape((panel // 2, outs_here))] * 4,
        [SMEM] + [VMEM] * 4,
        [VMEM] * 4,
        flops=4 * panel * outs_here * 4,
        moved=3 * MIB,
    )
    by_x = partial(at_z, *by_x)
    by_z = partial(at_x, *by_z)
    by_x = [lax.ppermute(c, ("zh", "core", "zl"), z_pairs(i)) for i, c in enumerate(by_x)]
    by_z = [lax.ppermute(c, ("x", "core", "zl"), x_pairs(i)) for i, c in enumerate(by_z)]
    grad_weight = call(
        functools.partial(total_kernel, scale),
        shape((outs_here, panel), F32),
        [VMEM] * 8,
        VMEM,
        flops=10 * panel * outs_here,
        moved=2 * MIB,
    )(*by_x, *by_z)

    grads = call(
        gradient_kernel,
        [shape((panel, length))] + [shape((panel, rows))] * BLOCKS,
        [SMEM] + [ANY] * 11 + [VMEM] * 2,
        [VMEM] + [ANY] * BLOCKS,
        scratch=[
            cot_held,
            pltpu.VMEM((panel, width), BF),
            pltpu.VMEM((panel, length), BF),
            ten,
            pltpu.SemaphoreType.DMA((16,)),
            pltpu.SemaphoreType.DMA((BLOCKS,)),
        ],
        flops=2 * length * width * panel,
        moved=17 * MIB,
    )(place, *cots, w_all, mixed, q_t)
    gm, gqs = grads[0], grads[1:]
    gps = call(
        backward_kernel,
        [shape((panel, rows))] * BLOCKS,
        [SMEM] + [VMEM] * 3,
        [ANY] * BLOCKS,
        scratch=[pltpu.VMEM((panel, length), BF), pltpu.SemaphoreType.DMA((BLOCKS,))],
        flops=2 * groups * TAPS * TAPS * 2 * TAPS,
        moved=5 * MIB,
    )(place, gm, table, gain)

    def home(chunks):
        moved = []
        for c, (d, i) in zip(chunks, SLOTS):
            pairs = [(b, a) for a, b in stream_pairs(d, i)]
            moved.append(lax.ppermute(c, ("core", "zl", "y"), pairs))
        return moved

    gqs, gps = home(gqs), home(gps)
    sums = call(
        filter_kernel,
        shape((40, TAPS), F32),
        [VMEM, VMEM],
        VMEM,
        flops=2 * groups * TAPS * TAPS * 2 * TAPS,
        moved=3 * MIB,
    )(gm, p_t)
    sums = lax.all_gather(sums, ("x", "zh", "zl"), axis=0)
    sums = jnp.sum(sums, 0) * scale
    sums = lax.ppermute(sums, ("core", "zl"), SWAP)
    grad_filters = sums[:groups]
    grad_gain = sums[groups : groups + panel // TAPS].reshape(panel)

    grad_query, grad_key, grad_value = call(
        finish_kernel,
        [shape((rows, width))] * 3,
        [SMEM] + [VMEM] * 18,
        [VMEM] * 3,
        flops=10 * rows * width,
        moved=14 * rows * width,
    )(channels, k, v, *gqs, *gps)
    return (
        grad_query[None],
        grad_key[None],
        grad_value[None],
        grad_weight,
        grad_filters,
        grad_gain,
    )


def solution(mesh):
    fine = Mesh(mesh.devices.reshape(4, 2, 2, 2, 4), ("x", "zh", "core", "zl", "y"))
    stream = P(DP, SEQ, None)
    return jax.shard_map(
        shards,
        mesh=fine,
        in_specs=(stream, stream, stream, stream, P(DP, SEQ), P(), P()),
        out_specs=(stream, stream, stream, P(DP, SEQ), P(SEQ, None), P(SEQ)),
        check_vma=False,
    )
```

time: 381 us -> 291 us (0.76)
  starting transfers between devices: 28.1 us -> 116 us
  waiting for transfers between devices: 130 us -> 43.3 us
  blocking collectives: 90.1 us -> 34.9 us
  Pallas kernels: 0 us -> 52 us
  local copies, waits for them, and re-layouts: 71.8 us -> 24.2 us
  matrix products: 29.2 us -> 0 us
  other arithmetic: 15.7 us -> 2.42 us
    ppermute x0 -> x50, starting transfers between devices: none -> 116 us  [the longest x8 30.9 us: shards(): lax.ppermute(c, ('core', 'zl', 'y'), stream_pairs(d, i))]
    all_gather x2 -> x1, waiting for transfers between devices: 90.7 us -> 0.01 us  [shards(): w_all = lax.all_gather(w_t, ('x', 'zh', 'zl'), axis=0)]
    psum x1 -> x0, blocking collectives: 69.3 us -> none  [shards(): grad_filters, grad_gain = lax.psum((filter_part, gain_part), 'dp')]
    pallas_call x0 -> x12, Pallas kernels: none -> 52 us  [the longest x1 11.6 us: shards(): call(filter_kernel, shape((40, TAPS), F32), [VMEM, VMEM], VMEM, flops=2 *...]
    ppermute x0 -> x50, waiting for transfers between devices: none -> 43.2 us  [the longest x8 14.5 us: shards(): lax.ppermute(c, ('core', 'zl', 'y'), stream_pairs(d, i))]
    all_to_all x5 -> x0, waiting for transfers between devices: 38.2 us -> none  [the longest x1 13.2 us: shards(): lax.all_to_all(value_rows, 'seq', split_axis=1, concat_axis=0, tiled=True)]
    all_gather x0 -> x1, blocking collectives: none -> 34.9 us  [shards(): sums = lax.all_gather(sums, ('x', 'zh', 'zl'), axis=0)]
    dot_general x5 -> x0, matrix products: 29.2 us -> none  [the longest x1 12.1 us: shards(): jnp.dot(columns, lax.all_gather(out_weight, 'dp', axis=0, tiled=True), pr...]
  transfers between devices with their start and end apart: 8 -> 51, of which waited for: 5 -> 11; matrix products, arithmetic and copies ran while one was open for 15% -> 2% of each run, Pallas kernels for 0% -> 17%
where the time goes in v1:
time: 291 us; the launch traced here: 287 us
  starting transfers between devices  116 us (40%)
  Pallas kernels  52 us (18%)
  waiting for transfers between devices  43.3 us (15%)
  blocking collectives  34.9 us (12%)
  local copies, waits for them, and re-layouts  24.2 us (8%)
  between operations  14.5 us (5%)
    all_gather x1, blocking collectives, shards(): sums = lax.all_gather(sums, ('x', 'zh', 'zl'), axis=0)  34.9 us
    ppermute x8, starting transfers between devices, shards(): lax.ppermute(c, ('core', 'zl', 'y'), stream_pairs(d, i))  30.9 us
    ppermute x16, starting transfers between devices, home(): moved.append(lax.ppermute(c, ('core', 'zl', 'y'), pairs))  26.8 us
    unnamed x88, local copies, waits for them, and re-layouts  20.7 us
    ppermute x8, waiting for transfers between devices, shards(): lax.ppermute(c, ('core', 'zl', 'y'), stream_pairs(d, i))  14.5 us
    ppermute x3, starting transfers between devices, shards(): lax.ppermute(by_x[i], 'x', ring(4, i))  14.2 us
    pallas_call x1, Pallas kernels, shards(): call(filter_kernel, shape((40, TAPS), F32), [VMEM, VMEM], VMEM, flops=2 *...  11.6 us
    pallas_call x1, Pallas kernels, shards(): call(weight_kernel, [shape((4, panel // 2, outs_here))] * 8, [SMEM, SMEM]...  11.6 us
  transfers between devices with their start and end apart: 51, of which 11 were waited for; matrix products, arithmetic and copies ran while one was open for 2% of the time, Pallas kernels for 17%

profile of v1, /device:TPU:8, one launch (start us, length us, event | category | flops | bytes accessed | tf_op | source)
XLA Modules:
  0.0 287.2 jit_solution(17103834651259786728)
XLA Ops:
  9.7 9.5 %collective-permute-start = (bf16[128,4096]{1,0:T(8,128)(2,1)}, bf16[128,4096]{1,0:T(8,128)(2,1)}, u32[]{:S(2)}, u32[]{:S(2)}) collective-permute-start(bf16[128,4096]{1,0:T(8,128)(2,1)} %bitcast.39), channel_id=1, source_target_pairs={{0,0},{4,8},{8,4},{12,12},{1,1},{5,9},{9,5},{13,13},{2,2},{6,10},{... | collective-permute-start | bytes 3145736 | tf_op jit(solution)/shard_map/ppermute | solution.py:360
  31.9 5.1 %collective-permute-done.12.refs_1_ = bf16[2,512,128]{2,1,0:T(8,128)(2,1)S(1)} collective-permute-done((bf16[2,512,128]{2,1,0:T(8,128)(2,1)S(1)}, bf16[2,512,128]{2,1,0:T(8,128)(2,1)S(1)}, u32[]{:S(2)}, u32[]{:S(2)}) %collective-permute-start.12) | collective-permute-done | bytes 262176 | tf_op jit(solution)/shard_map/ppermute | solution.py:377
  37.0 17.9 %collective-permute-start.15 = (bf16[2,512,128]{2,1,0:T(8,128)(2,1)S(1)}, bf16[2,512,128]{2,1,0:T(8,128)(2,1)S(1)}, u32[]{:S(2)}, u32[]{:S(2)}) collective-permute-start(bf16[2,512,128]{2,1,0:T(8,128)(2,1)S(1)} %get-tuple-element.60), channel_id=1, source_target_pairs={{0,8},{1,9},{2,10},{3,11},{4,0},{5,1},{6,2},{7,3},{8,12},{9,13},{1... | collective-permute-start | bytes 786440 | tf_op jit(solution)/shard_map/ppermute | solution.py:377
  54.9 4.1 %collective-permute-start.16 = (bf16[2,512,128]{2,1,0:T(8,128)(2,1)S(1)}, bf16[2,512,128]{2,1,0:T(8,128)(2,1)S(1)}, u32[]{:S(2)}, u32[]{:S(2)}) collective-permute-start(bf16[2,512,128]{2,1,0:T(8,128)(2,1)S(1)} %get-tuple-element.61), channel_id=1, source_target_pairs={{0,9},{1,10},{2,11},{3,8},{4,1},{5,2},{6,3},{7,0},{8,13},{9,14},{1... | collective-permute-start | bytes 786440 | tf_op jit(solution)/shard_map/ppermute | solution.py:377
  67.3 9.3 %collective-permute-done.15.refs_4_ = bf16[2,512,128]{2,1,0:T(8,128)(2,1)S(1)} collective-permute-done((bf16[2,512,128]{2,1,0:T(8,128)(2,1)S(1)}, bf16[2,512,128]{2,1,0:T(8,128)(2,1)S(1)}, u32[]{:S(2)}, u32[]{:S(2)}) %collective-permute-start.15) | collective-permute-done | bytes 262176 | tf_op jit(solution)/shard_map/ppermute | solution.py:377
  82.9 8.2 %collective-permute-done.3.refs_3_ = bf16[64,4096]{1,0:T(8,128)(2,1)} collective-permute-done((bf16[64,4096]{1,0:T(8,128)(2,1)S(1)}, bf16[64,4096]{1,0:T(8,128)(2,1)}, u32[]{:S(2)}, u32[]{:S(2)}) %collective-permute-start.3) | collective-permute-done | bytes 524320 | tf_op jit(solution)/shard_map/ppermute | solution.py:363
  91.1 4.4 %collective-permute-done.4.refs_4_ = bf16[64,4096]{1,0:T(8,128)(2,1)} collective-permute-done((bf16[64,4096]{1,0:T(8,128)(2,1)S(1)}, bf16[64,4096]{1,0:T(8,128)(2,1)}, u32[]{:S(2)}, u32[]{:S(2)}) %collective-permute-start.4) | collective-permute-done | bytes 524320 | tf_op jit(solution)/shard_map/ppermute | solution.py:364
  95.6 3.9 %shard_map.120 = (bf16[32,128,256]{2,1,0:T(8,128)(2,1)S(1)}, f32[512,128]{1,0:T(8,128)S(1)}) custom-call(s32[1]{0:T(128)} %bitcast.21.panel_ref, bf16[256,128]{1,0:T(8,128)(2,1)S(1)} %copy-done.16, f32[8,4,128]{2,1,0:T(4,128)S(1)} %bitcast.36), custom_call_target="tpu_custom_call" | custom-call | flops 4194304 | bytes 3145728 | tf_op jit(solution)/shard_map/pallas_call | solution.py:379
  109.8 11.6 %shard_map.125 = (bf16[4,256,256]{2,1,0:T(8,128)(2,1)S(1)}, bf16[4,256,256]{2,1,0:T(8,128)(2,1)S(1)}, bf16[4,256,256]{2,1,0:T(8,128)(2,1)S(1)}, bf16[4,256,256]{...) custom-call(s32[8]{0:T(128)S(1)} %stack.78.place_ref, ...), custom_call_target="tpu_custom_call" | custom-call | flops 4294967296 | bytes 13631488 | tf_op jit(solution)/shard_map/pallas_call | solution.py:399
  122.6 3.9 %collective-permute-start.43 = (bf16[4,256,256]{2,1,0:T(8,128)(2,1)S(1)}, bf16[4,256,256]{2,1,0:T(8,128)(2,1)S(1)}, u32[]{:S(2)}, u32[]{:S(2)}) collective-permute-start(bf16[4,256,256]{2,1,0:T(8,128)(2,1)S(1)} %get-tuple-element.99), channel_id=1, source_target_pairs={{0,16},{4,20},{16,0},{20,4},{1,17},{5,21},{17,1},{21,5},{2,18},{6,... | collective-permute-start | bytes 1572872 | tf_op jit(solution)/shard_map/ppermute | solution.py:410
  128.9 3.7 %collective-permute-start.35 = (bf16[4,256,256]{2,1,0:T(8,128)(2,1)S(1)}, bf16[4,256,256]{2,1,0:T(8,128)(2,1)S(1)}, u32[]{:S(2)}, u32[]{:S(2)}) collective-permute-start(bf16[4,256,256]{2,1,0:T(8,128)(2,1)S(1)} %get-tuple-element.90), channel_id=1, source_target_pairs={{0,32},{32,64},{64,96},{96,0},{1,33},{33,65},{65,97},{97,1},{2,34}... | collective-permute-start | bytes 1572872 | tf_op jit(solution)/shard_map/ppermute | solution.py:409
  132.6 3.7 %collective-permute-start.36 = (bf16[4,256,256]{2,1,0:T(8,128)(2,1)S(1)}, bf16[4,256,256]{2,1,0:T(8,128)(2,1)S(1)}, u32[]{:S(2)}, u32[]{:S(2)}) collective-permute-start(bf16[4,256,256]{2,1,0:T(8,128)(2,1)S(1)} %get-tuple-element.91), channel_id=1, source_target_pairs={{0,64},{32,96},{64,0},{96,32},{1,65},{33,97},{65,1},{97,33},{2,66}... | collective-permute-start | bytes 1572872 | tf_op jit(solution)/shard_map/ppermute | solution.py:409
  137.6 6.8 %collective-permute-start.37 = (bf16[4,256,256]{2,1,0:T(8,128)(2,1)S(1)}, bf16[4,256,256]{2,1,0:T(8,128)(2,1)S(1)}, u32[]{:S(2)}, u32[]{:S(2)}) collective-permute-start(bf16[4,256,256]{2,1,0:T(8,128)(2,1)S(1)} %get-tuple-element.92), channel_id=1, source_target_pairs={{0,96},{32,0},{64,32},{96,64},{1,97},{33,1},{65,33},{97,65},{2,98}... | collective-permute-start | bytes 1572872 | tf_op jit(solution)/shard_map/ppermute | solution.py:409
  144.4 5.6 %collective-permute-done.43.refs_2_ = bf16[4,256,256]{2,1,0:T(8,128)(2,1)S(1)} collective-permute-done((bf16[4,256,256]{2,1,0:T(8,128)(2,1)S(1)}, bf16[4,256,256]{2,1,0:T(8,128)(2,1)S(1)}, u32[]{:S(2)}, u32[]{:S(2)}) %collective-permute-start.43) | collective-permute-done | bytes 524320 | tf_op jit(solution)/shard_map/ppermute | solution.py:410
  152.6 4.6 %collective-permute-start.46 = (bf16[256,256]{1,0:T(8,128)(2,1)}, bf16[256,256]{1,0:T(8,128)(2,1)}, u32[]{:S(2)}, u32[]{:S(2)}) collective-permute-start(bf16[256,256]{1,0:T(8,128)(2,1)} %get-tuple-element.102), channel_id=1, source_target_pairs={{0,32},{4,40},{8,36},{12,44},{32,64},{36,72},{40,68},{44,76},{64,9... | collective-permute-start | bytes 393224 | tf_op jit(solution)/shard_map/ppermute | solution.py:422
  157.1 3.7 %collective-permute-start.47 = (bf16[256,256]{1,0:T(8,128)(2,1)}, bf16[256,256]{1,0:T(8,128)(2,1)}, u32[]{:S(2)}, u32[]{:S(2)}) collective-permute-start(bf16[256,256]{1,0:T(8,128)(2,1)} %get-tuple-element.103), channel_id=1, source_target_pairs={{0,64},{4,72},{8,68},{12,76},{32,96},{36,104},{40,100},{44,108},{6... | collective-permute-start | bytes 393224 | tf_op jit(solution)/shard_map/ppermute | solution.py:422
  169.6 10.8 %shard_map.122 = (bf16[512,1024]{1,0:T(8,128)(2,1)S(1)}, bf16[512,128]{1,0:T(8,128)(2,1)S(1)}, bf16[512,128]{1,0:T(8,128)(2,1)S(1)}, bf16[512,128]{1,0:T(8,128)(...) custom-call(s32[8]{0:T(128)S(1)} %stack.78.place_ref, ...), custom_call_target="tpu_custom_call" | custom-call | flops 4294967296 | bytes 17825792 | tf_op jit(solution)/shard_map/pallas_call | solution.py:432
  181.1 11.6 %shard_map.129 = f32[40,128]{1,0:T(8,128)S(1)} custom-call(bf16[512,1024]{1,0:T(8,128)(2,1)S(1)} %get-tuple-element.76.gm_ref, bf16[512,1024]{1,0:T(8,128)(2,1)S(1)} %copy-done.6), custom_call_target="tpu_custom_call" | custom-call | flops 268435456 | bytes 3145728 | tf_op jit(solution)/shard_map/pallas_call | solution.py:467
  192.8 34.9 %all-gather.1 = f32[640,128]{1,0:T(8,128)} all-gather(f32[40,128]{1,0:T(8,128)S(1)} %shard_map.129), channel_id=3, replica_groups=mesh['x'=4,'zh'=2,'core'=2,'zl'=2,'y'=4] {'x','zh','zl'}, dimensions={0}, use_global_device_ids=true | all-gather | bytes 348160 | tf_op jit(solution)/shard_map/all_gather | solution.py:475
  247.1 4.1 %collective-permute-start.31 = (bf16[512,128]{1,0:T(8,128)(2,1)S(1)}, bf16[512,128]{1,0:T(8,128)(2,1)S(1)}, u32[]{:S(2)}, u32[]{:S(2)}) collective-permute-start(bf16[512,128]{1,0:T(8,128)(2,1)S(1)} %get-tuple-element.81), channel_id=1, source_target_pairs={{8,0},{9,1},{10,2},{11,3},{0,4},{1,5},{2,6},{3,7},{12,8},{13,9},{1... | collective-permute-start | bytes 393224 | tf_op jit(solution)/shard_map/ppermute | solution.py:463
  251.2 5.1 %collective-permute-start.33 = (bf16[512,128]{1,0:T(8,128)(2,1)S(1)}, bf16[512,128]{1,0:T(8,128)(2,1)S(1)}, u32[]{:S(2)}, u32[]{:S(2)}) collective-permute-start(bf16[512,128]{1,0:T(8,128)(2,1)S(1)} %get-tuple-element.83), channel_id=1, source_target_pairs={{10,0},{11,1},{8,2},{9,3},{2,4},{3,5},{0,6},{1,7},{14,8},{15,9},{1... | collective-permute-start | bytes 393224 | tf_op jit(solution)/shard_map/ppermute | solution.py:463
  264.2 3.3 %collective-permute-start.23 = (bf16[512,128]{1,0:T(8,128)(2,1)S(1)}, bf16[512,128]{1,0:T(8,128)(2,1)S(1)}, u32[]{:S(2)}, u32[]{:S(2)}) collective-permute-start(bf16[512,128]{1,0:T(8,128)(2,1)S(1)} %copy-done.29), channel_id=1, source_target_pairs={{8,0},{9,1},{10,2},{11,3},{0,4},{1,5},{2,6},{3,7},{12,8},{13,9},{1... | collective-permute-start | bytes 393224 | tf_op jit(solution)/shard_map/ppermute | solution.py:463
  267.5 3.9 %collective-permute-start.25 = (bf16[512,128]{1,0:T(8,128)(2,1)S(1)}, bf16[512,128]{1,0:T(8,128)(2,1)S(1)}, u32[]{:S(2)}, u32[]{:S(2)}) collective-permute-start(bf16[512,128]{1,0:T(8,128)(2,1)S(1)} %copy-done.25), channel_id=1, source_target_pairs={{10,0},{11,1},{8,2},{9,3},{2,4},{3,5},{0,6},{1,7},{14,8},{15,9},{1... | collective-permute-start | bytes 393224 | tf_op jit(solution)/shard_map/ppermute | solution.py:463
  273.0 4.3 %collective-permute-done.25.refs_6_ = bf16[512,128]{1,0:T(8,128)(2,1)S(1)} collective-permute-done((bf16[512,128]{1,0:T(8,128)(2,1)S(1)}, bf16[512,128]{1,0:T(8,128)(2,1)S(1)}, u32[]{:S(2)}, u32[]{:S(2)}) %collective-permute-start.25) | collective-permute-done | bytes 131104 | tf_op jit(solution)/shard_map/ppermute | solution.py:463
  (189 shorter events, 88.7 us)
Async XLA Ops:
  7.2 159.6 %all-gather.4.cloned.1.call-start = ((), (), s32[]{:S(2)}) async-start(), calls=%async_computation | async-start | bytes 4456448 | tf_op jit(solution)/shard_map/all_gather | solution.py:358
  19.2 39.8 %collective-permute-start.1 = (bf16[128,4096]{1,0:T(8,128)(2,1)}, bf16[128,4096]{1,0:T(8,128)(2,1)}, u32[]{:S(2)}, u32[]{:S(2)}) collective-permute-start(bf16[128,4096]{1,0:T(8,128)(2,1)} %collective-permute-done.refs_0_), channel_id=1, source_target_pairs={{0,1},{1,2},{2,3},{3,0},{4,5},{5,6},{6,7},{7,4},{8,9},{9,10},{10,1... | collective-permute-start | bytes 3145736 | tf_op jit(solution)/shard_map/ppermute | solution.py:361
  20.8 39.3 %collective-permute-start.2 = (bf16[128,4096]{1,0:T(8,128)(2,1)}, bf16[128,4096]{1,0:T(8,128)(2,1)}, u32[]{:S(2)}, u32[]{:S(2)}) collective-permute-start(bf16[128,4096]{1,0:T(8,128)(2,1)} %collective-permute-done.refs_0_), channel_id=1, source_target_pairs={{0,3},{1,0},{2,1},{3,2},{4,7},{5,4},{6,5},{7,6},{8,11},{9,8},{10,9... | collective-permute-start | bytes 3145736 | tf_op jit(solution)/shard_map/ppermute | solution.py:362
  28.5 26.4 %collective-permute-start.13 = (bf16[2,512,128]{2,1,0:T(8,128)(2,1)S(1)}, bf16[2,512,128]{2,1,0:T(8,128)(2,1)S(1)}, u32[]{:S(2)}, u32[]{:S(2)}) collective-permute-start(bf16[2,512,128]{2,1,0:T(8,128)(2,1)S(1)} %get-tuple-element.58), channel_id=1, source_target_pairs={{0,2},{1,3},{2,0},{3,1},{4,10},{5,11},{6,8},{7,9},{8,6},{9,7},{10,... | collective-permute-start | bytes 786440 | tf_op jit(solution)/shard_map/ppermute | solution.py:377
  30.6 33.8 %collective-permute-start.14 = (bf16[2,512,128]{2,1,0:T(8,128)(2,1)S(1)}, bf16[2,512,128]{2,1,0:T(8,128)(2,1)S(1)}, u32[]{:S(2)}, u32[]{:S(2)}) collective-permute-start(bf16[2,512,128]{2,1,0:T(8,128)(2,1)S(1)} %get-tuple-element.59), channel_id=1, source_target_pairs={{0,3},{1,0},{2,1},{3,2},{4,11},{5,8},{6,9},{7,10},{8,7},{9,4},{10,... | collective-permute-start | bytes 786440 | tf_op jit(solution)/shard_map/ppermute | solution.py:377
  37.0 39.7 %collective-permute-start.15 = (bf16[2,512,128]{2,1,0:T(8,128)(2,1)S(1)}, bf16[2,512,128]{2,1,0:T(8,128)(2,1)S(1)}, u32[]{:S(2)}, u32[]{:S(2)}) collective-permute-start(bf16[2,512,128]{2,1,0:T(8,128)(2,1)S(1)} %get-tuple-element.60), channel_id=1, source_target_pairs={{0,8},{1,9},{2,10},{3,11},{4,0},{5,1},{6,2},{7,3},{8,12},{9,13},{1... | collective-permute-start | bytes 786440 | tf_op jit(solution)/shard_map/ppermute | solution.py:377
  54.9 24.0 %collective-permute-start.16 = (bf16[2,512,128]{2,1,0:T(8,128)(2,1)S(1)}, bf16[2,512,128]{2,1,0:T(8,128)(2,1)S(1)}, u32[]{:S(2)}, u32[]{:S(2)}) collective-permute-start(bf16[2,512,128]{2,1,0:T(8,128)(2,1)S(1)} %get-tuple-element.61), channel_id=1, source_target_pairs={{0,9},{1,10},{2,11},{3,8},{4,1},{5,2},{6,3},{7,0},{8,13},{9,14},{1... | collective-permute-start | bytes 786440 | tf_op jit(solution)/shard_map/ppermute | solution.py:377
  59.0 20.7 %collective-permute-start.17 = (bf16[2,512,128]{2,1,0:T(8,128)(2,1)S(1)}, bf16[2,512,128]{2,1,0:T(8,128)(2,1)S(1)}, u32[]{:S(2)}, u32[]{:S(2)}) collective-permute-start(bf16[2,512,128]{2,1,0:T(8,128)(2,1)S(1)} %get-tuple-element.62), channel_id=1, source_target_pairs={{0,10},{1,11},{2,8},{3,9},{4,2},{5,3},{6,0},{7,1},{8,14},{9,15},{1... | collective-permute-start | bytes 786440 | tf_op jit(solution)/shard_map/ppermute | solution.py:377
  60.1 20.8 %collective-permute-start.18 = (bf16[2,512,128]{2,1,0:T(8,128)(2,1)S(1)}, bf16[2,512,128]{2,1,0:T(8,128)(2,1)S(1)}, u32[]{:S(2)}, u32[]{:S(2)}) collective-permute-start(bf16[2,512,128]{2,1,0:T(8,128)(2,1)S(1)} %get-tuple-element.63), channel_id=1, source_target_pairs={{0,11},{1,8},{2,9},{3,10},{4,3},{5,0},{6,1},{7,2},{8,15},{9,12},{1... | collective-permute-start | bytes 786440 | tf_op jit(solution)/shard_map/ppermute | solution.py:377
  64.4 45.3 %collective-permute-start.5 = (bf16[128,4096]{1,0:T(8,128)(2,1)}, bf16[128,4096]{1,0:T(8,128)(2,1)}, u32[]{:S(2)}, u32[]{:S(2)}) collective-permute-start(bf16[128,4096]{1,0:T(8,128)(2,1)} %collective-permute-done.refs_0_), channel_id=1, source_target_pairs={{0,8},{8,0},{1,9},{9,1},{2,10},{10,2},{3,11},{11,3},{4,12},{12,4},... | collective-permute-start | bytes 3145736 | tf_op jit(solution)/shard_map/ppermute | solution.py:366
  79.6 30.1 %collective-permute-start.6 = (bf16[128,4096]{1,0:T(8,128)(2,1)}, bf16[128,4096]{1,0:T(8,128)(2,1)}, u32[]{:S(2)}, u32[]{:S(2)}) collective-permute-start(bf16[128,4096]{1,0:T(8,128)(2,1)} %collective-permute-done.1.refs_1_), channel_id=1, source_target_pairs={{0,8},{8,0},{1,9},{9,1},{2,10},{10,2},{3,11},{11,3},{4,12},{12,4},... | collective-permute-start | bytes 3145736 | tf_op jit(solution)/shard_map/ppermute | solution.py:366
  80.3 29.4 %collective-permute-start.7 = (bf16[128,4096]{1,0:T(8,128)(2,1)}, bf16[128,4096]{1,0:T(8,128)(2,1)}, u32[]{:S(2)}, u32[]{:S(2)}) collective-permute-start(bf16[128,4096]{1,0:T(8,128)(2,1)} %collective-permute-done.2.refs_2_), channel_id=1, source_target_pairs={{0,8},{8,0},{1,9},{9,1},{2,10},{10,2},{3,11},{11,3},{4,12},{12,4},... | collective-permute-start | bytes 3145736 | tf_op jit(solution)/shard_map/ppermute | solution.py:366
  91.1 18.7 %collective-permute-start.8 = (bf16[64,4096]{1,0:T(8,128)(2,1)}, bf16[64,4096]{1,0:T(8,128)(2,1)}, u32[]{:S(2)}, u32[]{:S(2)}) collective-permute-start(bf16[64,4096]{1,0:T(8,128)(2,1)} %collective-permute-done.3.refs_3_), channel_id=1, source_target_pairs={{0,8},{8,0},{1,9},{9,1},{2,10},{10,2},{3,11},{11,3},{4,12},{12,4},... | collective-permute-start | bytes 1572872 | tf_op jit(solution)/shard_map/ppermute | solution.py:366
  121.4 16.3 %collective-permute-start.42 = (bf16[4,256,256]{2,1,0:T(8,128)(2,1)S(1)}, bf16[4,256,256]{2,1,0:T(8,128)(2,1)S(1)}, u32[]{:S(2)}, u32[]{:S(2)}) collective-permute-start(bf16[4,256,256]{2,1,0:T(8,128)(2,1)S(1)} %get-tuple-element.98), channel_id=1, source_target_pairs={{0,4},{4,16},{16,20},{20,0},{1,5},{5,17},{17,21},{21,1},{2,6},{6,1... | collective-permute-start | bytes 1572872 | tf_op jit(solution)/shard_map/ppermute | solution.py:410
  122.6 27.5 %collective-permute-start.43 = (bf16[4,256,256]{2,1,0:T(8,128)(2,1)S(1)}, bf16[4,256,256]{2,1,0:T(8,128)(2,1)S(1)}, u32[]{:S(2)}, u32[]{:S(2)}) collective-permute-start(bf16[4,256,256]{2,1,0:T(8,128)(2,1)S(1)} %get-tuple-element.99), channel_id=1, source_target_pairs={{0,16},{4,20},{16,0},{20,4},{1,17},{5,21},{17,1},{21,5},{2,18},{6,... | collective-permute-start | bytes 1572872 | tf_op jit(solution)/shard_map/ppermute | solution.py:410
  126.5 23.6 %collective-permute-start.44 = (bf16[4,256,256]{2,1,0:T(8,128)(2,1)S(1)}, bf16[4,256,256]{2,1,0:T(8,128)(2,1)S(1)}, u32[]{:S(2)}, u32[]{:S(2)}) collective-permute-start(bf16[4,256,256]{2,1,0:T(8,128)(2,1)S(1)} %get-tuple-element.100), channel_id=1, source_target_pairs={{0,20},{4,0},{16,4},{20,16},{1,21},{5,1},{17,5},{21,17},{2,22},{6,... | collective-permute-start | bytes 1572872 | tf_op jit(solution)/shard_map/ppermute | solution.py:410
  128.9 28.3 %collective-permute-start.35 = (bf16[4,256,256]{2,1,0:T(8,128)(2,1)S(1)}, bf16[4,256,256]{2,1,0:T(8,128)(2,1)S(1)}, u32[]{:S(2)}, u32[]{:S(2)}) collective-permute-start(bf16[4,256,256]{2,1,0:T(8,128)(2,1)S(1)} %get-tuple-element.90), channel_id=1, source_target_pairs={{0,32},{32,64},{64,96},{96,0},{1,33},{33,65},{65,97},{97,1},{2,34}... | collective-permute-start | bytes 1572872 | tf_op jit(solution)/shard_map/ppermute | solution.py:409
  132.6 28.2 %collective-permute-start.36 = (bf16[4,256,256]{2,1,0:T(8,128)(2,1)S(1)}, bf16[4,256,256]{2,1,0:T(8,128)(2,1)S(1)}, u32[]{:S(2)}, u32[]{:S(2)}) collective-permute-start(bf16[4,256,256]{2,1,0:T(8,128)(2,1)S(1)} %get-tuple-element.91), channel_id=1, source_target_pairs={{0,64},{32,96},{64,0},{96,32},{1,65},{33,97},{65,1},{97,33},{2,66}... | collective-permute-start | bytes 1572872 | tf_op jit(solution)/shard_map/ppermute | solution.py:409
  137.6 24.2 %collective-permute-start.37 = (bf16[4,256,256]{2,1,0:T(8,128)(2,1)S(1)}, bf16[4,256,256]{2,1,0:T(8,128)(2,1)S(1)}, u32[]{:S(2)}, u32[]{:S(2)}) collective-permute-start(bf16[4,256,256]{2,1,0:T(8,128)(2,1)S(1)} %get-tuple-element.92), channel_id=1, source_target_pairs={{0,96},{32,0},{64,32},{96,64},{1,97},{33,1},{65,33},{97,65},{2,98}... | collective-permute-start | bytes 1572872 | tf_op jit(solution)/shard_map/ppermute | solution.py:409
  151.0 81.1 %collective-permute-start.45 = (bf16[256,256]{1,0:T(8,128)(2,1)}, bf16[256,256]{1,0:T(8,128)(2,1)S(1)}, u32[]{:S(2)}, u32[]{:S(2)}) collective-permute-start(bf16[256,256]{1,0:T(8,128)(2,1)} %get-tuple-element.101), channel_id=1, source_target_pairs={{0,0},{4,8},{8,4},{12,12},{32,32},{36,40},{40,36},{44,44},{64,64},... | collective-permute-start | bytes 393224 | tf_op jit(solution)/shard_map/ppermute | solution.py:422
  152.6 79.7 %collective-permute-start.46 = (bf16[256,256]{1,0:T(8,128)(2,1)}, bf16[256,256]{1,0:T(8,128)(2,1)}, u32[]{:S(2)}, u32[]{:S(2)}) collective-permute-start(bf16[256,256]{1,0:T(8,128)(2,1)} %get-tuple-element.102), channel_id=1, source_target_pairs={{0,32},{4,40},{8,36},{12,44},{32,64},{36,72},{40,68},{44,76},{64,9... | collective-permute-start | bytes 393224 | tf_op jit(solution)/shard_map/ppermute | solution.py:422
  157.1 77.8 %collective-permute-start.47 = (bf16[256,256]{1,0:T(8,128)(2,1)}, bf16[256,256]{1,0:T(8,128)(2,1)}, u32[]{:S(2)}, u32[]{:S(2)}) collective-permute-start(bf16[256,256]{1,0:T(8,128)(2,1)} %get-tuple-element.103), channel_id=1, source_target_pairs={{0,64},{4,72},{8,68},{12,76},{32,96},{36,104},{40,100},{44,108},{6... | collective-permute-start | bytes 393224 | tf_op jit(solution)/shard_map/ppermute | solution.py:422
  160.8 75.7 %collective-permute-start.48 = (bf16[256,256]{1,0:T(8,128)(2,1)}, bf16[256,256]{1,0:T(8,128)(2,1)}, u32[]{:S(2)}, u32[]{:S(2)}) collective-permute-start(bf16[256,256]{1,0:T(8,128)(2,1)} %get-tuple-element.104), channel_id=1, source_target_pairs={{0,96},{4,104},{8,100},{12,108},{32,0},{36,8},{40,4},{44,12},{64,3... | collective-permute-start | bytes 393224 | tf_op jit(solution)/shard_map/ppermute | solution.py:422
  164.6 73.4 %collective-permute-start.38 = (bf16[256,256]{1,0:T(8,128)(2,1)}, bf16[256,256]{1,0:T(8,128)(2,1)}, u32[]{:S(2)}, u32[]{:S(2)}) collective-permute-start(bf16[256,256]{1,0:T(8,128)(2,1)} %get-tuple-element.93), channel_id=1, source_target_pairs={{0,0},{4,8},{8,4},{12,12},{16,16},{20,24},{24,20},{28,28},{1,1},{5... | collective-permute-start | bytes 393224 | tf_op jit(solution)/shard_map/ppermute | solution.py:421
  (71 other events, 1139.9 us)
Sparse Core Ops, SparseCore 0:
  10.7 77.8 all-gather.3

commit v2 on v1

v2 whole, which is shorter than its diff:
```python
import functools
import math

import jax
import jax.numpy as jnp
from jax import lax
from jax.experimental import pallas as pl
from jax.experimental.pallas import tpu as pltpu
from jax.sharding import Mesh
from jax.sharding import PartitionSpec as P

GROUP = 16
TAPS = 128
BLOCKS = 8
BF = jnp.bfloat16
F32 = jnp.float32
LIMIT = 60 * 1024 * 1024
DP = ("x", "zh", "core")
SEQ = ("zl", "y")

ANY = pl.BlockSpec(memory_space=pl.ANY)
SMEM = pl.BlockSpec(memory_space=pltpu.SMEM)
VMEM = pl.BlockSpec(memory_space=pltpu.VMEM)


def call(body, out_shape, in_specs, out_specs, scratch=(), micros=1):
    return pl.pallas_call(
        body,
        out_shape=out_shape,
        in_specs=in_specs,
        out_specs=out_specs,
        scratch_shapes=list(scratch),
        compiler_params=pltpu.CompilerParams(vmem_limit_bytes=LIMIT),
        cost_estimate=pl.CostEstimate(flops=1, bytes_accessed=micros * 3000000, transcendentals=0),
    )


def shape(dims, dtype=BF):
    return jax.ShapeDtypeStruct(dims, dtype)


def table_kernel(panel_ref, filters_ref, gain_ref, table_ref, gain_out_ref):
    groups = table_ref.shape[0]
    panel = panel_ref[0]
    row = lax.broadcasted_iota(jnp.int32, (8, 2 * TAPS), 0)
    first = pl.multiple_of(panel * groups, groups)
    taps_all = filters_ref[pl.ds(first, groups), :].astype(F32)
    for g in range(groups):
        taps = jnp.broadcast_to(taps_all[g : g + 1, :], (8, TAPS))
        rows = jnp.concatenate([taps, jnp.zeros((8, TAPS), F32)], 1)
        for bit in (1, 2, 4):
            rows = jnp.where((row & bit) != 0, pltpu.roll(rows, bit, 1), rows)
        count = 8
        while count < TAPS:
            rows = jnp.concatenate([rows, pltpu.roll(rows, count, 1)], 0)
            count *= 2
        table_ref[g] = rows.astype(BF)
    gain_rows = gain_ref[panel]
    for i in range(gain_rows.shape[0]):
        gain_out_ref[TAPS * i : TAPS * (i + 1), :] = jnp.broadcast_to(
            gain_rows[i : i + 1, :], (TAPS, TAPS)
        ).T


def transpose_kernel(w_ref, out_ref):
    out_ref[...] = w_ref[...].astype(F32).T.astype(BF)


def prepare_kernel(q_ref, k_ref, v_ref, out_ref):
    width = out_ref.shape[2]
    for j in range(out_ref.shape[0]):
        cols = slice(j * width, (j + 1) * width)
        product = k_ref[:, cols].astype(F32) * v_ref[:, cols].astype(F32)
        out_ref[j, 0] = product.T.astype(BF)
        out_ref[j, 1] = q_ref[:, cols].astype(F32).T.astype(BF)


def forward_kernel(slot_ref, pq_ref, table_ref, gain_ref, mixed_ref, gated_ref):
    def one_group(g, carry):
        rows = pl.ds(pl.multiple_of(g * GROUP, GROUP), GROUP)
        x = [pq_ref[b, 0, rows, :] for b in range(BLOCKS)]
        zero = jnp.zeros((GROUP, TAPS), BF)
        lhs = jnp.concatenate(
            [jnp.concatenate(x, 0), jnp.concatenate([zero] + x[:-1], 0)], 1
        )
        table = table_ref[g]
        rhs = jnp.concatenate([table[:, :TAPS], table[:, TAPS:]], 0)
        conv = jnp.dot(lhs, rhs, preferred_element_type=F32)
        gain = gain_ref[rows, :]
        for b in range(BLOCKS):
            mixed = conv[GROUP * b : GROUP * (b + 1)] + gain * x[b].astype(F32)
            mixed_ref[b, rows, :] = mixed
            lanes = pl.ds(pl.multiple_of(slot_ref[b] * TAPS, TAPS), TAPS)
            gated_ref[rows, lanes] = (pq_ref[b, 1, rows, :].astype(F32) * mixed).astype(BF)
        return carry

    lax.fori_loop(0, table_ref.shape[0], one_group, 0, unroll=4)


def cot_copies(refs, held, sem_of, cols=slice(None)):
    copies = []
    half = TAPS // 2
    for zl in range(2):
        own, up, down, far_a, far_b = refs[5 * zl : 5 * zl + 5]
        for ref, k, first, count in (
            (own, 0, 0, TAPS),
            (up, 1, 0, TAPS),
            (far_a, 2, 0, half),
            (far_b, 2, half, half),
            (down, 3, 0, TAPS),
        ):
            slot = 4 * zl + k
            rows = slice(slot * TAPS + first, slot * TAPS + first + count)
            copies.append(
                pltpu.make_async_copy(ref.at[:, cols], held.at[rows, cols], sem_of(slot))
            )
    return copies


def weight_kernel(core_ref, *refs):
    cot = refs[:10]
    gated_ref, mine_ref, other_ref, held, total, sems, out_sems = refs[10:]
    blocks, channels, width = mine_ref.shape
    stripes = sems.shape[0]
    span = held.shape[1] // stripes
    each = blocks // stripes
    for n in range(stripes):
        for c in cot_copies(cot, held, lambda slot, n=n: sems.at[n], slice(span * n, span * (n + 1))):
            c.start()

    def out_copies(n):
        part = pl.ds(n * each, each)
        return [
            pltpu.make_async_copy(total.at[lax.rem(core_ref[0] + i, 2), part], ref.at[part], out_sems.at[i, n])
            for i, ref in enumerate((mine_ref, other_ref))
        ]

    def stripe(n, carry):
        cols = pl.ds(pl.multiple_of(n * span, span), span)
        pltpu.make_async_copy(held.at[:, cols], held.at[:, cols], sems.at[n]).wait()
        for i in range(2 * each):
            cols = pl.ds(pl.multiple_of(n * span + i * width, width), width)
            total[i % 2, n * each + i // 2] = jnp.dot(
                gated_ref[...], held[:, cols], preferred_element_type=F32
            ).astype(BF)
        for c in out_copies(n):
            c.start()
        return carry

    lax.fori_loop(0, stripes, stripe, 0)
    for n in range(stripes):
        for c in out_copies(n):
            c.wait()


def gradient_kernel(place_ref, *refs):
    cot = refs[:10]
    w_ref, mixed_ref, pq_ref, table_ref, gain_ref, gm_ref, out_ref = refs[10:17]
    held, w_held, result, sems, w_sems, out_sems = refs[17:]
    blocks, channels, width = w_ref.shape
    weights = []
    for d in range(blocks):
        weights.append(
            pltpu.make_async_copy(w_ref.at[d], w_held.at[:, width * d : width * (d + 1)], w_sems.at[d])
        )
    for c in weights + cot_copies(cot, held, lambda slot: sems.at[slot // 2]):
        c.start()
    for c in weights:
        c.wait()
    span = 2 * TAPS

    def part(n, carry):
        toks = pl.ds(pl.multiple_of(n * span, span), span)
        pltpu.make_async_copy(held.at[toks, :], held.at[toks, :], sems.at[n]).wait()
        grad = lax.dot_general(
            w_held[...], held[toks, :], (((1,), (1,)), ((), ())), preferred_element_type=F32
        )
        for i in range(2):
            one = grad[:, TAPS * i : TAPS * (i + 1)]
            place = place_ref[2 * n + i]
            result[place, 0] = (one * mixed_ref[place]).astype(BF)
            gm_ref[place] = (one * pq_ref[place, 1].astype(F32)).astype(BF)
        return carry

    lax.fori_loop(0, held.shape[0] // span, part, 0)
    back = pltpu.make_async_copy(result.at[:, 0], out_ref.at[:, 0], out_sems.at[0])
    back.start()

    def one_group(g, carry):
        rows = pl.ds(pl.multiple_of(g * GROUP, GROUP), GROUP)
        x = [gm_ref[b, rows, :] for b in range(BLOCKS)]
        zero = jnp.zeros((GROUP, TAPS), BF)
        lhs = jnp.concatenate(
            [jnp.concatenate(x, 0), jnp.concatenate(x[1:] + [zero], 0)], 1
        )
        conv = lax.dot_general(
            lhs, table_ref[g], (((1,), (1,)), ((), ())), preferred_element_type=F32
        )
        gain = gain_ref[rows, :]
        for b in range(BLOCKS):
            total = conv[GROUP * b : GROUP * (b + 1)] + gain * x[b].astype(F32)
            result[b, 1, rows, :] = total.astype(BF)
        return carry

    lax.fori_loop(0, table_ref.shape[0], one_group, 0, unroll=4)
    rest = pltpu.make_async_copy(result.at[:, 1], out_ref.at[:, 1], out_sems.at[1])
    rest.start()
    back.wait()
    rest.wait()


def filter_kernel(gm_ref, pq_ref, out_ref):
    channels = gm_ref.shape[1]
    groups = channels // GROUP
    span = 2 * TAPS
    row = lax.broadcasted_iota(jnp.int32, (8, span), 0)

    def one_group(g, carry):
        rows = pl.ds(pl.multiple_of(g * GROUP, GROUP), GROUP)
        x = jnp.concatenate([pq_ref[b, 0, rows, :] for b in range(BLOCKS)], 0)
        y = [gm_ref[b, rows, :] for b in range(BLOCKS)]
        zero = jnp.zeros((GROUP, TAPS), BF)
        window = jnp.concatenate(
            [jnp.concatenate(y, 0), jnp.concatenate(y[1:] + [zero], 0)], 1
        )
        pairs = lax.dot_general(x, window, (((0,), (0,)), ((), ())), preferred_element_type=F32)
        count = TAPS
        while count > 8:
            count //= 2
            pairs = pairs[:count] + pltpu.roll(pairs[count:], span - count, 1)
        for bit in (4, 2, 1):
            pairs = jnp.where((row & bit) != 0, pltpu.roll(pairs, span - bit, 1), pairs)
        out_ref[pl.ds(g, 1), :] = jnp.sum(pairs, 0, keepdims=True)[:, :TAPS]
        return carry

    lax.fori_loop(0, groups, one_group, 0, unroll=8)
    for i in range(channels // TAPS):
        rows = slice(TAPS * i, TAPS * (i + 1))
        total = jnp.zeros((TAPS, TAPS), F32)
        for b in range(BLOCKS):
            total += gm_ref[b, rows, :].astype(F32) * pq_ref[b, 0, rows, :].astype(F32)
        out_ref[groups + i : groups + i + 1, :] = jnp.sum(total.T, 0, keepdims=True)
    first = groups + channels // TAPS
    out_ref[first:, :] = jnp.zeros((out_ref.shape[0] - first, TAPS), F32)


def pair_kernel(order_ref, mine_ref, other_ref, sums_ref, other_sums_ref, *outs):
    channels = mine_ref.shape[1]
    small = sums_ref[...] + other_sums_ref[...]
    high = small.astype(BF)
    low = (small - high.astype(F32)).astype(BF)
    for i, out in enumerate(outs):
        to = order_ref[i]
        out[:channels] = (mine_ref[to].astype(F32) + other_ref[to].astype(F32)).astype(BF)
        out[channels:, :TAPS] = high
        out[channels:, TAPS:] = low


def total_kernel(scale, source_ref, *refs):
    pieces = refs[:8]
    weight_ref, filter_ref, gain_ref, held = refs[8:]
    channels = weight_ref.shape[1]
    total = pieces[0][:channels].astype(F32)
    for piece in pieces[1:]:
        total += piece[:channels].astype(F32)
    weight_ref[...] = (total * scale).T
    for i, piece in enumerate(pieces):
        small = piece[channels:].astype(F32)
        held[source_ref[i]] = small[:, :TAPS] + small[:, TAPS:]
    total = held[0]
    for i in range(1, 8):
        total += held[i]
    total = total * scale
    groups = filter_ref.shape[0]
    filter_ref[...] = total[:groups]
    gain_ref[...] = total[groups : groups + gain_ref.shape[0]]


def finish_kernel(k_ref, v_ref, grads_ref, gq_ref, gk_ref, gv_ref):
    width = grads_ref.shape[2]
    for j in range(grads_ref.shape[0]):
        cols = slice(j * width, (j + 1) * width)
        gq_ref[:, cols] = grads_ref[j, 0].astype(F32).T.astype(BF)
        gp = grads_ref[j, 1].astype(F32).T
        gk_ref[:, cols] = (gp * v_ref[:, cols].astype(F32)).astype(BF)
        gv_ref[:, cols] = (gp * k_ref[:, cols].astype(F32)).astype(BF)


SLOTS = [(d, k) for d in range(2) for k in range(4)]
ROUTES = [(0, 0), (2, 1), (2, 0), (1, 1), (3, 1), (0, 1), (1, 0), (3, 0)]


def after(value, *others):
    return lax.optimization_barrier((value, *others))[0]


def ring(n, k):
    return [(i, (i + k) % n) for i in range(n)]


def route(k, d):
    return [(x * 2 + zh, (x + k) % 4 * 2 + (zh ^ d)) for x in range(4) for zh in range(2)]


def numbers(values):
    return jnp.stack(values).astype(jnp.int32)


def shards(queries, key_input, value_input, cotangent, out_weight, filters, skip_gain):
    q, k, v, cot = queries[0], key_input[0], value_input[0], cotangent[0]
    rows, width = q.shape
    half = rows // 2
    panel = width // 8
    outs_here = out_weight.shape[0]
    length = rows * 8
    groups = panel // GROUP
    scale = 1.0 / math.sqrt(16 * length)
    x, zh, core, zl, y = (lax.axis_index(n) for n in ("x", "zh", "core", "zl", "y"))
    place = numbers([(zl ^ d) * 4 + (y - i) % 4 for d, i in SLOTS])
    slot_of = numbers([(zl ^ (p // 4)) * 4 + (y - p) % 4 for p in range(BLOCKS)])
    order = numbers([(x + i) % 4 * 2 + (zh ^ d) for i, d in ROUTES])
    source = numbers([(x - i) % 4 * 2 + (zh ^ d) for i, d in ROUTES])
    stream = shape((8, 2, panel, rows))

    w_t = call(transpose_kernel, shape((panel, outs_here)), [VMEM], VMEM)(out_weight)
    w_all = lax.all_gather(w_t, DP, axis=0)

    own = cot
    own_z = lax.ppermute(own, "zl", ring(2, 1))
    up = lax.ppermute(own, "y", ring(4, 1))
    down = lax.ppermute(own, "y", ring(4, -1))

    pq = call(prepare_kernel, stream, [VMEM] * 3, VMEM, micros=4)(q, k, v)
    pq = after(pq, up, down, own_z)
    pq = lax.all_to_all(pq, SEQ, split_axis=0, concat_axis=0, tiled=True)

    far_a = lax.ppermute(up[:half], "y", ring(4, 1))
    far_b = lax.ppermute(down[half:], "y", ring(4, -1))
    up_z = lax.ppermute(own_z, "y", ring(4, 1))
    down_z = lax.ppermute(own_z, "y", ring(4, -1))
    table, gain = call(
        table_kernel,
        [shape((groups, TAPS, 2 * TAPS)), shape((panel, TAPS), F32)],
        [SMEM, VMEM, VMEM],
        [VMEM, VMEM],
        micros=6,
    )((zl * 4 + y).astype(jnp.int32).reshape(1), filters, skip_gain.reshape(8, panel // TAPS, TAPS))
    mixed, gated = call(
        forward_kernel,
        [shape((BLOCKS, panel, rows), F32), shape((panel, length))],
        [SMEM] + [VMEM] * 3,
        [VMEM] * 2,
        micros=7,
    )(slot_of, pq, table, gain)
    far_a_z = lax.ppermute(far_a, "zl", ring(2, 1))
    far_b_z = lax.ppermute(far_b, "zl", ring(2, 1))
    cots = [own, up, down, far_a, far_b, own_z, up_z, down_z, far_a_z, far_b_z]

    cot_held = pltpu.VMEM((length, width), BF)
    mine, other = call(
        weight_kernel,
        [shape((8, panel, outs_here))] * 2,
        [SMEM] + [ANY] * 10 + [VMEM],
        [ANY] * 2,
        scratch=[
            cot_held,
            pltpu.VMEM((2, 8, panel, outs_here), BF),
            pltpu.SemaphoreType.DMA((4,)),
            pltpu.SemaphoreType.DMA((2, 4)),
        ],
        micros=9,
    )(core.astype(jnp.int32).reshape(1), *cots, gated)
    mixed = after(mixed, other)
    other = lax.ppermute(other, "core", ring(2, 1))

    gm, grads = call(
        gradient_kernel,
        [shape((BLOCKS, panel, rows)), stream],
        [SMEM] + [ANY] * 11 + [VMEM] * 4,
        [VMEM, ANY],
        scratch=[
            cot_held,
            pltpu.VMEM((panel, width), BF),
            pltpu.VMEM((BLOCKS, 2, panel, rows), BF),
            pltpu.SemaphoreType.DMA((4,)),
            pltpu.SemaphoreType.DMA((16,)),
            pltpu.SemaphoreType.DMA((2,)),
        ],
        micros=17,
    )(place, *cots, w_all, mixed, pq, table, gain)

    grads = lax.all_to_all(grads, SEQ, split_axis=0, concat_axis=0, tiled=True)

    sums = call(filter_kernel, shape((48, TAPS), F32), [VMEM, VMEM], VMEM, micros=6)(gm, pq)
    messages = call(
        pair_kernel,
        [shape((panel + 48, outs_here))] * 8,
        [SMEM] + [VMEM] * 4,
        [VMEM] * 8,
        micros=3,
    )(order, mine, other, sums, lax.ppermute(sums, "core", ring(2, 1)))
    messages = [messages[0]] + [
        lax.ppermute(m, ("x", "zh"), route(i, d)) for m, (i, d) in zip(messages[1:], ROUTES[1:])
    ]
    grad_query, grad_key, grad_value = call(
        finish_kernel, [shape((rows, width))] * 3, [VMEM] * 3, [VMEM] * 3, micros=5
    )(k, v, grads)
    messages[1] = after(messages[1], grad_query)
    grad_weight, grad_filters, grad_gain = call(
        functools.partial(total_kernel, scale),
        [shape((outs_here, panel), F32), shape((groups, TAPS), F32), shape((panel // TAPS, TAPS), F32)],
        [SMEM] + [VMEM] * 8,
        [VMEM] * 3,
        scratch=[pltpu.VMEM((8, 48, TAPS), F32)],
        micros=3,
    )(source, *messages)
    return (
        grad_query[None],
        grad_key[None],
        grad_value[None],
        grad_weight,
        grad_filters,
        grad_gain.reshape(panel),
    )


def solution(mesh):
    fine = Mesh(mesh.devices.reshape(4, 2, 2, 2, 4), ("x", "zh", "core", "zl", "y"))
    stream = P(DP, SEQ, None)
    return jax.shard_map(
        shards,
        mesh=fine,
        in_specs=(stream, stream, stream, stream, P(DP, SEQ), P(), P()),
        out_specs=(stream, stream, stream, P(DP, SEQ), P(SEQ, None), P(SEQ)),
        check_vma=False,
    )
```

time: 291 us -> 201 us (0.69)
  starting transfers between devices: 116 us -> 40.4 us
  blocking collectives: 34.9 us -> 0 us
  waiting for transfers between devices: 43.3 us -> 75.6 us
  local copies, waits for them, and re-layouts: 24.2 us -> 8.57 us
  Pallas kernels: 52 us -> 59.9 us
    ppermute x48 -> x16, starting transfers between devices: 114 us -> 25.4 us  [the longest x7 16.4 us: shards(): lax.ppermute(m, ('x', 'zh'), route(i, d))]
    all_gather x1 -> x0, blocking collectives: 34.9 us -> none  [shards(): sums = lax.all_gather(sums, ('x', 'zh', 'zl'), axis=0)]
    ppermute x48 -> x16, waiting for transfers between devices: 43.2 us -> 75.5 us  [the longest x1 30.5 us: shards(): far_a = lax.ppermute(up[:half], 'y', ring(4, 1))]
    unnamed x88 -> x20, local copies, waits for them, and re-layouts: 20.7 us -> 4.9 us
    all_to_all x0 -> x2, starting transfers between devices: none -> 12.9 us  [the longest x1 6.83 us: shards(): grads = lax.all_to_all(grads, SEQ, split_axis=0, concat_axis=0, tiled=True)]
    pallas_call x11 -> x9, Pallas kernels: 48.2 us -> 54 us  [the longest x1 16.4 us: shards(): call(gradient_kernel, [shape((BLOCKS, panel, rows)), stream], [SMEM] + [A...]
  transfers between devices with their start and end apart: 51 -> 21, of which waited for: 11 -> 8; matrix products, arithmetic and copies ran while one was open for 2% -> 2% of each run, Pallas kernels for 17% -> 28%
where the time goes in v2:
time: 201 us; the launch traced here: 199 us
  waiting for transfers between devices  75.6 us (38%)
  Pallas kernels  59.9 us (30%)
  starting transfers between devices  40.4 us (20%)
  between operations  14.1 us (7%)
  local copies, waits for them, and re-layouts  8.57 us (4%)
    ppermute x1, waiting for transfers between devices, shards(): far_a = lax.ppermute(up[:half], 'y', ring(4, 1))  30.5 us
    ppermute x1, waiting for transfers between devices, shards(): own_z = lax.ppermute(own, 'zl', ring(2, 1))  20.4 us
    ppermute x7, waiting for transfers between devices, shards(): lax.ppermute(m, ('x', 'zh'), route(i, d))  17.6 us
    ppermute x7, starting transfers between devices, shards(): lax.ppermute(m, ('x', 'zh'), route(i, d))  16.4 us
    pallas_call x1, Pallas kernels, shards(): call(gradient_kernel, [shape((BLOCKS, panel, rows)), stream], [SMEM] + [A...  16.4 us
    pallas_call x1, Pallas kernels, shards(): call(weight_kernel, [shape((8, panel, outs_here))] * 2, [SMEM] + [ANY] *...  8.92 us
    all_to_all x1, starting transfers between devices, shards(): grads = lax.all_to_all(grads, SEQ, split_axis=0, concat_axis=0, tiled=True)  6.83 us
    ppermute x1, waiting for transfers between devices, shards(): far_b_z = lax.ppermute(far_b, 'zl', ring(2, 1))  6.31 us
  transfers between devices with their start and end apart: 21, of which 8 were waited for; matrix products, arithmetic and copies ran while one was open for 2% of the time, Pallas kernels for 28%

profile of v2, /device:TPU:8, one launch (start us, length us, event | category | flops | bytes accessed | tf_op | source)
XLA Modules:
  0.0 198.6 jit_solution(18012757225051229331)
XLA Ops:
  7.2 1.8 shard_map.118
  9.0 2.0 %collective-permute-start.4 = (bf16[128,4096]{1,0:T(8,128)(2,1)}, bf16[128,4096]{1,0:T(8,128)(2,1)}, u32[]{:S(2)}, u32[]{:S(2)}) collective-permute-start(bf16[128,4096]{1,0:T(8,128)(2,1)} %bitcast.38), channel_id=1, source_target_pairs={{0,4},{4,0},{1,5},{5,1},{2,6},{6,2},{3,7},{7,3},{8,12},{12,8},{9,1... | collective-permute-start | bytes 3145736 | tf_op jit(solution)/shard_map/ppermute | solution.py:329
  13.1 3.9 %shard_map.119 = bf16[8,2,512,128]{3,2,1,0:T(8,128)(2,1)} custom-call(bf16[128,4096]{1,0:T(8,128)(2,1)} %bitcast.48, bf16[128,4096]{1,0:T(8,128)(2,1)} %bitcast.43, bf16[128,4096]{1,0:T(8,128)(2,1)} %bitcast.45), custom_call_target="tpu_custom_call" | custom-call | flops 1 | bytes 12000000 | tf_op jit(solution)/shard_map/pallas_call | solution.py:333
  16.9 20.4 %collective-permute-done.4.refs_5_ = bf16[128,4096]{1,0:T(8,128)(2,1)} collective-permute-done((bf16[128,4096]{1,0:T(8,128)(2,1)}, bf16[128,4096]{1,0:T(8,128)(2,1)}, u32[]{:S(2)}, u32[]{:S(2)}) %collective-permute-start.4) | collective-permute-done | bytes 1048608 | tf_op jit(solution)/shard_map/ppermute | solution.py:329
  37.3 6.1 %all-to-all-start = ((bf16[8,2,512,128]{3,2,1,0:T(8,128)(2,1)}), bf16[8,2,512,128]{3,2,1,0:T(8,128)(2,1)S(1)}, u32[]{:S(2)}, u32[]{:S(2)}) async-start(bf16[8,2,512,128]{3,2,1,0:T(8,128)(2,1)} %shard_map.119), calls=%async_computation | async-start | bytes 4194304 | tf_op jit(solution)/shard_map/all_to_all | solution.py:335
  48.7 30.5 %collective-permute-done.2.refs_3_ = bf16[64,4096]{1,0:T(8,128)(2,1)} collective-permute-done((bf16[64,4096]{1,0:T(8,128)(2,1)S(1)}, bf16[64,4096]{1,0:T(8,128)(2,1)}, u32[]{:S(2)}, u32[]{:S(2)}) %collective-permute-start.2) | collective-permute-done | bytes 524320 | tf_op jit(solution)/shard_map/ppermute | solution.py:337
  79.2 1.9 collective-permute-start.7
  82.0 5.9 %shard_map.120 = (bf16[32,128,256]{2,1,0:T(8,128)(2,1)}, f32[512,128]{1,0:T(8,128)}) custom-call(s32[1]{0:T(128)} %bitcast.17.panel_ref, bf16[256,128]{1,0:T(8,128)(2,1)} %filters_ref.1, f32[8,4,128]{2,1,0:T(4,128)} %bitcast.49), custom_call_target="tpu_custom_call" | custom-call | flops 1 | bytes 18000000 | tf_op jit(solution)/shard_map/pallas_call | solution.py:341
  89.8 5.7 %shard_map.121 = (f32[8,512,128]{2,1,0:T(8,128)}, bf16[512,1024]{1,0:T(8,128)(2,1)}) custom-call(s32[8]{0:T(128)} %stack.109.slot_ref, bf16[8,2,512,128]{3,2,1,0:T(8,128)(2,1)} %copy-done, bf16[32,128,256]{2,1,0:T(8,128)(2,1)} %get-tuple-element.32.table_ref.refs_13_, f32[512,128]{1,0:T(8,128)} %get-tuple-element.33.gain_ref.refs_14_), custom_call_target="tpu_custom_call" | custom-call | flops 1 | bytes 21000000 | tf_op jit(solution)/shard_map/pallas_call | solution.py:348
  95.5 6.3 %collective-permute-done.8.refs_9_ = bf16[64,4096]{1,0:T(8,128)(2,1)} collective-permute-done((bf16[64,4096]{1,0:T(8,128)(2,1)}, bf16[64,4096]{1,0:T(8,128)(2,1)}, u32[]{:S(2)}, u32[]{:S(2)}) %collective-permute-start.8) | collective-permute-done | bytes 524320 | tf_op jit(solution)/shard_map/ppermute | solution.py:356
  102.8 8.9 %shard_map.122 = (bf16[8,512,256]{2,1,0:T(8,128)(2,1)}, bf16[8,512,256]{2,1,0:T(8,128)(2,1)}) custom-call(s32[1]{0:T(128)} %bitcast.19.core_ref, bf16[128,4096]{1,0:T(8,128)(2,1)} %bitcast.41, bf16[128,4096]{1,0:T(8,128)(2,1)} %copy-done.2, bf16[128,4096]{1,0:T(8,128)(2,1)} %collective-permute-done.1.refs_2_, ...), custom_call_target="tpu_custom_call" | custom-call | flops 1 | bytes 27000000 | tf_op jit(solution)/shard_map/pallas_call | solution.py:360
  112.5 16.4 %shard_map.123 = (bf16[8,512,128]{2,1,0:T(8,128)(2,1)}, bf16[8,2,512,128]{3,2,1,0:T(8,128)(2,1)}) custom-call(s32[8]{0:T(128)} %stack.104.place_ref, bf16[128,4096]{1,0:T(8,128)(2,1)} %bitcast.42, bf16[128,4096]{1,0:T(8,128)(2,1)} %copy-done.2, bf16[128,4096]{1,0:T(8,128)(2,1)} %collective-permute-done.1.refs_2_, ...), custom_call_target="tpu_custom_call" | custom-call | flops 1 | bytes 51000000 | tf_op jit(solution)/shard_map/pallas_call | solution.py:376
  128.9 6.8 %all-to-all-start.1 = ((bf16[8,2,512,128]{3,2,1,0:T(8,128)(2,1)}), bf16[8,2,512,128]{3,2,1,0:T(8,128)(2,1)S(1)}, u32[]{:S(2)}, u32[]{:S(2)}) async-start(bf16[8,2,512,128]{3,2,1,0:T(8,128)(2,1)} %get-tuple-element.38), calls=%async_computation.1 | async-start | bytes 4194304 | tf_op jit(solution)/shard_map/all_to_all | solution.py:392
  135.7 6.2 %shard_map.125.sums_ref = f32[48,128]{1,0:T(8,128)} custom-call(bf16[8,512,128]{2,1,0:T(8,128)(2,1)} %get-tuple-element.43.gm_ref, bf16[8,2,512,128]{3,2,1,0:T(8,128)(2,1)} %copy-done), custom_call_target="tpu_custom_call" | custom-call | flops 1 | bytes 18000000 | tf_op jit(solution)/shard_map/pallas_call | solution.py:394
  143.9 3.8 %shard_map.126 = (bf16[560,256]{1,0:T(8,128)(2,1)}, bf16[560,256]{1,0:T(8,128)(2,1)}, bf16[560,256]{1,0:T(8,128)(2,1)}, bf16[560,256]{1,0:T(8,128)(2,1)}, bf16[5...) custom-call(s32[8]{0:T(128)} %stack.125.order_ref, ...), custom_call_target="tpu_custom_call" | custom-call | flops 1 | bytes 9000000 | tf_op jit(solution)/shard_map/pallas_call | solution.py:395
  147.7 6.0 %collective-permute-start.11 = (bf16[560,256]{1,0:T(8,128)(2,1)}, bf16[560,256]{1,0:T(8,128)(2,1)S(1)}, u32[]{:S(2)}, u32[]{:S(2)}) collective-permute-start(bf16[560,256]{1,0:T(8,128)(2,1)} %get-tuple-element.45), channel_id=1, source_target_pairs={{0,80},{16,64},{32,112},{48,96},{64,16},{80,0},{96,48},{112,32},{1... | collective-permute-start | bytes 860168 | tf_op jit(solution)/shard_map/ppermute | solution.py:403
  155.1 4.8 %collective-permute-start.14 = (bf16[560,256]{1,0:T(8,128)(2,1)}, bf16[560,256]{1,0:T(8,128)(2,1)S(1)}, u32[]{:S(2)}, u32[]{:S(2)}) collective-permute-start(bf16[560,256]{1,0:T(8,128)(2,1)} %get-tuple-element.49), channel_id=1, source_target_pairs={{0,112},{16,96},{32,16},{48,0},{64,48},{80,32},{96,80},{112,64},{1... | collective-permute-start | bytes 860168 | tf_op jit(solution)/shard_map/ppermute | solution.py:403
  160.0 7.9 %collective-permute-done.11.refs_1_ = bf16[560,256]{1,0:T(8,128)(2,1)S(1)} collective-permute-done((bf16[560,256]{1,0:T(8,128)(2,1)}, bf16[560,256]{1,0:T(8,128)(2,1)S(1)}, u32[]{:S(2)}, u32[]{:S(2)}) %collective-permute-start.11) | collective-permute-done | bytes 286752 | tf_op jit(solution)/shard_map/ppermute | solution.py:403
  167.9 4.1 %collective-permute-start.16 = (bf16[560,256]{1,0:T(8,128)(2,1)}, bf16[560,256]{1,0:T(8,128)(2,1)}, u32[]{:S(2)}, u32[]{:S(2)}) collective-permute-start(bf16[560,256]{1,0:T(8,128)(2,1)} %get-tuple-element.51), channel_id=1, source_target_pairs={{0,32},{16,48},{32,64},{48,80},{64,96},{80,112},{96,0},{112,16},{1... | collective-permute-start | bytes 860168 | tf_op jit(solution)/shard_map/ppermute | solution.py:403
  172.0 2.5 %collective-permute-done.12.refs_2_ = bf16[560,256]{1,0:T(8,128)(2,1)S(1)} collective-permute-done((bf16[560,256]{1,0:T(8,128)(2,1)}, bf16[560,256]{1,0:T(8,128)(2,1)S(1)}, u32[]{:S(2)}, u32[]{:S(2)}) %collective-permute-start.12) | collective-permute-done | bytes 286752 | tf_op jit(solution)/shard_map/ppermute | solution.py:403
  176.5 4.6 %shard_map.124 = (bf16[128,4096]{1,0:T(8,128)(2,1)}, bf16[128,4096]{1,0:T(8,128)(2,1)}, bf16[128,4096]{1,0:T(8,128)(2,1)}) custom-call(bf16[128,4096]{1,0:T(8,128)(2,1)} %bitcast.44, bf16[128,4096]{1,0:T(8,128)(2,1)} %bitcast.46, bf16[8,2,512,128]{3,2,1,0:T(8,128)(2,1)} %copy-done.1), custom_call_target="tpu_custom_call" | custom-call | flops 1 | bytes 15000000 | tf_op jit(solution)/shard_map/pallas_call | solution.py:405
  181.1 1.9 collective-permute-done.13.refs_3_
  183.0 5.4 %collective-permute-done.15.refs_5_ = bf16[560,256]{1,0:T(8,128)(2,1)S(1)} collective-permute-done((bf16[560,256]{1,0:T(8,128)(2,1)}, bf16[560,256]{1,0:T(8,128)(2,1)S(1)}, u32[]{:S(2)}, u32[]{:S(2)}) %collective-permute-start.15) | collective-permute-done | bytes 286752 | tf_op jit(solution)/shard_map/ppermute | solution.py:403
  189.0 2.7 %shard_map.127 = (f32[256,512]{1,0:T(8,128)}, f32[32,128]{1,0:T(8,128)}, f32[4,128]{1,0:T(4,128)}) custom-call(s32[8]{0:T(128)} %stack.118.source_ref, bf16[560,256]{1,0:T(8,128)(2,1)} %get-tuple-element.44.refs_0_, bf16[560,256]{1,0:T(8,128)(2,1)} %copy-done.4, bf16[560,256]{1,0:T(8,128)(2,1)} %copy-done.5, bf16[560,256]{1,0:T(8,128)(2,1)} %copy-done.6, ...), custom_call_target="tpu_custom_call" | custom-call | flops 1 | bytes 9000000 | tf_op jit(solution)/shard_map/pallas_call | solution.py:409
  (55 shorter events, 18.0 us)
Async XLA Ops:
  7.2 105.3 %all-gather.3.cloned.1.call-start = ((), (), s32[]{:S(2)}) async-start(), calls=%async_computation.2 | async-start | bytes 4456448 | tf_op jit(solution)/shard_map/all_gather | solution.py:326
  9.0 28.3 %collective-permute-start.4 = (bf16[128,4096]{1,0:T(8,128)(2,1)}, bf16[128,4096]{1,0:T(8,128)(2,1)}, u32[]{:S(2)}, u32[]{:S(2)}) collective-permute-start(bf16[128,4096]{1,0:T(8,128)(2,1)} %bitcast.38), channel_id=1, source_target_pairs={{0,4},{4,0},{1,5},{5,1},{2,6},{6,2},{3,7},{7,3},{8,12},{12,8},{9,1... | collective-permute-start | bytes 3145736 | tf_op jit(solution)/shard_map/ppermute | solution.py:329
  11.0 26.3 %collective-permute-start = (bf16[128,4096]{1,0:T(8,128)(2,1)}, bf16[128,4096]{1,0:T(8,128)(2,1)S(1)}, u32[]{:S(2)}, u32[]{:S(2)}) collective-permute-start(bf16[128,4096]{1,0:T(8,128)(2,1)} %bitcast.39), channel_id=1, source_target_pairs={{0,1},{1,2},{2,3},{3,0},{4,5},{5,6},{6,7},{7,4},{8,9},{9,10},{10,1... | collective-permute-start | bytes 3145736 | tf_op jit(solution)/shard_map/ppermute | solution.py:330
  12.6 24.7 %collective-permute-start.1 = (bf16[128,4096]{1,0:T(8,128)(2,1)}, bf16[128,4096]{1,0:T(8,128)(2,1)}, u32[]{:S(2)}, u32[]{:S(2)}) collective-permute-start(bf16[128,4096]{1,0:T(8,128)(2,1)} %bitcast.40), channel_id=1, source_target_pairs={{0,3},{1,0},{2,1},{3,2},{4,7},{5,4},{6,5},{7,6},{8,11},{9,8},{10,9... | collective-permute-start | bytes 3145736 | tf_op jit(solution)/shard_map/ppermute | solution.py:331
  37.3 6.1 %copy-start.2 = (bf16[128,4096]{1,0:T(8,128)(2,1)}, bf16[128,4096]{1,0:T(8,128)(2,1)S(1)}, u32[]{:S(2)}) copy-start(bf16[128,4096]{1,0:T(8,128)(2,1)S(1)} %collective-permute-done.refs_1_) | copy-start | bytes 3145732
  37.3 51.2 %all-to-all-start = ((bf16[8,2,512,128]{3,2,1,0:T(8,128)(2,1)}), bf16[8,2,512,128]{3,2,1,0:T(8,128)(2,1)S(1)}, u32[]{:S(2)}, u32[]{:S(2)}) async-start(bf16[8,2,512,128]{3,2,1,0:T(8,128)(2,1)} %shard_map.119), calls=%async_computation | async-start | bytes 4194304 | tf_op jit(solution)/shard_map/all_to_all | solution.py:335
  43.5 35.8 %collective-permute-start.2 = (bf16[64,4096]{1,0:T(8,128)(2,1)S(1)}, bf16[64,4096]{1,0:T(8,128)(2,1)}, u32[]{:S(2)}, u32[]{:S(2)}) collective-permute-start(bf16[64,4096]{1,0:T(8,128)(2,1)S(1)} %slice.8), channel_id=1, source_target_pairs={{0,1},{1,2},{2,3},{3,0},{4,5},{5,6},{6,7},{7,4},{8,9},{9,10},{10,1... | collective-permute-start | bytes 1572872 | tf_op jit(solution)/shard_map/ppermute | solution.py:337
  46.1 35.1 %collective-permute-start.3 = (bf16[64,4096]{1,0:T(8,128)(2,1)S(1)}, bf16[64,4096]{1,0:T(8,128)(2,1)}, u32[]{:S(2)}, u32[]{:S(2)}) collective-permute-start(bf16[64,4096]{1,0:T(8,128)(2,1)S(1)} %slice.9), channel_id=1, source_target_pairs={{0,3},{1,0},{2,1},{3,2},{4,7},{5,4},{6,5},{7,6},{8,11},{9,8},{10,9... | collective-permute-start | bytes 1572872 | tf_op jit(solution)/shard_map/ppermute | solution.py:338
  46.7 55.1 %collective-permute-start.5 = (bf16[128,4096]{1,0:T(8,128)(2,1)}, bf16[128,4096]{1,0:T(8,128)(2,1)S(1)}, u32[]{:S(2)}, u32[]{:S(2)}) collective-permute-start(bf16[128,4096]{1,0:T(8,128)(2,1)} %collective-permute-done.4.refs_5_), channel_id=1, source_target_pairs={{0,1},{1,2},{2,3},{3,0},{4,5},{5,6},{6,7},{7,4},{8,9},{9,10},{10,1... | collective-permute-start | bytes 3145736 | tf_op jit(solution)/shard_map/ppermute | solution.py:339
  48.2 53.7 %collective-permute-start.6 = (bf16[128,4096]{1,0:T(8,128)(2,1)}, bf16[128,4096]{1,0:T(8,128)(2,1)}, u32[]{:S(2)}, u32[]{:S(2)}) collective-permute-start(bf16[128,4096]{1,0:T(8,128)(2,1)} %collective-permute-done.4.refs_5_), channel_id=1, source_target_pairs={{0,3},{1,0},{2,1},{3,2},{4,7},{5,4},{6,5},{7,6},{8,11},{9,8},{10,9... | collective-permute-start | bytes 3145736 | tf_op jit(solution)/shard_map/ppermute | solution.py:340
  79.2 16.3 %collective-permute-start.7 = (bf16[64,4096]{1,0:T(8,128)(2,1)}, bf16[64,4096]{1,0:T(8,128)(2,1)}, u32[]{:S(2)}, u32[]{:S(2)}) collective-permute-start(bf16[64,4096]{1,0:T(8,128)(2,1)} %collective-permute-done.2.refs_3_), channel_id=1, source_target_pairs={{0,4},{4,0},{1,5},{5,1},{2,6},{6,2},{3,7},{7,3},{8,12},{12,8},{9,1... | collective-permute-start | bytes 1572872 | tf_op jit(solution)/shard_map/ppermute | solution.py:355
  81.2 20.7 %collective-permute-start.8 = (bf16[64,4096]{1,0:T(8,128)(2,1)}, bf16[64,4096]{1,0:T(8,128)(2,1)}, u32[]{:S(2)}, u32[]{:S(2)}) collective-permute-start(bf16[64,4096]{1,0:T(8,128)(2,1)} %collective-permute-done.3.refs_4_), channel_id=1, source_target_pairs={{0,4},{4,0},{1,5},{5,1},{2,6},{6,2},{3,7},{7,3},{8,12},{12,8},{9,1... | collective-permute-start | bytes 1572872 | tf_op jit(solution)/shard_map/ppermute | solution.py:356
  111.8 30.8 %collective-permute-start.9 = (bf16[8,512,256]{2,1,0:T(8,128)(2,1)}, bf16[8,512,256]{2,1,0:T(8,128)(2,1)}, u32[]{:S(2)}, u32[]{:S(2)}) collective-permute-start(bf16[8,512,256]{2,1,0:T(8,128)(2,1)} %get-tuple-element.36), channel_id=1, source_target_pairs={{0,8},{8,0},{1,9},{9,1},{2,10},{10,2},{3,11},{11,3},{4,12},{12,4},... | collective-permute-start | bytes 6291464 | tf_op jit(solution)/shard_map/ppermute | solution.py:374
  128.9 46.3 %all-to-all-start.1 = ((bf16[8,2,512,128]{3,2,1,0:T(8,128)(2,1)}), bf16[8,2,512,128]{3,2,1,0:T(8,128)(2,1)S(1)}, u32[]{:S(2)}, u32[]{:S(2)}) async-start(bf16[8,2,512,128]{3,2,1,0:T(8,128)(2,1)} %get-tuple-element.38), calls=%async_computation.1 | async-start | bytes 4194304 | tf_op jit(solution)/shard_map/all_to_all | solution.py:392
  141.9 1.4 collective-permute-start.10
  147.7 20.2 %collective-permute-start.11 = (bf16[560,256]{1,0:T(8,128)(2,1)}, bf16[560,256]{1,0:T(8,128)(2,1)S(1)}, u32[]{:S(2)}, u32[]{:S(2)}) collective-permute-start(bf16[560,256]{1,0:T(8,128)(2,1)} %get-tuple-element.45), channel_id=1, source_target_pairs={{0,80},{16,64},{32,112},{48,96},{64,16},{80,0},{96,48},{112,32},{1... | collective-permute-start | bytes 860168 | tf_op jit(solution)/shard_map/ppermute | solution.py:403
  153.7 20.8 %collective-permute-start.12 = (bf16[560,256]{1,0:T(8,128)(2,1)}, bf16[560,256]{1,0:T(8,128)(2,1)S(1)}, u32[]{:S(2)}, u32[]{:S(2)}) collective-permute-start(bf16[560,256]{1,0:T(8,128)(2,1)} %get-tuple-element.47), channel_id=1, source_target_pairs={{0,64},{16,80},{32,96},{48,112},{64,0},{80,16},{96,32},{112,48},{1... | collective-permute-start | bytes 860168 | tf_op jit(solution)/shard_map/ppermute | solution.py:403
  154.2 28.7 %collective-permute-start.13 = (bf16[560,256]{1,0:T(8,128)(2,1)}, bf16[560,256]{1,0:T(8,128)(2,1)S(1)}, u32[]{:S(2)}, u32[]{:S(2)}) collective-permute-start(bf16[560,256]{1,0:T(8,128)(2,1)} %get-tuple-element.48), channel_id=1, source_target_pairs={{0,48},{16,32},{32,80},{48,64},{64,112},{80,96},{96,16},{112,0},{1... | collective-permute-start | bytes 860168 | tf_op jit(solution)/shard_map/ppermute | solution.py:403
  155.1 27.8 %collective-permute-start.14 = (bf16[560,256]{1,0:T(8,128)(2,1)}, bf16[560,256]{1,0:T(8,128)(2,1)S(1)}, u32[]{:S(2)}, u32[]{:S(2)}) collective-permute-start(bf16[560,256]{1,0:T(8,128)(2,1)} %get-tuple-element.49), channel_id=1, source_target_pairs={{0,112},{16,96},{32,16},{48,0},{64,48},{80,32},{96,80},{112,64},{1... | collective-permute-start | bytes 860168 | tf_op jit(solution)/shard_map/ppermute | solution.py:403
  159.9 28.4 %collective-permute-start.15 = (bf16[560,256]{1,0:T(8,128)(2,1)}, bf16[560,256]{1,0:T(8,128)(2,1)S(1)}, u32[]{:S(2)}, u32[]{:S(2)}) collective-permute-start(bf16[560,256]{1,0:T(8,128)(2,1)} %get-tuple-element.50), channel_id=1, source_target_pairs={{0,16},{16,0},{32,48},{48,32},{64,80},{80,64},{96,112},{112,96},{1... | collective-permute-start | bytes 860168 | tf_op jit(solution)/shard_map/ppermute | solution.py:403
  167.9 20.4 %copy-start.4 = (bf16[560,256]{1,0:T(8,128)(2,1)}, bf16[560,256]{1,0:T(8,128)(2,1)S(1)}, u32[]{:S(2)}) copy-start(bf16[560,256]{1,0:T(8,128)(2,1)S(1)} %collective-permute-done.11.refs_1_) | copy-start | bytes 860164
  167.9 20.4 %collective-permute-start.16 = (bf16[560,256]{1,0:T(8,128)(2,1)}, bf16[560,256]{1,0:T(8,128)(2,1)}, u32[]{:S(2)}, u32[]{:S(2)}) collective-permute-start(bf16[560,256]{1,0:T(8,128)(2,1)} %get-tuple-element.51), channel_id=1, source_target_pairs={{0,32},{16,48},{32,64},{48,80},{64,96},{80,112},{96,0},{112,16},{1... | collective-permute-start | bytes 860168 | tf_op jit(solution)/shard_map/ppermute | solution.py:403
  174.5 13.9 %copy-start.5 = (bf16[560,256]{1,0:T(8,128)(2,1)}, bf16[560,256]{1,0:T(8,128)(2,1)S(1)}, u32[]{:S(2)}) copy-start(bf16[560,256]{1,0:T(8,128)(2,1)S(1)} %collective-permute-done.12.refs_2_) | copy-start | bytes 860164
  174.5 13.8 %collective-permute-start.17 = (bf16[560,256]{1,0:T(8,128)(2,1)}, bf16[560,256]{1,0:T(8,128)(2,1)}, u32[]{:S(2)}, u32[]{:S(2)}) collective-permute-start(bf16[560,256]{1,0:T(8,128)(2,1)} %get-tuple-element.52), channel_id=1, source_target_pairs={{0,96},{16,112},{32,0},{48,16},{64,32},{80,48},{96,64},{112,80},{1... | collective-permute-start | bytes 860168 | tf_op jit(solution)/shard_map/ppermute | solution.py:403
  (7 other events, 15.8 us)
Sparse Core Ops, SparseCore 0:
  11.0 78.9 all-gather.2

commit v3 on v2

v3 whole, which is shorter than its diff:
```python
import functools
import math

import jax
import jax.numpy as jnp
from jax import lax
from jax.experimental import pallas as pl
from jax.experimental.pallas import tpu as pltpu
from jax.sharding import Mesh
from jax.sharding import PartitionSpec as P

GROUP = 16
TAPS = 128
BLOCKS = 8
SMALL = 48
BF = jnp.bfloat16
F32 = jnp.float32
LIMIT = 60 * 1024 * 1024
DP = ("x", "zh", "core")
SEQ = ("zl", "y")

ANY = pl.BlockSpec(memory_space=pl.ANY)
SMEM = pl.BlockSpec(memory_space=pltpu.SMEM)
VMEM = pl.BlockSpec(memory_space=pltpu.VMEM)


def call(body, out_shape, in_specs, out_specs, scratch=(), micros=0):
    return pl.pallas_call(
        body,
        out_shape=out_shape,
        in_specs=in_specs,
        out_specs=out_specs,
        scratch_shapes=list(scratch),
        compiler_params=pltpu.CompilerParams(vmem_limit_bytes=LIMIT),
        cost_estimate=pl.CostEstimate(flops=1, bytes_accessed=1 + micros * 3000000, transcendentals=0),
    )


def shape(dims, dtype=BF):
    return jax.ShapeDtypeStruct(dims, dtype)


def table_kernel(panel_ref, filters_ref, gain_ref, table_ref, gain_out_ref):
    groups = table_ref.shape[0]
    panel = panel_ref[0]
    row = lax.broadcasted_iota(jnp.int32, (8, 2 * TAPS), 0)
    first = pl.multiple_of(panel * groups, groups)
    taps_all = filters_ref[pl.ds(first, groups), :].astype(F32)
    for g in range(groups):
        taps = jnp.broadcast_to(taps_all[g : g + 1, :], (8, TAPS))
        rows = jnp.concatenate([taps, jnp.zeros((8, TAPS), F32)], 1)
        for bit in (1, 2, 4):
            rows = jnp.where((row & bit) != 0, pltpu.roll(rows, bit, 1), rows)
        count = 8
        while count < TAPS:
            rows = jnp.concatenate([rows, pltpu.roll(rows, count, 1)], 0)
            count *= 2
        table_ref[g] = rows.astype(BF)
    gain_rows = gain_ref[panel]
    for i in range(gain_rows.shape[0]):
        gain_out_ref[TAPS * i : TAPS * (i + 1), :] = jnp.broadcast_to(
            gain_rows[i : i + 1, :], (TAPS, TAPS)
        ).T


def transpose_kernel(w_ref, out_ref):
    out_ref[...] = w_ref[...].astype(F32).T.astype(BF)


def prepare_kernel(q_ref, k_ref, v_ref, out_ref):
    width = out_ref.shape[2]
    for j in range(out_ref.shape[0]):
        cols = slice(j * width, (j + 1) * width)
        product = k_ref[:, cols].astype(F32) * v_ref[:, cols].astype(F32)
        out_ref[j, 0] = product.T.astype(BF)
        out_ref[j, 1] = q_ref[:, cols].astype(F32).T.astype(BF)


def forward_kernel(slot_ref, pq_ref, table_ref, gain_ref, mixed_ref, gated_ref):
    def one_group(g, carry):
        rows = pl.ds(pl.multiple_of(g * GROUP, GROUP), GROUP)
        x = [pq_ref[b, 0, rows, :] for b in range(BLOCKS)]
        zero = jnp.zeros((GROUP, TAPS), BF)
        lhs = jnp.concatenate(
            [jnp.concatenate(x, 0), jnp.concatenate([zero] + x[:-1], 0)], 1
        )
        table = table_ref[g]
        rhs = jnp.concatenate([table[:, :TAPS], table[:, TAPS:]], 0)
        conv = jnp.dot(lhs, rhs, preferred_element_type=F32)
        gain = gain_ref[rows, :]
        for b in range(BLOCKS):
            mixed = conv[GROUP * b : GROUP * (b + 1)] + gain * x[b].astype(F32)
            mixed_ref[b, rows, :] = mixed
            lanes = pl.ds(pl.multiple_of(slot_ref[b] * TAPS, TAPS), TAPS)
            gated_ref[rows, lanes] = (pq_ref[b, 1, rows, :].astype(F32) * mixed).astype(BF)
        return carry

    lax.fori_loop(0, table_ref.shape[0], one_group, 0, unroll=4)


def backward_kernel(grad_ref, mixed_ref, pq_ref, table_ref, gain_ref, gm_ref, out_ref):
    def one_group(g, carry):
        rows = pl.ds(pl.multiple_of(g * GROUP, GROUP), GROUP)
        table = table_ref[g]
        gain = gain_ref[rows, :]
        zero = jnp.zeros((GROUP, TAPS), BF)
        x = []
        for b in range(BLOCKS):
            grad = grad_ref[b, rows, :]
            out_ref[b, 0, rows, :] = (grad * mixed_ref[b, rows, :]).astype(BF)
            x.append((grad * pq_ref[b, 1, rows, :].astype(F32)).astype(BF))
            gm_ref[b, rows, :] = x[b]
        lhs = jnp.concatenate(
            [jnp.concatenate(x, 0), jnp.concatenate(x[1:] + [zero], 0)], 1
        )
        conv = lax.dot_general(lhs, table, (((1,), (1,)), ((), ())), preferred_element_type=F32)
        for b in range(BLOCKS):
            total = conv[GROUP * b : GROUP * (b + 1)] + gain * x[b].astype(F32)
            out_ref[b, 1, rows, :] = total.astype(BF)
        return carry

    lax.fori_loop(0, table_ref.shape[0], one_group, 0, unroll=4)


def cot_copies(refs, held, sem_of, cols=slice(None)):
    copies = []
    half = TAPS // 2
    for zl in range(2):
        own, up, down, far_a, far_b = refs[5 * zl : 5 * zl + 5]
        for ref, k, first, count in (
            (own, 0, 0, TAPS),
            (up, 1, 0, TAPS),
            (far_a, 2, 0, half),
            (far_b, 2, half, half),
            (down, 3, 0, TAPS),
        ):
            slot = 4 * zl + k
            rows = slice(slot * TAPS + first, slot * TAPS + first + count)
            copies.append(
                pltpu.make_async_copy(ref.at[:, cols], held.at[rows, cols], sem_of(slot))
            )
    return copies


def product_kernel(core_ref, place_ref, *refs):
    cot = refs[:10]
    gated_ref, w_ref, mine_ref, other_ref, grad_ref, held, w_held, total, sems, w_sems, out_sems = refs[10:]
    blocks, channels, width = mine_ref.shape
    stripes = sems.shape[0]
    span = held.shape[1] // stripes
    each = blocks // stripes
    for n in range(stripes):
        for c in cot_copies(cot, held, lambda slot, n=n: sems.at[n], slice(span * n, span * (n + 1))):
            c.start()
    weights = []
    for d in range(2 * blocks):
        weights.append(
            pltpu.make_async_copy(w_ref.at[d], w_held.at[:, width * d : width * (d + 1)], w_sems.at[d])
        )
    for c in weights:
        c.start()

    def out_copies(n):
        part = pl.ds(n * each, each)
        return [
            pltpu.make_async_copy(total.at[lax.rem(core_ref[0] + i, 2), part], ref.at[part], out_sems.at[i, n])
            for i, ref in enumerate((mine_ref, other_ref))
        ]

    def stripe(n, carry):
        cols = pl.ds(pl.multiple_of(n * span, span), span)
        pltpu.make_async_copy(held.at[:, cols], held.at[:, cols], sems.at[n]).wait()
        grad = jnp.dot(gated_ref[...], held[:, cols], preferred_element_type=F32)
        for i in range(2 * each):
            total[i % 2, n * each + i // 2] = grad[:, width * i : width * (i + 1)].astype(BF)
        for c in out_copies(n):
            c.start()
        return carry

    lax.fori_loop(0, stripes, stripe, 0)
    for c in weights:
        c.wait()
    span = 4 * TAPS

    def tokens(n, carry):
        toks = pl.ds(pl.multiple_of(n * span, span), span)
        grad = lax.dot_general(
            w_held[...], held[toks, :], (((1,), (1,)), ((), ())), preferred_element_type=F32
        )
        for i in range(4):
            grad_ref[place_ref[4 * n + i]] = grad[:, TAPS * i : TAPS * (i + 1)]
        return carry

    lax.fori_loop(0, 2, tokens, 0)
    for n in range(stripes):
        for c in out_copies(n):
            c.wait()


def filter_kernel(gm_ref, pq_ref, out_ref):
    channels = gm_ref.shape[1]
    groups = channels // GROUP
    span = 2 * TAPS
    row = lax.broadcasted_iota(jnp.int32, (8, span), 0)

    def one_group(g, carry):
        rows = pl.ds(pl.multiple_of(g * GROUP, GROUP), GROUP)
        x = jnp.concatenate([pq_ref[b, 0, rows, :] for b in range(BLOCKS)], 0)
        y = [gm_ref[b, rows, :] for b in range(BLOCKS)]
        zero = jnp.zeros((GROUP, TAPS), BF)
        window = jnp.concatenate(
            [jnp.concatenate(y, 0), jnp.concatenate(y[1:] + [zero], 0)], 1
        )
        pairs = lax.dot_general(x, window, (((0,), (0,)), ((), ())), preferred_element_type=F32)
        count = TAPS
        while count > 8:
            count //= 2
            pairs = pairs[:count] + pltpu.roll(pairs[count:], span - count, 1)
        for bit in (4, 2, 1):
            pairs = jnp.where((row & bit) != 0, pltpu.roll(pairs, span - bit, 1), pairs)
        out_ref[pl.ds(g, 1), :] = jnp.sum(pairs, 0, keepdims=True)[:, :TAPS]
        return carry

    lax.fori_loop(0, groups, one_group, 0, unroll=8)
    for i in range(channels // TAPS):
        rows = slice(TAPS * i, TAPS * (i + 1))
        total = jnp.zeros((TAPS, TAPS), F32)
        for b in range(BLOCKS):
            total += gm_ref[b, rows, :].astype(F32) * pq_ref[b, 0, rows, :].astype(F32)
        out_ref[groups + i : groups + i + 1, :] = jnp.sum(total.T, 0, keepdims=True)
    first = groups + channels // TAPS
    out_ref[first:, :] = jnp.zeros((out_ref.shape[0] - first, TAPS), F32)


def put_small(ref, small):
    high = small.astype(BF)
    rows = slice(ref.shape[0] - small.shape[0], ref.shape[0])
    ref[rows, :TAPS] = high
    ref[rows, TAPS:] = (small - high.astype(F32)).astype(BF)


def get_small(piece):
    small = piece[piece.shape[0] - SMALL :].astype(F32)
    return small[:, :TAPS] + small[:, TAPS:]


def pair_kernel(order_ref, mine_ref, other_ref, *outs):
    for i, out in enumerate(outs):
        for d in range(2):
            to = order_ref[i] * 2 + d
            out[d] = (mine_ref[to].astype(F32) + other_ref[to].astype(F32)).astype(BF)


def line_kernel(source_ref, zh_ref, *refs):
    pieces, smalls, outs, held = refs[:4], refs[4:8], refs[8:10], refs[10]
    channels = pieces[0].shape[1]
    for i, piece in enumerate(smalls):
        held[source_ref[i]] = piece[...]
    small = ((held[0] + held[1]) + held[2]) + held[3]
    for out, zh in zip(outs, (zh_ref[0], 1 - zh_ref[0])):
        total = pieces[0][zh].astype(F32)
        for piece in pieces[1:]:
            total += piece[zh].astype(F32)
        out[:channels] = total.astype(BF)
        put_small(out, small)


def total_kernel(scale, mine_ref, other_ref, weight_ref, filter_ref, gain_ref):
    channels = weight_ref.shape[1]
    total = mine_ref[:channels].astype(F32) + other_ref[:channels].astype(F32)
    weight_ref[...] = (total * scale).T
    small = (get_small(mine_ref[...]) + get_small(other_ref[...])) * scale
    groups = filter_ref.shape[0]
    filter_ref[...] = small[:groups]
    gain_ref[...] = small[groups : groups + gain_ref.shape[0]]


def finish_kernel(k_ref, v_ref, grads_ref, gq_ref, gk_ref, gv_ref):
    width = grads_ref.shape[2]
    for j in range(grads_ref.shape[0]):
        cols = slice(j * width, (j + 1) * width)
        gq_ref[:, cols] = grads_ref[j, 0].astype(F32).T.astype(BF)
        gp = grads_ref[j, 1].astype(F32).T
        gk_ref[:, cols] = (gp * v_ref[:, cols].astype(F32)).astype(BF)
        gv_ref[:, cols] = (gp * k_ref[:, cols].astype(F32)).astype(BF)


SLOTS = [(d, k) for d in range(2) for k in range(4)]


def after(value, *others):
    return lax.optimization_barrier((value, *others))[0]


def ring(n, k):
    return [(i, (i + k) % n) for i in range(n)]


def numbers(values):
    return jnp.stack(values).astype(jnp.int32)


def shards(queries, key_input, value_input, cotangent, out_weight, filters, skip_gain):
    q, k, v, cot = queries[0], key_input[0], value_input[0], cotangent[0]
    rows, width = q.shape
    half = rows // 2
    panel = width // 8
    outs_here = out_weight.shape[0]
    length = rows * 8
    groups = panel // GROUP
    scale = 1.0 / math.sqrt(16 * length)
    x, zh, core, zl, y = (lax.axis_index(n) for n in ("x", "zh", "core", "zl", "y"))
    place = numbers([(zl ^ d) * 4 + (y - i) % 4 for d, i in SLOTS])
    slot_of = numbers([(zl ^ (p // 4)) * 4 + (y - p) % 4 for p in range(BLOCKS)])
    order = numbers([(x + i) % 4 for i in range(4)])
    source = numbers([(x - i) % 4 for i in range(4)])
    stream = shape((8, 2, panel, rows))

    w_t = call(transpose_kernel, shape((panel, outs_here)), [VMEM], VMEM)(out_weight)
    w_all = lax.all_gather(w_t, DP, axis=0)

    own = cot
    own_z = lax.ppermute(own, "zl", ring(2, 1))
    up = lax.ppermute(own, "y", ring(4, 1))
    down = lax.ppermute(own, "y", ring(4, -1))

    pq = call(prepare_kernel, stream, [VMEM] * 3, VMEM)(q, k, v)
    table, gain = call(
        table_kernel,
        [shape((groups, TAPS, 2 * TAPS)), shape((panel, TAPS), F32)],
        [SMEM, VMEM, VMEM],
        [VMEM, VMEM],
    )((zl * 4 + y).astype(jnp.int32).reshape(1), filters, skip_gain.reshape(8, panel // TAPS, TAPS))
    up, down, own_z, table = lax.optimization_barrier((up, down, own_z, table))
    far_a = lax.ppermute(up[:half], "y", ring(4, 1))
    far_b = lax.ppermute(down[half:], "y", ring(4, -1))
    up_z = lax.ppermute(own_z, "y", ring(4, 1))
    down_z = lax.ppermute(own_z, "y", ring(4, -1))
    far_a_z = lax.ppermute(far_a, "zl", ring(2, 1))
    far_b_z = lax.ppermute(far_b, "zl", ring(2, 1))
    cots = [own, up, down, far_a, far_b, own_z, up_z, down_z, far_a_z, far_b_z]
    pq = lax.all_to_all(pq, SEQ, split_axis=0, concat_axis=0, tiled=True)

    mixed, gated = call(
        forward_kernel,
        [shape((BLOCKS, panel, rows), F32), shape((panel, length))],
        [SMEM] + [VMEM] * 3,
        [VMEM] * 2,
    )(slot_of, pq, table, gain)

    by_core = (8, panel, outs_here)
    mine, other, grad = call(
        product_kernel,
        [shape(by_core), shape(by_core), shape((BLOCKS, panel, rows), F32)],
        [SMEM] * 2 + [ANY] * 10 + [VMEM, ANY],
        [ANY, ANY, VMEM],
        scratch=[
            pltpu.VMEM((length, width), BF),
            pltpu.VMEM((panel, width), BF),
            pltpu.VMEM((2, *by_core), BF),
            pltpu.SemaphoreType.DMA((4,)),
            pltpu.SemaphoreType.DMA((16,)),
            pltpu.SemaphoreType.DMA((2, 4)),
        ],
        micros=100,
    )(core.astype(jnp.int32).reshape(1), place, *cots, gated, w_all)
    other = lax.ppermute(other, "core", ring(2, 1))

    gm, grads = call(
        backward_kernel,
        [shape((BLOCKS, panel, rows)), stream],
        [VMEM] * 5,
        [VMEM] * 2,
    )(grad, mixed, pq, table, gain)
    mine = after(mine, gm)
    grads = lax.all_to_all(grads, SEQ, split_axis=0, concat_axis=0, tiled=True)

    lines = call(
        pair_kernel, [shape((2, panel, outs_here))] * 4, [SMEM] + [VMEM] * 2, [VMEM] * 4
    )(order, mine, other)
    gm = after(gm, lines[0])
    lines = [lines[0]] + [lax.ppermute(lines[i], "x", ring(4, i)) for i in (1, 2, 3)]
    sums = call(filter_kernel, shape((SMALL, TAPS), F32), [VMEM, VMEM], VMEM)(gm, pq)
    sums = sums + lax.ppermute(sums, "core", ring(2, 1))
    sums = [sums] + [lax.ppermute(sums, "x", ring(4, i)) for i in (1, 2, 3)]
    keep, send = call(
        line_kernel,
        [shape((panel + SMALL, outs_here))] * 2,
        [SMEM] * 2 + [VMEM] * 8,
        [VMEM] * 2,
        scratch=[pltpu.VMEM((4, SMALL, TAPS), F32)],
    )(source, zh.astype(jnp.int32).reshape(1), *lines, *sums)
    send = lax.ppermute(send, "zh", ring(2, 1))
    grad_query, grad_key, grad_value = call(
        finish_kernel, [shape((rows, width))] * 3, [VMEM] * 3, [VMEM] * 3
    )(k, v, grads)
    grad_weight, grad_filters, grad_gain = call(
        functools.partial(total_kernel, scale),
        [shape((outs_here, panel), F32), shape((groups, TAPS), F32), shape((panel // TAPS, TAPS), F32)],
        [VMEM] * 2,
        [VMEM] * 3,
    )(keep, send)
    return (
        grad_query[None],
        grad_key[None],
        grad_value[None],
        grad_weight,
        grad_filters,
        grad_gain.reshape(panel),
    )


def solution(mesh):
    fine = Mesh(mesh.devices.reshape(4, 2, 2, 2, 4), ("x", "zh", "core", "zl", "y"))
    stream = P(DP, SEQ, None)
    return jax.shard_map(
        shards,
        mesh=fine,
        in_specs=(stream, stream, stream, stream, P(DP, SEQ), P(), P()),
        out_specs=(stream, stream, stream, P(DP, SEQ), P(SEQ, None), P(SEQ)),
        check_vma=False,
    )
```

time: 201 us -> 182 us (0.905); the launches traced: 199 us -> 182 us
  waiting for transfers between devices: 75.6 us -> 48.6 us
  starting transfers between devices: 40.4 us -> 52.4 us
    ppermute x1, waiting for transfers between devices: 30.5 us -> 9.12 us  [shards(): far_a = lax.ppermute(up[:half], 'y', ring(4, 1))]
    ppermute x1, waiting for transfers between devices: 20.4 us -> 0.01 us  [shards(): own_z = lax.ppermute(own, 'zl', ring(2, 1))]
    ppermute x1, waiting for transfers between devices: 0.01 us -> 17.4 us  [shards(): up = lax.ppermute(own, 'y', ring(4, 1))]
    ppermute x1, starting transfers between devices: 1.53 us -> 18.6 us  [shards(): far_a = lax.ppermute(up[:half], 'y', ring(4, 1))]
    ppermute x8, starting transfers between devices: 16.4 us -> 11.3 us  [the longest x3 5.65 us: shards(): lax.ppermute(lines[i], 'x', ring(4, i))]
    ppermute x1, waiting for transfers between devices: 6.31 us -> 3.91 us  [shards(): far_b_z = lax.ppermute(far_b, 'zl', ring(2, 1))]
    pallas_call x6 -> x7, Pallas kernels: 43.8 us -> 42.6 us  [the longest x1 14.2 us: shards(): call(product_kernel, [shape(by_core), shape(by_core), shape((BLOCKS, pane...]
  transfers between devices with their start and end apart: 21 -> 21, of which waited for: 8 -> 8; matrix products, arithmetic and copies ran while one was open for 2% -> 2% of each run, Pallas kernels for 28% -> 22%
where the time goes in v3:
time: 182 us
  Pallas kernels  58 us (32%)
  starting transfers between devices  52.4 us (29%)
  waiting for transfers between devices  48.6 us (27%)
  between operations  14.1 us (8%)
  local copies, waits for them, and re-layouts  6.82 us (4%)
  other arithmetic  2.01 us (1%)
    ppermute x1, starting transfers between devices, shards(): far_a = lax.ppermute(up[:half], 'y', ring(4, 1))  18.6 us
    ppermute x1, waiting for transfers between devices, shards(): up = lax.ppermute(own, 'y', ring(4, 1))  17.4 us
    ppermute x3, waiting for transfers between devices, shards(): sums = [sums] + [lax.ppermute(sums, 'x', ring(4, i)) for i in (1, 2, 3)]  15.3 us
    pallas_call x1, Pallas kernels, shards(): call(product_kernel, [shape(by_core), shape(by_core), shape((BLOCKS, pane...  14.2 us
    ppermute x1, waiting for transfers between devices, shards(): far_a = lax.ppermute(up[:half], 'y', ring(4, 1))  9.12 us
    pallas_call x1, Pallas kernels, shards(): call(backward_kernel, [shape((BLOCKS, panel, rows)), stream], [VMEM] * 5,...  6.97 us
    pallas_call x1, Pallas kernels, shards(): call(filter_kernel, shape((SMALL, TAPS), F32), [VMEM, VMEM], VMEM)(gm, pq)  6.19 us
    all_to_all x1, starting transfers between devices, shards(): grads = lax.all_to_all(grads, SEQ, split_axis=0, concat_axis=0, tiled=True)  6.06 us
  transfers between devices with their start and end apart: 21, of which 8 were waited for; matrix products, arithmetic and copies ran while one was open for 2% of the time, Pallas kernels for 22%

profile of v3, /device:TPU:8, one launch (start us, length us, event | category | flops | bytes accessed | tf_op | source)
XLA Modules:
  0.0 181.9 jit_solution(5726500252642275502)
XLA Ops:
  11.1 1.9 %collective-permute-start.2 = (bf16[128,4096]{1,0:T(8,128)(2,1)}, bf16[128,4096]{1,0:T(8,128)(2,1)}, u32[]{:S(2)}, u32[]{:S(2)}) collective-permute-start(bf16[128,4096]{1,0:T(8,128)(2,1)} %bitcast.40), channel_id=1, source_target_pairs={{0,4},{4,0},{1,5},{5,1},{2,6},{6,2},{3,7},{7,3},{8,12},{12,8},{9,1... | collective-permute-start | bytes 3145736 | tf_op jit(solution)/shard_map/ppermute | solution.py:323
  13.0 3.9 %shard_map.119 = bf16[8,2,512,128]{3,2,1,0:T(8,128)(2,1)} custom-call(bf16[128,4096]{1,0:T(8,128)(2,1)} %bitcast.37, bf16[128,4096]{1,0:T(8,128)(2,1)} %bitcast.33, bf16[128,4096]{1,0:T(8,128)(2,1)} %bitcast.35), custom_call_target="tpu_custom_call" | custom-call | flops 1 | bytes 1 | tf_op jit(solution)/shard_map/pallas_call | solution.py:327
  17.0 5.2 %all-to-all-start = ((bf16[8,2,512,128]{3,2,1,0:T(8,128)(2,1)}), bf16[8,2,512,128]{3,2,1,0:T(8,128)(2,1)S(1)}, u32[]{:S(2)}, u32[]{:S(2)}) async-start(bf16[8,2,512,128]{3,2,1,0:T(8,128)(2,1)} %shard_map.119), calls=%async_computation | async-start | bytes 4194304 | tf_op jit(solution)/shard_map/all_to_all | solution.py:342
  22.1 5.9 %shard_map.118 = (bf16[32,128,256]{2,1,0:T(8,128)(2,1)}, f32[512,128]{1,0:T(8,128)}) custom-call(s32[1]{0:T(128)} %bitcast.12.panel_ref, bf16[256,128]{1,0:T(8,128)(2,1)} %filters_ref.1, f32[8,4,128]{2,1,0:T(4,128)} %bitcast.42), custom_call_target="tpu_custom_call" | custom-call | flops 1 | bytes 1 | tf_op jit(solution)/shard_map/pallas_call | solution.py:328
  28.0 17.4 %collective-permute-done.refs_1_ = bf16[128,4096]{1,0:T(8,128)(2,1)S(1)} collective-permute-done((bf16[128,4096]{1,0:T(8,128)(2,1)}, bf16[128,4096]{1,0:T(8,128)(2,1)S(1)}, u32[]{:S(2)}, u32[]{:S(2)}) %collective-permute-start) | collective-permute-done | bytes 1048608 | tf_op jit(solution)/shard_map/ppermute | solution.py:324
  45.4 18.6 %collective-permute-start.3 = (bf16[64,4096]{1,0:T(8,128)(2,1)S(1)}, bf16[64,4096]{1,0:T(8,128)(2,1)}, u32[]{:S(2)}, u32[]{:S(2)}) collective-permute-start(bf16[64,4096]{1,0:T(8,128)(2,1)S(1)} %slice.6), channel_id=1, source_target_pairs={{0,1},{1,2},{2,3},{3,0},{4,5},{5,6},{6,7},{7,4},{8,9},{9,10},{10,1... | collective-permute-start | bytes 1572872 | tf_op jit(solution)/shard_map/ppermute | solution.py:335
  65.2 2.0 %collective-permute-start.5 = (bf16[128,4096]{1,0:T(8,128)(2,1)}, bf16[128,4096]{1,0:T(8,128)(2,1)}, u32[]{:S(2)}, u32[]{:S(2)}) collective-permute-start(bf16[128,4096]{1,0:T(8,128)(2,1)} %collective-permute-done.2.refs_5_), channel_id=1, source_target_pairs={{0,1},{1,2},{2,3},{3,0},{4,5},{5,6},{6,7},{7,4},{8,9},{9,10},{10,1... | collective-permute-start | bytes 3145736 | tf_op jit(solution)/shard_map/ppermute | solution.py:337
  67.3 9.1 %collective-permute-done.3.refs_3_ = bf16[64,4096]{1,0:T(8,128)(2,1)} collective-permute-done((bf16[64,4096]{1,0:T(8,128)(2,1)S(1)}, bf16[64,4096]{1,0:T(8,128)(2,1)}, u32[]{:S(2)}, u32[]{:S(2)}) %collective-permute-start.3) | collective-permute-done | bytes 524320 | tf_op jit(solution)/shard_map/ppermute | solution.py:335
  76.4 2.5 %collective-permute-start.7 = (bf16[64,4096]{1,0:T(8,128)(2,1)}, bf16[64,4096]{1,0:T(8,128)(2,1)}, u32[]{:S(2)}, u32[]{:S(2)}) collective-permute-start(bf16[64,4096]{1,0:T(8,128)(2,1)} %collective-permute-done.3.refs_3_), channel_id=1, source_target_pairs={{0,4},{4,0},{1,5},{5,1},{2,6},{6,2},{3,7},{7,3},{8,12},{12,8},{9,1... | collective-permute-start | bytes 1572872 | tf_op jit(solution)/shard_map/ppermute | solution.py:339
  80.1 2.5 %collective-permute-start.8 = (bf16[64,4096]{1,0:T(8,128)(2,1)}, bf16[64,4096]{1,0:T(8,128)(2,1)}, u32[]{:S(2)}, u32[]{:S(2)}) collective-permute-start(bf16[64,4096]{1,0:T(8,128)(2,1)} %collective-permute-done.4.refs_4_), channel_id=1, source_target_pairs={{0,4},{4,0},{1,5},{5,1},{2,6},{6,2},{3,7},{7,3},{8,12},{12,8},{9,1... | collective-permute-start | bytes 1572872 | tf_op jit(solution)/shard_map/ppermute | solution.py:340
  85.3 5.7 %shard_map.120 = (f32[8,512,128]{2,1,0:T(8,128)}, bf16[512,1024]{1,0:T(8,128)(2,1)}) custom-call(s32[8]{0:T(128)} %stack.87.slot_ref, bf16[8,2,512,128]{3,2,1,0:T(8,128)(2,1)} %copy-done, bf16[32,128,256]{2,1,0:T(8,128)(2,1)} %get-tuple-element.37.table_ref, f32[512,128]{1,0:T(8,128)} %get-tuple-element.38.gain_ref), custom_call_target="tpu_custom_call" | custom-call | flops 1 | bytes 1 | tf_op jit(solution)/shard_map/pallas_call | solution.py:344
  91.1 3.9 %collective-permute-done.8.refs_9_ = bf16[64,4096]{1,0:T(8,128)(2,1)} collective-permute-done((bf16[64,4096]{1,0:T(8,128)(2,1)}, bf16[64,4096]{1,0:T(8,128)(2,1)}, u32[]{:S(2)}, u32[]{:S(2)}) %collective-permute-start.8) | collective-permute-done | bytes 524320 | tf_op jit(solution)/shard_map/ppermute | solution.py:340
  95.0 14.2 %shard_map.122 = (bf16[8,512,256]{2,1,0:T(8,128)(2,1)}, bf16[8,512,256]{2,1,0:T(8,128)(2,1)}, f32[8,512,128]{2,1,0:T(8,128)}) custom-call(s32[1]{0:T(128)} %bitcast.2.core_ref, s32[8]{0:T(128)} %stack.82.place_ref, bf16[128,4096]{1,0:T(8,128)(2,1)} %bitcast.41, bf16[128,4096]{1,0:T(8,128)(2,1)} %copy-done.2, ...), custom_call_target="tpu_custom_call" | custom-call | flops 1 | bytes 300000000 | tf_op jit(solution)/shard_map/pallas_call | solution.py:352
  109.3 7.0 %shard_map.123 = (bf16[8,512,128]{2,1,0:T(8,128)(2,1)}, bf16[8,2,512,128]{3,2,1,0:T(8,128)(2,1)}) custom-call(f32[8,512,128]{2,1,0:T(8,128)} %get-tuple-element.40.grad_ref, f32[8,512,128]{2,1,0:T(8,128)} %get-tuple-element.41.mixed_ref, bf16[8,2,512,128]{3,2,1,0:T(8,128)(2,1)} %copy-done, bf16[32,128,256]{2,1,0:T(8,128)(2,1)} %get-tuple-element.37.table_ref, ...), custom_call_target="tpu_custom_call" | custom-call | flops 1 | bytes 1 | tf_op jit(solution)/shard_map/pallas_call | solution.py:369
  116.3 6.1 %all-to-all-start.1 = ((bf16[8,2,512,128]{3,2,1,0:T(8,128)(2,1)}), bf16[8,2,512,128]{3,2,1,0:T(8,128)(2,1)S(1)}, u32[]{:S(2)}, u32[]{:S(2)}) async-start(bf16[8,2,512,128]{3,2,1,0:T(8,128)(2,1)} %get-tuple-element.42), calls=%async_computation.1 | async-start | bytes 4194304 | tf_op jit(solution)/shard_map/all_to_all | solution.py:376
  123.0 4.0 %shard_map.125 = (bf16[2,512,256]{2,1,0:T(8,128)(2,1)}, bf16[2,512,256]{2,1,0:T(8,128)(2,1)}, bf16[2,512,256]{2,1,0:T(8,128)(2,1)}, bf16[2,512,256]{2,1,0:T(8,128)(2,1)}) custom-call(s32[4]{0:T(128)} %pad_add_fusion.1.order_ref, bf16[8,512,256]{2,1,0:T(8,128)(2,1)} %get-tuple-element.48.mine_ref, bf16[8,512,256]{2,1,0:T(8,128)(2,1)} %collective-permute-done.9.other_ref), custom_call_target="tpu_custom_call" | custom-call | flops 1 | bytes 1 | tf_op jit(solution)/shard_map/pallas_call | solution.py:378
  128.4 2.7 %collective-permute-start.11 = (bf16[2,512,256]{2,1,0:T(8,128)(2,1)}, bf16[2,512,256]{2,1,0:T(8,128)(2,1)S(1)}, u32[]{:S(2)}, u32[]{:S(2)}) collective-permute-start(bf16[2,512,256]{2,1,0:T(8,128)(2,1)} %get-tuple-element.52), channel_id=1, source_target_pairs={{0,64},{32,96},{64,0},{96,32},{1,65},{33,97},{65,1},{97,33},{2,66}... | collective-permute-start | bytes 1572872 | tf_op jit(solution)/shard_map/ppermute | solution.py:382
  132.6 6.2 %shard_map.126 = f32[48,128]{1,0:T(8,128)} custom-call(bf16[8,512,128]{2,1,0:T(8,128)(2,1)} %get-tuple-element.54.gm_ref, bf16[8,2,512,128]{3,2,1,0:T(8,128)(2,1)} %copy-done), custom_call_target="tpu_custom_call" | custom-call | flops 1 | bytes 1 | tf_op jit(solution)/shard_map/pallas_call | solution.py:383
  142.4 12.7 %collective-permute-done.14.refs_5_ = f32[48,128]{1,0:T(8,128)S(1)} collective-permute-done((f32[48,128]{1,0:T(8,128)S(1)}, f32[48,128]{1,0:T(8,128)S(1)}, u32[]{:S(2)}, u32[]{:S(2)}) %collective-permute-start.14) | collective-permute-done | bytes 24608 | tf_op jit(solution)/shard_map/ppermute | solution.py:385
  156.4 2.6 %collective-permute-done.16.refs_7_ = f32[48,128]{1,0:T(8,128)S(1)} collective-permute-done((f32[48,128]{1,0:T(8,128)S(1)}, f32[48,128]{1,0:T(8,128)S(1)}, u32[]{:S(2)}, u32[]{:S(2)}) %collective-permute-start.16) | collective-permute-done | bytes 24608 | tf_op jit(solution)/shard_map/ppermute | solution.py:385
  159.9 2.7 %shard_map.127 = (bf16[560,256]{1,0:T(8,128)(2,1)}, bf16[560,256]{1,0:T(8,128)(2,1)}) custom-call(s32[4]{0:T(128)} %pad_add_fusion.source_ref, s32[1]{0:T(128)} %bitcast.27.zh_ref, bf16[2,512,256]{2,1,0:T(8,128)(2,1)} %get-tuple-element.50.refs_0_, bf16[2,512,256]{2,1,0:T(8,128)(2,1)} %copy-done.3, bf16[2,512,256]{2,1,0:T(8,128)(2,1)} %copy-done.4, ...), custom_call_target="tpu_custom_call" | custom-call | flops 1 | bytes 1 | tf_op jit(solution)/shard_map/pallas_call | solution.py:386
  162.7 3.6 %collective-permute-start.17 = (bf16[560,256]{1,0:T(8,128)(2,1)}, bf16[560,256]{1,0:T(8,128)(2,1)S(1)}, u32[]{:S(2)}, u32[]{:S(2)}) collective-permute-start(bf16[560,256]{1,0:T(8,128)(2,1)} %get-tuple-element.56), channel_id=1, source_target_pairs={{0,16},{16,0},{1,17},{17,1},{2,18},{18,2},{3,19},{19,3},{4,20},{20... | collective-permute-start | bytes 860168 | tf_op jit(solution)/shard_map/ppermute | solution.py:393
  167.6 4.6 %shard_map.124 = (bf16[128,4096]{1,0:T(8,128)(2,1)}, bf16[128,4096]{1,0:T(8,128)(2,1)}, bf16[128,4096]{1,0:T(8,128)(2,1)}) custom-call(bf16[128,4096]{1,0:T(8,128)(2,1)} %bitcast.34, bf16[128,4096]{1,0:T(8,128)(2,1)} %bitcast.36, bf16[8,2,512,128]{3,2,1,0:T(8,128)(2,1)} %copy-done.1), custom_call_target="tpu_custom_call" | custom-call | flops 1 | bytes 1 | tf_op jit(solution)/shard_map/pallas_call | solution.py:394
  173.0 2.0 %shard_map.128 = (f32[256,512]{1,0:T(8,128)}, f32[32,128]{1,0:T(8,128)}, f32[4,128]{1,0:T(4,128)}) custom-call(bf16[560,256]{1,0:T(8,128)(2,1)} %get-tuple-element.55.mine_ref, bf16[560,256]{1,0:T(8,128)(2,1)} %copy-done.5), custom_call_target="tpu_custom_call" | custom-call | flops 1 | bytes 1 | tf_op jit(solution)/shard_map/pallas_call | solution.py:397
  (57 shorter events, 20.8 us)
Async XLA Ops:
  7.2 87.8 %all-gather.3.cloned.1.call-start = ((), (), s32[]{:S(2)}) async-start(), calls=%async_computation.2 | async-start | bytes 4456448 | tf_op jit(solution)/shard_map/all_gather | solution.py:320
  9.0 36.3 %collective-permute-start = (bf16[128,4096]{1,0:T(8,128)(2,1)}, bf16[128,4096]{1,0:T(8,128)(2,1)S(1)}, u32[]{:S(2)}, u32[]{:S(2)}) collective-permute-start(bf16[128,4096]{1,0:T(8,128)(2,1)} %bitcast.38), channel_id=1, source_target_pairs={{0,1},{1,2},{2,3},{3,0},{4,5},{5,6},{6,7},{7,4},{8,9},{9,10},{10,1... | collective-permute-start | bytes 3145736 | tf_op jit(solution)/shard_map/ppermute | solution.py:324
  10.7 34.7 %collective-permute-start.1 = (bf16[128,4096]{1,0:T(8,128)(2,1)}, bf16[128,4096]{1,0:T(8,128)(2,1)}, u32[]{:S(2)}, u32[]{:S(2)}) collective-permute-start(bf16[128,4096]{1,0:T(8,128)(2,1)} %bitcast.39), channel_id=1, source_target_pairs={{0,3},{1,0},{2,1},{3,2},{4,7},{5,4},{6,5},{7,6},{8,11},{9,8},{10,9... | collective-permute-start | bytes 3145736 | tf_op jit(solution)/shard_map/ppermute | solution.py:325
  11.1 34.2 %collective-permute-start.2 = (bf16[128,4096]{1,0:T(8,128)(2,1)}, bf16[128,4096]{1,0:T(8,128)(2,1)}, u32[]{:S(2)}, u32[]{:S(2)}) collective-permute-start(bf16[128,4096]{1,0:T(8,128)(2,1)} %bitcast.40), channel_id=1, source_target_pairs={{0,4},{4,0},{1,5},{5,1},{2,6},{6,2},{3,7},{7,3},{8,12},{12,8},{9,1... | collective-permute-start | bytes 3145736 | tf_op jit(solution)/shard_map/ppermute | solution.py:323
  17.0 67.0 %all-to-all-start = ((bf16[8,2,512,128]{3,2,1,0:T(8,128)(2,1)}), bf16[8,2,512,128]{3,2,1,0:T(8,128)(2,1)S(1)}, u32[]{:S(2)}, u32[]{:S(2)}) async-start(bf16[8,2,512,128]{3,2,1,0:T(8,128)(2,1)} %shard_map.119), calls=%async_computation | async-start | bytes 4194304 | tf_op jit(solution)/shard_map/all_to_all | solution.py:342
  45.4 45.7 %copy-start.2 = (bf16[128,4096]{1,0:T(8,128)(2,1)}, bf16[128,4096]{1,0:T(8,128)(2,1)S(1)}, u32[]{:S(2)}) copy-start(bf16[128,4096]{1,0:T(8,128)(2,1)S(1)} %collective-permute-done.refs_1_) | copy-start | bytes 3145732
  45.4 31.0 %collective-permute-start.3 = (bf16[64,4096]{1,0:T(8,128)(2,1)S(1)}, bf16[64,4096]{1,0:T(8,128)(2,1)}, u32[]{:S(2)}, u32[]{:S(2)}) collective-permute-start(bf16[64,4096]{1,0:T(8,128)(2,1)S(1)} %slice.6), channel_id=1, source_target_pairs={{0,1},{1,2},{2,3},{3,0},{4,5},{5,6},{6,7},{7,4},{8,9},{9,10},{10,1... | collective-permute-start | bytes 1572872 | tf_op jit(solution)/shard_map/ppermute | solution.py:335
  65.1 15.0 %collective-permute-start.4 = (bf16[64,4096]{1,0:T(8,128)(2,1)S(1)}, bf16[64,4096]{1,0:T(8,128)(2,1)}, u32[]{:S(2)}, u32[]{:S(2)}) collective-permute-start(bf16[64,4096]{1,0:T(8,128)(2,1)S(1)} %slice.7), channel_id=1, source_target_pairs={{0,3},{1,0},{2,1},{3,2},{4,7},{5,4},{6,5},{7,6},{8,11},{9,8},{10,9... | collective-permute-start | bytes 1572872 | tf_op jit(solution)/shard_map/ppermute | solution.py:336
  65.2 29.8 %collective-permute-start.5 = (bf16[128,4096]{1,0:T(8,128)(2,1)}, bf16[128,4096]{1,0:T(8,128)(2,1)}, u32[]{:S(2)}, u32[]{:S(2)}) collective-permute-start(bf16[128,4096]{1,0:T(8,128)(2,1)} %collective-permute-done.2.refs_5_), channel_id=1, source_target_pairs={{0,1},{1,2},{2,3},{3,0},{4,5},{5,6},{6,7},{7,4},{8,9},{9,10},{10,1... | collective-permute-start | bytes 3145736 | tf_op jit(solution)/shard_map/ppermute | solution.py:337
  67.2 27.8 %collective-permute-start.6 = (bf16[128,4096]{1,0:T(8,128)(2,1)}, bf16[128,4096]{1,0:T(8,128)(2,1)}, u32[]{:S(2)}, u32[]{:S(2)}) collective-permute-start(bf16[128,4096]{1,0:T(8,128)(2,1)} %collective-permute-done.2.refs_5_), channel_id=1, source_target_pairs={{0,3},{1,0},{2,1},{3,2},{4,7},{5,4},{6,5},{7,6},{8,11},{9,8},{10,9... | collective-permute-start | bytes 3145736 | tf_op jit(solution)/shard_map/ppermute | solution.py:338
  76.4 14.7 %collective-permute-start.7 = (bf16[64,4096]{1,0:T(8,128)(2,1)}, bf16[64,4096]{1,0:T(8,128)(2,1)}, u32[]{:S(2)}, u32[]{:S(2)}) collective-permute-start(bf16[64,4096]{1,0:T(8,128)(2,1)} %collective-permute-done.3.refs_3_), channel_id=1, source_target_pairs={{0,4},{4,0},{1,5},{5,1},{2,6},{6,2},{3,7},{7,3},{8,12},{12,8},{9,1... | collective-permute-start | bytes 1572872 | tf_op jit(solution)/shard_map/ppermute | solution.py:339
  80.1 14.8 %collective-permute-start.8 = (bf16[64,4096]{1,0:T(8,128)(2,1)}, bf16[64,4096]{1,0:T(8,128)(2,1)}, u32[]{:S(2)}, u32[]{:S(2)}) collective-permute-start(bf16[64,4096]{1,0:T(8,128)(2,1)} %collective-permute-done.4.refs_4_), channel_id=1, source_target_pairs={{0,4},{4,0},{1,5},{5,1},{2,6},{6,2},{3,7},{7,3},{8,12},{12,8},{9,1... | collective-permute-start | bytes 1572872 | tf_op jit(solution)/shard_map/ppermute | solution.py:340
  109.2 13.8 %collective-permute-start.9 = (bf16[8,512,256]{2,1,0:T(8,128)(2,1)}, bf16[8,512,256]{2,1,0:T(8,128)(2,1)}, u32[]{:S(2)}, u32[]{:S(2)}) collective-permute-start(bf16[8,512,256]{2,1,0:T(8,128)(2,1)} %get-tuple-element.49), channel_id=1, source_target_pairs={{0,8},{8,0},{1,9},{9,1},{2,10},{10,2},{3,11},{11,3},{4,12},{12,4},... | collective-permute-start | bytes 6291464 | tf_op jit(solution)/shard_map/ppermute | solution.py:367
  116.3 50.0 %all-to-all-start.1 = ((bf16[8,2,512,128]{3,2,1,0:T(8,128)(2,1)}), bf16[8,2,512,128]{3,2,1,0:T(8,128)(2,1)S(1)}, u32[]{:S(2)}, u32[]{:S(2)}) async-start(bf16[8,2,512,128]{3,2,1,0:T(8,128)(2,1)} %get-tuple-element.42), calls=%async_computation.1 | async-start | bytes 4194304 | tf_op jit(solution)/shard_map/all_to_all | solution.py:376
  126.9 32.0 %collective-permute-start.10 = (bf16[2,512,256]{2,1,0:T(8,128)(2,1)}, bf16[2,512,256]{2,1,0:T(8,128)(2,1)S(1)}, u32[]{:S(2)}, u32[]{:S(2)}) collective-permute-start(bf16[2,512,256]{2,1,0:T(8,128)(2,1)} %get-tuple-element.51), channel_id=1, source_target_pairs={{0,32},{32,64},{64,96},{96,0},{1,33},{33,65},{65,97},{97,1},{2,34}... | collective-permute-start | bytes 1572872 | tf_op jit(solution)/shard_map/ppermute | solution.py:382
  128.4 30.5 %collective-permute-start.11 = (bf16[2,512,256]{2,1,0:T(8,128)(2,1)}, bf16[2,512,256]{2,1,0:T(8,128)(2,1)S(1)}, u32[]{:S(2)}, u32[]{:S(2)}) collective-permute-start(bf16[2,512,256]{2,1,0:T(8,128)(2,1)} %get-tuple-element.52), channel_id=1, source_target_pairs={{0,64},{32,96},{64,0},{96,32},{1,65},{33,97},{65,1},{97,33},{2,66}... | collective-permute-start | bytes 1572872 | tf_op jit(solution)/shard_map/ppermute | solution.py:382
  131.2 27.8 %collective-permute-start.12 = (bf16[2,512,256]{2,1,0:T(8,128)(2,1)}, bf16[2,512,256]{2,1,0:T(8,128)(2,1)}, u32[]{:S(2)}, u32[]{:S(2)}) collective-permute-start(bf16[2,512,256]{2,1,0:T(8,128)(2,1)} %get-tuple-element.53), channel_id=1, source_target_pairs={{0,96},{32,0},{64,32},{96,64},{1,97},{33,1},{65,33},{97,65},{2,98}... | collective-permute-start | bytes 1572872 | tf_op jit(solution)/shard_map/ppermute | solution.py:382
  138.8 1.4 collective-permute-start.13
  140.9 18.1 %copy-start.6 = (f32[48,128]{1,0:T(8,128)}, f32[48,128]{1,0:T(8,128)S(1)}, u32[]{:S(2)}) copy-start(f32[48,128]{1,0:T(8,128)S(1)} %add.151.refs_4_) | copy-start | bytes 73732
  140.9 14.2 %collective-permute-start.14 = (f32[48,128]{1,0:T(8,128)S(1)}, f32[48,128]{1,0:T(8,128)S(1)}, u32[]{:S(2)}, u32[]{:S(2)}) collective-permute-start(f32[48,128]{1,0:T(8,128)S(1)} %add.151.refs_4_), channel_id=1, source_target_pairs={{0,32},{32,64},{64,96},{96,0},{1,33},{33,65},{65,97},{97,1},{2,34}... | collective-permute-start | bytes 73736 | tf_op jit(solution)/shard_map/ppermute | solution.py:385
  141.5 14.8 %collective-permute-start.15 = (f32[48,128]{1,0:T(8,128)S(1)}, f32[48,128]{1,0:T(8,128)S(1)}, u32[]{:S(2)}, u32[]{:S(2)}) collective-permute-start(f32[48,128]{1,0:T(8,128)S(1)} %add.151.refs_4_), channel_id=1, source_target_pairs={{0,64},{32,96},{64,0},{96,32},{1,65},{33,97},{65,1},{97,33},{2,66}... | collective-permute-start | bytes 73736 | tf_op jit(solution)/shard_map/ppermute | solution.py:385
  155.1 3.9 %copy-start.7 = (f32[48,128]{1,0:T(8,128)}, f32[48,128]{1,0:T(8,128)S(1)}, u32[]{:S(2)}) copy-start(f32[48,128]{1,0:T(8,128)S(1)} %collective-permute-done.14.refs_5_) | copy-start | bytes 73732
  155.1 3.8 %collective-permute-start.16 = (f32[48,128]{1,0:T(8,128)S(1)}, f32[48,128]{1,0:T(8,128)S(1)}, u32[]{:S(2)}, u32[]{:S(2)}) collective-permute-start(f32[48,128]{1,0:T(8,128)S(1)} %add.151.refs_4_), channel_id=1, source_target_pairs={{0,96},{32,0},{64,32},{96,64},{1,97},{33,1},{65,33},{97,65},{2,98}... | collective-permute-start | bytes 73736 | tf_op jit(solution)/shard_map/ppermute | solution.py:385
  162.7 9.7 %collective-permute-start.17 = (bf16[560,256]{1,0:T(8,128)(2,1)}, bf16[560,256]{1,0:T(8,128)(2,1)S(1)}, u32[]{:S(2)}, u32[]{:S(2)}) collective-permute-start(bf16[560,256]{1,0:T(8,128)(2,1)} %get-tuple-element.56), channel_id=1, source_target_pairs={{0,16},{16,0},{1,17},{17,1},{2,18},{18,2},{3,19},{19,3},{4,20},{20... | collective-permute-start | bytes 860168 | tf_op jit(solution)/shard_map/ppermute | solution.py:393
  (7 other events, 8.5 us)
Sparse Core Ops, SparseCore 0:
  11.0 75.9 all-gather.2

commit v4 on v3

--- a/solution.py
+++ b/solution.py
@@ -98,30 +98,6 @@
     lax.fori_loop(0, table_ref.shape[0], one_group, 0, unroll=4)
 
 
-def backward_kernel(grad_ref, mixed_ref, pq_ref, table_ref, gain_ref, gm_ref, out_ref):
-    def one_group(g, carry):
-        rows = pl.ds(pl.multiple_of(g * GROUP, GROUP), GROUP)
-        table = table_ref[g]
-        gain = gain_ref[rows, :]
-        zero = jnp.zeros((GROUP, TAPS), BF)
-        x = []
-        for b in range(BLOCKS):
-            grad = grad_ref[b, rows, :]
-            out_ref[b, 0, rows, :] = (grad * mixed_ref[b, rows, :]).astype(BF)
-            x.append((grad * pq_ref[b, 1, rows, :].astype(F32)).astype(BF))
-            gm_ref[b, rows, :] = x[b]
-        lhs = jnp.concatenate(
-            [jnp.concatenate(x, 0), jnp.concatenate(x[1:] + [zero], 0)], 1
-        )
-        conv = lax.dot_general(lhs, table, (((1,), (1,)), ((), ())), preferred_element_type=F32)
-        for b in range(BLOCKS):
-            total = conv[GROUP * b : GROUP * (b + 1)] + gain * x[b].astype(F32)
-            out_ref[b, 1, rows, :] = total.astype(BF)
-        return carry
-
-    lax.fori_loop(0, table_ref.shape[0], one_group, 0, unroll=4)
-
-
 def cot_copies(refs, held, sem_of, cols=slice(None)):
     copies = []
     half = TAPS // 2
@@ -144,7 +120,12 @@
 
 def product_kernel(core_ref, place_ref, *refs):
     cot = refs[:10]
-    gated_ref, w_ref, mine_ref, other_ref, grad_ref, held, w_held, total, sems, w_sems, out_sems = refs[10:]
+    gated_ref, w_ref, streams = refs[10], refs[11], refs[12:16]
+    mine_ref, other_ref, gm_ref, out_ref = refs[16:20]
+    held, w_held, total, grad_ref = refs[20:24]
+    stream_held = refs[24:28]
+    sems, w_sems, out_sems, stream_sems = refs[28:]
+    mixed_ref, pq_ref, table_ref, gain_ref = stream_held
     blocks, channels, width = mine_ref.shape
     stripes = sems.shape[0]
     span = held.shape[1] // stripes
@@ -157,7 +138,11 @@
         weights.append(
             pltpu.make_async_copy(w_ref.at[d], w_held.at[:, width * d : width * (d + 1)], w_sems.at[d])
         )
-    for c in weights:
+    ins = [
+        pltpu.make_async_copy(ref, dst, stream_sems.at[i])
+        for i, (ref, dst) in enumerate(zip(streams, stream_held))
+    ]
+    for c in weights + ins:
         c.start()
 
     def out_copies(n):
@@ -192,6 +177,30 @@
         return carry
 
     lax.fori_loop(0, 2, tokens, 0)
+    for c in ins:
+        c.wait()
+
+    def one_group(g, carry):
+        rows = pl.ds(pl.multiple_of(g * GROUP, GROUP), GROUP)
+        table = table_ref[g]
+        gain = gain_ref[rows, :]
+        zero = jnp.zeros((GROUP, TAPS), BF)
+        x = []
+        for b in range(BLOCKS):
+            grad = grad_ref[b, rows, :]
+            out_ref[b, 0, rows, :] = (grad * mixed_ref[b, rows, :]).astype(BF)
+            x.append((grad * pq_ref[b, 1, rows, :].astype(F32)).astype(BF))
+            gm_ref[b, rows, :] = x[b]
+        lhs = jnp.concatenate(
+            [jnp.concatenate(x, 0), jnp.concatenate(x[1:] + [zero], 0)], 1
+        )
+        conv = lax.dot_general(lhs, table, (((1,), (1,)), ((), ())), preferred_element_type=F32)
+        for b in range(BLOCKS):
+            result = conv[GROUP * b : GROUP * (b + 1)] + gain * x[b].astype(F32)
+            out_ref[b, 1, rows, :] = result.astype(BF)
+        return carry
+
+    lax.fori_loop(0, table_ref.shape[0], one_group, 0, unroll=4)
     for n in range(stripes):
         for c in out_copies(n):
             c.wait()
@@ -248,7 +257,7 @@
     for i, out in enumerate(outs):
         for d in range(2):
             to = order_ref[i] * 2 + d
-            out[d] = (mine_ref[to].astype(F32) + other_ref[to].astype(F32)).astype(BF)
+            out[d] = mine_ref[to] + other_ref[to]
 
 
 def line_kernel(source_ref, zh_ref, *refs):
@@ -349,40 +358,41 @@
     )(slot_of, pq, table, gain)
 
     by_core = (8, panel, outs_here)
-    mine, other, grad = call(
+    mine, other, gm, grads = call(
         product_kernel,
-        [shape(by_core), shape(by_core), shape((BLOCKS, panel, rows), F32)],
-        [SMEM] * 2 + [ANY] * 10 + [VMEM, ANY],
-        [ANY, ANY, VMEM],
+        [shape(by_core), shape(by_core), shape((BLOCKS, panel, rows)), stream],
+        [SMEM] * 2 + [ANY] * 10 + [VMEM] + [ANY] * 5,
+        [ANY, ANY, VMEM, VMEM],
         scratch=[
             pltpu.VMEM((length, width), BF),
             pltpu.VMEM((panel, width), BF),
             pltpu.VMEM((2, *by_core), BF),
+            pltpu.VMEM((BLOCKS, panel, rows), F32),
+            pltpu.VMEM((BLOCKS, panel, rows), F32),
+            pltpu.VMEM(stream.shape, BF),
+            pltpu.VMEM(table.shape, BF),
+            pltpu.VMEM(gain.shape, F32),
             pltpu.SemaphoreType.DMA((4,)),
             pltpu.SemaphoreType.DMA((16,)),
             pltpu.SemaphoreType.DMA((2, 4)),
+            pltpu.SemaphoreType.DMA((4,)),
         ],
         micros=100,
-    )(core.astype(jnp.int32).reshape(1), place, *cots, gated, w_all)
+    )(core.astype(jnp.int32).reshape(1), place, *cots, gated, w_all, mixed, pq, table, gain)
     other = lax.ppermute(other, "core", ring(2, 1))
-
-    gm, grads = call(
-        backward_kernel,
-        [shape((BLOCKS, panel, rows)), stream],
-        [VMEM] * 5,
-        [VMEM] * 2,
-    )(grad, mixed, pq, table, gain)
-    mine = after(mine, gm)
     grads = lax.all_to_all(grads, SEQ, split_axis=0, concat_axis=0, tiled=True)
 
     lines = call(
         pair_kernel, [shape((2, panel, outs_here))] * 4, [SMEM] + [VMEM] * 2, [VMEM] * 4
     )(order, mine, other)
     gm = after(gm, lines[0])
+    sums = call(filter_kernel, shape((SMALL, TAPS), F32), [VMEM, VMEM], VMEM)(gm, pq)
     lines = [lines[0]] + [lax.ppermute(lines[i], "x", ring(4, i)) for i in (1, 2, 3)]
-    sums = call(filter_kernel, shape((SMALL, TAPS), F32), [VMEM, VMEM], VMEM)(gm, pq)
     sums = sums + lax.ppermute(sums, "core", ring(2, 1))
     sums = [sums] + [lax.ppermute(sums, "x", ring(4, i)) for i in (1, 2, 3)]
+    grad_query, grad_key, grad_value = call(
+        finish_kernel, [shape((rows, width))] * 3, [VMEM] * 3, [VMEM] * 3
+    )(k, v, grads)
     keep, send = call(
         line_kernel,
         [shape((panel + SMALL, outs_here))] * 2,
@@ -391,9 +401,6 @@
         scratch=[pltpu.VMEM((4, SMALL, TAPS), F32)],
     )(source, zh.astype(jnp.int32).reshape(1), *lines, *sums)
     send = lax.ppermute(send, "zh", ring(2, 1))
-    grad_query, grad_key, grad_value = call(
-        finish_kernel, [shape((rows, width))] * 3, [VMEM] * 3, [VMEM] * 3
-    )(k, v, grads)
     grad_weight, grad_filters, grad_gain = call(
         functools.partial(total_kernel, scale),
         [shape((outs_here, panel), F32), shape((groups, TAPS), F32), shape((panel // TAPS, TAPS), F32)],

time: 182 us -> 179 us (0.984)
  Pallas kernels: 58 us -> 54.8 us
    pallas_call x1 -> x0, Pallas kernels: 6.97 us -> none  [shards(): call(backward_kernel, [shape((BLOCKS, panel, rows)), stream], [VMEM] * 5,...]
    pallas_call x1, Pallas kernels: 14.2 us -> 18.2 us  [shards(): call(product_kernel, [shape(by_core), shape(by_core), shape((BLOCKS, pane...]
  transfers between devices with their start and end apart: 21 -> 21, of which waited for: 8 -> 8; matrix products, arithmetic and copies ran while one was open for 2% -> 2% of each run, Pallas kernels for 22% -> 18%
where the time goes in v4:
time: 179 us
  Pallas kernels  54.8 us (31%)
  starting transfers between devices  52.4 us (29%)
  waiting for transfers between devices  48.7 us (27%)
  between operations  14.1 us (8%)
  local copies, waits for them, and re-layouts  6.71 us (4%)
  other arithmetic  2 us (1%)
    ppermute x1, starting transfers between devices, shards(): far_a = lax.ppermute(up[:half], 'y', ring(4, 1))  18.6 us
    pallas_call x1, Pallas kernels, shards(): call(product_kernel, [shape(by_core), shape(by_core), shape((BLOCKS, pane...  18.2 us
    ppermute x1, waiting for transfers between devices, shards(): up = lax.ppermute(own, 'y', ring(4, 1))  17.4 us
    ppermute x3, waiting for transfers between devices, shards(): sums = [sums] + [lax.ppermute(sums, 'x', ring(4, i)) for i in (1, 2, 3)]  15.3 us
    ppermute x1, waiting for transfers between devices, shards(): far_a = lax.ppermute(up[:half], 'y', ring(4, 1))  9.12 us
    pallas_call x1, Pallas kernels, shards(): call(filter_kernel, shape((SMALL, TAPS), F32), [VMEM, VMEM], VMEM)(gm, pq)  6.19 us
    all_to_all x1, starting transfers between devices, shards(): grads = lax.all_to_all(grads, SEQ, split_axis=0, concat_axis=0, tiled=True)  6.07 us
    pallas_call x1, Pallas kernels, shards(): call(table_kernel, [shape((groups, TAPS, 2 * TAPS)), shape((panel, TAPS),...  5.87 us
  transfers between devices with their start and end apart: 21, of which 8 were waited for; matrix products, arithmetic and copies ran while one was open for 2% of the time, Pallas kernels for 18%

profile of v4, /device:TPU:8, one launch (start us, length us, event | category | flops | bytes accessed | tf_op | source)
XLA Modules:
  0.0 178.8 jit_solution(17056111139570888001)
XLA Ops:
  7.2 1.8 %shard_map.121 = bf16[512,256]{1,0:T(8,128)(2,1)} custom-call(bf16[256,512]{1,0:T(8,128)(2,1)} %w_ref.1), custom_call_target="tpu_custom_call" | custom-call | flops 1 | bytes 1 | tf_op jit(solution)/shard_map/pallas_call | solution.py:328
  11.1 1.9 %collective-permute-start.2 = (bf16[128,4096]{1,0:T(8,128)(2,1)}, bf16[128,4096]{1,0:T(8,128)(2,1)}, u32[]{:S(2)}, u32[]{:S(2)}) collective-permute-start(bf16[128,4096]{1,0:T(8,128)(2,1)} %bitcast.40), channel_id=1, source_target_pairs={{0,4},{4,0},{1,5},{5,1},{2,6},{6,2},{3,7},{7,3},{8,12},{12,8},{9,1... | collective-permute-start | bytes 3145736 | tf_op jit(solution)/shard_map/ppermute | solution.py:332
  13.0 3.9 %shard_map.119 = bf16[8,2,512,128]{3,2,1,0:T(8,128)(2,1)} custom-call(bf16[128,4096]{1,0:T(8,128)(2,1)} %bitcast.37, bf16[128,4096]{1,0:T(8,128)(2,1)} %bitcast.33, bf16[128,4096]{1,0:T(8,128)(2,1)} %bitcast.35), custom_call_target="tpu_custom_call" | custom-call | flops 1 | bytes 1 | tf_op jit(solution)/shard_map/pallas_call | solution.py:336
  16.9 5.2 %all-to-all-start = ((bf16[8,2,512,128]{3,2,1,0:T(8,128)(2,1)}), bf16[8,2,512,128]{3,2,1,0:T(8,128)(2,1)S(1)}, u32[]{:S(2)}, u32[]{:S(2)}) async-start(bf16[8,2,512,128]{3,2,1,0:T(8,128)(2,1)} %shard_map.119), calls=%async_computation | async-start | bytes 4194304 | tf_op jit(solution)/shard_map/all_to_all | solution.py:351
  22.1 5.9 %shard_map.118 = (bf16[32,128,256]{2,1,0:T(8,128)(2,1)}, f32[512,128]{1,0:T(8,128)}) custom-call(s32[1]{0:T(128)} %bitcast.12.panel_ref, bf16[256,128]{1,0:T(8,128)(2,1)} %filters_ref.1, f32[8,4,128]{2,1,0:T(4,128)} %bitcast.42), custom_call_target="tpu_custom_call" | custom-call | flops 1 | bytes 1 | tf_op jit(solution)/shard_map/pallas_call | solution.py:337
  28.0 17.4 %collective-permute-done.refs_1_ = bf16[128,4096]{1,0:T(8,128)(2,1)S(1)} collective-permute-done((bf16[128,4096]{1,0:T(8,128)(2,1)}, bf16[128,4096]{1,0:T(8,128)(2,1)S(1)}, u32[]{:S(2)}, u32[]{:S(2)}) %collective-permute-start) | collective-permute-done | bytes 1048608 | tf_op jit(solution)/shard_map/ppermute | solution.py:333
  45.4 18.6 %collective-permute-start.3 = (bf16[64,4096]{1,0:T(8,128)(2,1)S(1)}, bf16[64,4096]{1,0:T(8,128)(2,1)}, u32[]{:S(2)}, u32[]{:S(2)}) collective-permute-start(bf16[64,4096]{1,0:T(8,128)(2,1)S(1)} %slice.6), channel_id=1, source_target_pairs={{0,1},{1,2},{2,3},{3,0},{4,5},{5,6},{6,7},{7,4},{8,9},{9,10},{10,1... | collective-permute-start | bytes 1572872 | tf_op jit(solution)/shard_map/ppermute | solution.py:344
  65.2 2.0 %collective-permute-start.5 = (bf16[128,4096]{1,0:T(8,128)(2,1)}, bf16[128,4096]{1,0:T(8,128)(2,1)}, u32[]{:S(2)}, u32[]{:S(2)}) collective-permute-start(bf16[128,4096]{1,0:T(8,128)(2,1)} %collective-permute-done.2.refs_5_), channel_id=1, source_target_pairs={{0,1},{1,2},{2,3},{3,0},{4,5},{5,6},{6,7},{7,4},{8,9},{9,10},{10,1... | collective-permute-start | bytes 3145736 | tf_op jit(solution)/shard_map/ppermute | solution.py:346
  67.3 9.1 %collective-permute-done.3.refs_3_ = bf16[64,4096]{1,0:T(8,128)(2,1)} collective-permute-done((bf16[64,4096]{1,0:T(8,128)(2,1)S(1)}, bf16[64,4096]{1,0:T(8,128)(2,1)}, u32[]{:S(2)}, u32[]{:S(2)}) %collective-permute-start.3) | collective-permute-done | bytes 524320 | tf_op jit(solution)/shard_map/ppermute | solution.py:344
  76.4 2.5 %collective-permute-start.7 = (bf16[64,4096]{1,0:T(8,128)(2,1)}, bf16[64,4096]{1,0:T(8,128)(2,1)}, u32[]{:S(2)}, u32[]{:S(2)}) collective-permute-start(bf16[64,4096]{1,0:T(8,128)(2,1)} %collective-permute-done.3.refs_3_), channel_id=1, source_target_pairs={{0,4},{4,0},{1,5},{5,1},{2,6},{6,2},{3,7},{7,3},{8,12},{12,8},{9,1... | collective-permute-start | bytes 1572872 | tf_op jit(solution)/shard_map/ppermute | solution.py:348
  80.1 2.5 %collective-permute-start.8 = (bf16[64,4096]{1,0:T(8,128)(2,1)}, bf16[64,4096]{1,0:T(8,128)(2,1)}, u32[]{:S(2)}, u32[]{:S(2)}) collective-permute-start(bf16[64,4096]{1,0:T(8,128)(2,1)} %collective-permute-done.4.refs_4_), channel_id=1, source_target_pairs={{0,4},{4,0},{1,5},{5,1},{2,6},{6,2},{3,7},{7,3},{8,12},{12,8},{9,1... | collective-permute-start | bytes 1572872 | tf_op jit(solution)/shard_map/ppermute | solution.py:349
  85.2 5.7 %shard_map.120 = (f32[8,512,128]{2,1,0:T(8,128)}, bf16[512,1024]{1,0:T(8,128)(2,1)}) custom-call(s32[8]{0:T(128)} %stack.87.slot_ref, bf16[8,2,512,128]{3,2,1,0:T(8,128)(2,1)} %copy-done, bf16[32,128,256]{2,1,0:T(8,128)(2,1)} %get-tuple-element.35.table_ref.refs_14_, f32[512,128]{1,0:T(8,128)} %get-tuple-element.36.gain_ref.refs_15_), custom_call_target="tpu_custom_call" | custom-call | flops 1 | bytes 1 | tf_op jit(solution)/shard_map/pallas_call | solution.py:353
  91.0 4.0 %collective-permute-done.8.refs_9_ = bf16[64,4096]{1,0:T(8,128)(2,1)} collective-permute-done((bf16[64,4096]{1,0:T(8,128)(2,1)}, bf16[64,4096]{1,0:T(8,128)(2,1)}, u32[]{:S(2)}, u32[]{:S(2)}) %collective-permute-start.8) | collective-permute-done | bytes 524320 | tf_op jit(solution)/shard_map/ppermute | solution.py:349
  95.0 18.2 %shard_map.122 = (bf16[8,512,256]{2,1,0:T(8,128)(2,1)}, bf16[8,512,256]{2,1,0:T(8,128)(2,1)}, bf16[8,512,128]{2,1,0:T(8,128)(2,1)}, bf16[8,2,512,128]{3,2,1,0:T(8,128)(2,1)}) custom-call(s32[1]{0:T(128)} %bitcast.2.core_ref, s32[8]{0:T(128)} %stack.82.place_ref, bf16[128,4096]{1,0:T(8,128)(2,1)} %bitcast.41, bf16[128,4096]{1,0:T(8,128)(2,1)} %copy-done.2, ...), custom_call_target="tpu_custom_call" | custom-call | flops 1 | bytes 300000000 | tf_op jit(solution)/shard_map/pallas_call | solution.py:361
  113.3 6.1 %all-to-all-start.1 = ((bf16[8,2,512,128]{3,2,1,0:T(8,128)(2,1)}), bf16[8,2,512,128]{3,2,1,0:T(8,128)(2,1)S(1)}, u32[]{:S(2)}, u32[]{:S(2)}) async-start(bf16[8,2,512,128]{3,2,1,0:T(8,128)(2,1)} %get-tuple-element.39), calls=%async_computation.1 | async-start | bytes 4194304 | tf_op jit(solution)/shard_map/all_to_all | solution.py:383
  120.0 3.7 %shard_map.124 = (bf16[2,512,256]{2,1,0:T(8,128)(2,1)}, bf16[2,512,256]{2,1,0:T(8,128)(2,1)}, bf16[2,512,256]{2,1,0:T(8,128)(2,1)}, bf16[2,512,256]{2,1,0:T(8,128)(2,1)}) custom-call(s32[4]{0:T(128)} %pad_add_fusion.1.order_ref, bf16[8,512,256]{2,1,0:T(8,128)(2,1)} %get-tuple-element.43.mine_ref, bf16[8,512,256]{2,1,0:T(8,128)(2,1)} %collective-permute-done.9.other_ref), custom_call_target="tpu_custom_call" | custom-call | flops 1 | bytes 1 | tf_op jit(solution)/shard_map/pallas_call | solution.py:385
  125.3 2.7 %collective-permute-start.11 = (bf16[2,512,256]{2,1,0:T(8,128)(2,1)}, bf16[2,512,256]{2,1,0:T(8,128)(2,1)S(1)}, u32[]{:S(2)}, u32[]{:S(2)}) collective-permute-start(bf16[2,512,256]{2,1,0:T(8,128)(2,1)} %get-tuple-element.47), channel_id=1, source_target_pairs={{0,64},{32,96},{64,0},{96,32},{1,65},{33,97},{65,1},{97,33},{2,66}... | collective-permute-start | bytes 1572872 | tf_op jit(solution)/shard_map/ppermute | solution.py:390
  129.4 6.2 %shard_map.125 = f32[48,128]{1,0:T(8,128)} custom-call(bf16[8,512,128]{2,1,0:T(8,128)(2,1)} %get-tuple-element.50.gm_ref, bf16[8,2,512,128]{3,2,1,0:T(8,128)(2,1)} %copy-done), custom_call_target="tpu_custom_call" | custom-call | flops 1 | bytes 1 | tf_op jit(solution)/shard_map/pallas_call | solution.py:389
  139.3 12.7 %collective-permute-done.14.refs_5_ = f32[48,128]{1,0:T(8,128)S(1)} collective-permute-done((f32[48,128]{1,0:T(8,128)S(1)}, f32[48,128]{1,0:T(8,128)S(1)}, u32[]{:S(2)}, u32[]{:S(2)}) %collective-permute-start.14) | collective-permute-done | bytes 24608 | tf_op jit(solution)/shard_map/ppermute | solution.py:392
  153.2 2.6 %collective-permute-done.16.refs_7_ = f32[48,128]{1,0:T(8,128)S(1)} collective-permute-done((f32[48,128]{1,0:T(8,128)S(1)}, f32[48,128]{1,0:T(8,128)S(1)}, u32[]{:S(2)}, u32[]{:S(2)}) %collective-permute-start.16) | collective-permute-done | bytes 24608 | tf_op jit(solution)/shard_map/ppermute | solution.py:392
  156.8 2.7 %shard_map.126 = (bf16[560,256]{1,0:T(8,128)(2,1)}, bf16[560,256]{1,0:T(8,128)(2,1)}) custom-call(s32[4]{0:T(128)} %pad_add_fusion.source_ref, s32[1]{0:T(128)} %bitcast.27.zh_ref, bf16[2,512,256]{2,1,0:T(8,128)(2,1)} %get-tuple-element.45.refs_0_, bf16[2,512,256]{2,1,0:T(8,128)(2,1)} %copy-done.3, bf16[2,512,256]{2,1,0:T(8,128)(2,1)} %copy-done.4, ...), custom_call_target="tpu_custom_call" | custom-call | flops 1 | bytes 1 | tf_op jit(solution)/shard_map/pallas_call | solution.py:396
  159.5 3.6 %collective-permute-start.17 = (bf16[560,256]{1,0:T(8,128)(2,1)}, bf16[560,256]{1,0:T(8,128)(2,1)S(1)}, u32[]{:S(2)}, u32[]{:S(2)}) collective-permute-start(bf16[560,256]{1,0:T(8,128)(2,1)} %get-tuple-element.52), channel_id=1, source_target_pairs={{0,16},{16,0},{1,17},{17,1},{2,18},{18,2},{3,19},{19,3},{4,20},{20... | collective-permute-start | bytes 860168 | tf_op jit(solution)/shard_map/ppermute | solution.py:403
  164.4 4.6 %shard_map.123 = (bf16[128,4096]{1,0:T(8,128)(2,1)}, bf16[128,4096]{1,0:T(8,128)(2,1)}, bf16[128,4096]{1,0:T(8,128)(2,1)}) custom-call(bf16[128,4096]{1,0:T(8,128)(2,1)} %bitcast.34, bf16[128,4096]{1,0:T(8,128)(2,1)} %bitcast.36, bf16[8,2,512,128]{3,2,1,0:T(8,128)(2,1)} %copy-done.1), custom_call_target="tpu_custom_call" | custom-call | flops 1 | bytes 1 | tf_op jit(solution)/shard_map/pallas_call | solution.py:393
  169.9 2.0 %shard_map.127 = (f32[256,512]{1,0:T(8,128)}, f32[32,128]{1,0:T(8,128)}, f32[4,128]{1,0:T(4,128)}) custom-call(bf16[560,256]{1,0:T(8,128)(2,1)} %get-tuple-element.51.mine_ref, bf16[560,256]{1,0:T(8,128)(2,1)} %copy-done.5), custom_call_target="tpu_custom_call" | custom-call | flops 1 | bytes 1 | tf_op jit(solution)/shard_map/pallas_call | solution.py:404
  (56 shorter events, 18.9 us)
Async XLA Ops:
  7.2 87.8 %all-gather.3.cloned.1.call-start = ((), (), s32[]{:S(2)}) async-start(), calls=%async_computation.2 | async-start | bytes 4456448 | tf_op jit(solution)/shard_map/all_gather | solution.py:329
  9.0 36.3 %collective-permute-start = (bf16[128,4096]{1,0:T(8,128)(2,1)}, bf16[128,4096]{1,0:T(8,128)(2,1)S(1)}, u32[]{:S(2)}, u32[]{:S(2)}) collective-permute-start(bf16[128,4096]{1,0:T(8,128)(2,1)} %bitcast.38), channel_id=1, source_target_pairs={{0,1},{1,2},{2,3},{3,0},{4,5},{5,6},{6,7},{7,4},{8,9},{9,10},{10,1... | collective-permute-start | bytes 3145736 | tf_op jit(solution)/shard_map/ppermute | solution.py:333
  10.7 34.7 %collective-permute-start.1 = (bf16[128,4096]{1,0:T(8,128)(2,1)}, bf16[128,4096]{1,0:T(8,128)(2,1)}, u32[]{:S(2)}, u32[]{:S(2)}) collective-permute-start(bf16[128,4096]{1,0:T(8,128)(2,1)} %bitcast.39), channel_id=1, source_target_pairs={{0,3},{1,0},{2,1},{3,2},{4,7},{5,4},{6,5},{7,6},{8,11},{9,8},{10,9... | collective-permute-start | bytes 3145736 | tf_op jit(solution)/shard_map/ppermute | solution.py:334
  11.1 34.2 %collective-permute-start.2 = (bf16[128,4096]{1,0:T(8,128)(2,1)}, bf16[128,4096]{1,0:T(8,128)(2,1)}, u32[]{:S(2)}, u32[]{:S(2)}) collective-permute-start(bf16[128,4096]{1,0:T(8,128)(2,1)} %bitcast.40), channel_id=1, source_target_pairs={{0,4},{4,0},{1,5},{5,1},{2,6},{6,2},{3,7},{7,3},{8,12},{12,8},{9,1... | collective-permute-start | bytes 3145736 | tf_op jit(solution)/shard_map/ppermute | solution.py:332
  16.9 66.9 %all-to-all-start = ((bf16[8,2,512,128]{3,2,1,0:T(8,128)(2,1)}), bf16[8,2,512,128]{3,2,1,0:T(8,128)(2,1)S(1)}, u32[]{:S(2)}, u32[]{:S(2)}) async-start(bf16[8,2,512,128]{3,2,1,0:T(8,128)(2,1)} %shard_map.119), calls=%async_computation | async-start | bytes 4194304 | tf_op jit(solution)/shard_map/all_to_all | solution.py:351
  45.4 45.6 %copy-start.2 = (bf16[128,4096]{1,0:T(8,128)(2,1)}, bf16[128,4096]{1,0:T(8,128)(2,1)S(1)}, u32[]{:S(2)}) copy-start(bf16[128,4096]{1,0:T(8,128)(2,1)S(1)} %collective-permute-done.refs_1_) | copy-start | bytes 3145732
  45.4 31.0 %collective-permute-start.3 = (bf16[64,4096]{1,0:T(8,128)(2,1)S(1)}, bf16[64,4096]{1,0:T(8,128)(2,1)}, u32[]{:S(2)}, u32[]{:S(2)}) collective-permute-start(bf16[64,4096]{1,0:T(8,128)(2,1)S(1)} %slice.6), channel_id=1, source_target_pairs={{0,1},{1,2},{2,3},{3,0},{4,5},{5,6},{6,7},{7,4},{8,9},{9,10},{10,1... | collective-permute-start | bytes 1572872 | tf_op jit(solution)/shard_map/ppermute | solution.py:344
  65.1 15.0 %collective-permute-start.4 = (bf16[64,4096]{1,0:T(8,128)(2,1)S(1)}, bf16[64,4096]{1,0:T(8,128)(2,1)}, u32[]{:S(2)}, u32[]{:S(2)}) collective-permute-start(bf16[64,4096]{1,0:T(8,128)(2,1)S(1)} %slice.7), channel_id=1, source_target_pairs={{0,3},{1,0},{2,1},{3,2},{4,7},{5,4},{6,5},{7,6},{8,11},{9,8},{10,9... | collective-permute-start | bytes 1572872 | tf_op jit(solution)/shard_map/ppermute | solution.py:345
  65.2 29.8 %collective-permute-start.5 = (bf16[128,4096]{1,0:T(8,128)(2,1)}, bf16[128,4096]{1,0:T(8,128)(2,1)}, u32[]{:S(2)}, u32[]{:S(2)}) collective-permute-start(bf16[128,4096]{1,0:T(8,128)(2,1)} %collective-permute-done.2.refs_5_), channel_id=1, source_target_pairs={{0,1},{1,2},{2,3},{3,0},{4,5},{5,6},{6,7},{7,4},{8,9},{9,10},{10,1... | collective-permute-start | bytes 3145736 | tf_op jit(solution)/shard_map/ppermute | solution.py:346
  67.2 27.8 %collective-permute-start.6 = (bf16[128,4096]{1,0:T(8,128)(2,1)}, bf16[128,4096]{1,0:T(8,128)(2,1)}, u32[]{:S(2)}, u32[]{:S(2)}) collective-permute-start(bf16[128,4096]{1,0:T(8,128)(2,1)} %collective-permute-done.2.refs_5_), channel_id=1, source_target_pairs={{0,3},{1,0},{2,1},{3,2},{4,7},{5,4},{6,5},{7,6},{8,11},{9,8},{10,9... | collective-permute-start | bytes 3145736 | tf_op jit(solution)/shard_map/ppermute | solution.py:347
  76.4 14.6 %collective-permute-start.7 = (bf16[64,4096]{1,0:T(8,128)(2,1)}, bf16[64,4096]{1,0:T(8,128)(2,1)}, u32[]{:S(2)}, u32[]{:S(2)}) collective-permute-start(bf16[64,4096]{1,0:T(8,128)(2,1)} %collective-permute-done.3.refs_3_), channel_id=1, source_target_pairs={{0,4},{4,0},{1,5},{5,1},{2,6},{6,2},{3,7},{7,3},{8,12},{12,8},{9,1... | collective-permute-start | bytes 1572872 | tf_op jit(solution)/shard_map/ppermute | solution.py:348
  80.1 14.8 %collective-permute-start.8 = (bf16[64,4096]{1,0:T(8,128)(2,1)}, bf16[64,4096]{1,0:T(8,128)(2,1)}, u32[]{:S(2)}, u32[]{:S(2)}) collective-permute-start(bf16[64,4096]{1,0:T(8,128)(2,1)} %collective-permute-done.4.refs_4_), channel_id=1, source_target_pairs={{0,4},{4,0},{1,5},{5,1},{2,6},{6,2},{3,7},{7,3},{8,12},{12,8},{9,1... | collective-permute-start | bytes 1572872 | tf_op jit(solution)/shard_map/ppermute | solution.py:349
  113.2 6.8 %collective-permute-start.9 = (bf16[8,512,256]{2,1,0:T(8,128)(2,1)}, bf16[8,512,256]{2,1,0:T(8,128)(2,1)}, u32[]{:S(2)}, u32[]{:S(2)}) collective-permute-start(bf16[8,512,256]{2,1,0:T(8,128)(2,1)} %get-tuple-element.44), channel_id=1, source_target_pairs={{0,8},{8,0},{1,9},{9,1},{2,10},{10,2},{3,11},{11,3},{4,12},{12,4},... | collective-permute-start | bytes 6291464 | tf_op jit(solution)/shard_map/ppermute | solution.py:382
  113.3 49.8 %all-to-all-start.1 = ((bf16[8,2,512,128]{3,2,1,0:T(8,128)(2,1)}), bf16[8,2,512,128]{3,2,1,0:T(8,128)(2,1)S(1)}, u32[]{:S(2)}, u32[]{:S(2)}) async-start(bf16[8,2,512,128]{3,2,1,0:T(8,128)(2,1)} %get-tuple-element.39), calls=%async_computation.1 | async-start | bytes 4194304 | tf_op jit(solution)/shard_map/all_to_all | solution.py:383
  123.8 32.0 %collective-permute-start.10 = (bf16[2,512,256]{2,1,0:T(8,128)(2,1)}, bf16[2,512,256]{2,1,0:T(8,128)(2,1)S(1)}, u32[]{:S(2)}, u32[]{:S(2)}) collective-permute-start(bf16[2,512,256]{2,1,0:T(8,128)(2,1)} %get-tuple-element.46), channel_id=1, source_target_pairs={{0,32},{32,64},{64,96},{96,0},{1,33},{33,65},{65,97},{97,1},{2,34}... | collective-permute-start | bytes 1572872 | tf_op jit(solution)/shard_map/ppermute | solution.py:390
  125.3 30.5 %collective-permute-start.11 = (bf16[2,512,256]{2,1,0:T(8,128)(2,1)}, bf16[2,512,256]{2,1,0:T(8,128)(2,1)S(1)}, u32[]{:S(2)}, u32[]{:S(2)}) collective-permute-start(bf16[2,512,256]{2,1,0:T(8,128)(2,1)} %get-tuple-element.47), channel_id=1, source_target_pairs={{0,64},{32,96},{64,0},{96,32},{1,65},{33,97},{65,1},{97,33},{2,66}... | collective-permute-start | bytes 1572872 | tf_op jit(solution)/shard_map/ppermute | solution.py:390
  128.0 27.8 %collective-permute-start.12 = (bf16[2,512,256]{2,1,0:T(8,128)(2,1)}, bf16[2,512,256]{2,1,0:T(8,128)(2,1)}, u32[]{:S(2)}, u32[]{:S(2)}) collective-permute-start(bf16[2,512,256]{2,1,0:T(8,128)(2,1)} %get-tuple-element.48), channel_id=1, source_target_pairs={{0,96},{32,0},{64,32},{96,64},{1,97},{33,1},{65,33},{97,65},{2,98}... | collective-permute-start | bytes 1572872 | tf_op jit(solution)/shard_map/ppermute | solution.py:390
  135.6 1.4 collective-permute-start.13
  137.8 18.0 %copy-start.6 = (f32[48,128]{1,0:T(8,128)}, f32[48,128]{1,0:T(8,128)S(1)}, u32[]{:S(2)}) copy-start(f32[48,128]{1,0:T(8,128)S(1)} %add.151.refs_4_) | copy-start | bytes 73732
  137.8 14.2 %collective-permute-start.14 = (f32[48,128]{1,0:T(8,128)S(1)}, f32[48,128]{1,0:T(8,128)S(1)}, u32[]{:S(2)}, u32[]{:S(2)}) collective-permute-start(f32[48,128]{1,0:T(8,128)S(1)} %add.151.refs_4_), channel_id=1, source_target_pairs={{0,32},{32,64},{64,96},{96,0},{1,33},{33,65},{65,97},{97,1},{2,34}... | collective-permute-start | bytes 73736 | tf_op jit(solution)/shard_map/ppermute | solution.py:392
  138.4 14.8 %collective-permute-start.15 = (f32[48,128]{1,0:T(8,128)S(1)}, f32[48,128]{1,0:T(8,128)S(1)}, u32[]{:S(2)}, u32[]{:S(2)}) collective-permute-start(f32[48,128]{1,0:T(8,128)S(1)} %add.151.refs_4_), channel_id=1, source_target_pairs={{0,64},{32,96},{64,0},{96,32},{1,65},{33,97},{65,1},{97,33},{2,66}... | collective-permute-start | bytes 73736 | tf_op jit(solution)/shard_map/ppermute | solution.py:392
  152.0 3.9 %copy-start.7 = (f32[48,128]{1,0:T(8,128)}, f32[48,128]{1,0:T(8,128)S(1)}, u32[]{:S(2)}) copy-start(f32[48,128]{1,0:T(8,128)S(1)} %collective-permute-done.14.refs_5_) | copy-start | bytes 73732
  152.0 3.8 %collective-permute-start.16 = (f32[48,128]{1,0:T(8,128)S(1)}, f32[48,128]{1,0:T(8,128)S(1)}, u32[]{:S(2)}, u32[]{:S(2)}) collective-permute-start(f32[48,128]{1,0:T(8,128)S(1)} %add.151.refs_4_), channel_id=1, source_target_pairs={{0,96},{32,0},{64,32},{96,64},{1,97},{33,1},{65,33},{97,65},{2,98}... | collective-permute-start | bytes 73736 | tf_op jit(solution)/shard_map/ppermute | solution.py:392
  159.5 9.7 %collective-permute-start.17 = (bf16[560,256]{1,0:T(8,128)(2,1)}, bf16[560,256]{1,0:T(8,128)(2,1)S(1)}, u32[]{:S(2)}, u32[]{:S(2)}) collective-permute-start(bf16[560,256]{1,0:T(8,128)(2,1)} %get-tuple-element.52), channel_id=1, source_target_pairs={{0,16},{16,0},{1,17},{17,1},{2,18},{18,2},{3,19},{19,3},{4,20},{20... | collective-permute-start | bytes 860168 | tf_op jit(solution)/shard_map/ppermute | solution.py:403
  (7 other events, 8.5 us)
Sparse Core Ops, SparseCore 0:
  11.0 75.9 all-gather.2

commit v5 on v4

--- a/solution.py
+++ b/solution.py
@@ -130,9 +130,12 @@
     stripes = sems.shape[0]
     span = held.shape[1] // stripes
     each = blocks // stripes
-    for n in range(stripes):
-        for c in cot_copies(cot, held, lambda slot, n=n: sems.at[n], slice(span * n, span * (n + 1))):
+    def stripe_start(n):
+        for c in cot_copies(cot, held, lambda slot: sems.at[n], slice(span * n, span * (n + 1))):
             c.start()
+
+    stripe_start(0)
+    stripe_start(1)
     weights = []
     for d in range(2 * blocks):
         weights.append(
@@ -142,8 +145,6 @@
         pltpu.make_async_copy(ref, dst, stream_sems.at[i])
         for i, (ref, dst) in enumerate(zip(streams, stream_held))
     ]
-    for c in weights + ins:
-        c.start()
 
     def out_copies(n):
         part = pl.ds(n * each, each)
@@ -152,17 +153,18 @@
             for i, ref in enumerate((mine_ref, other_ref))
         ]
 
-    def stripe(n, carry):
-        cols = pl.ds(pl.multiple_of(n * span, span), span)
+    for n in range(stripes):
+        cols = slice(span * n, span * (n + 1))
         pltpu.make_async_copy(held.at[:, cols], held.at[:, cols], sems.at[n]).wait()
+        if n + 2 < stripes:
+            stripe_start(n + 2)
+        for c in {stripes - 3: weights[:blocks], stripes - 2: weights[blocks:], stripes - 1: ins}.get(n, []):
+            c.start()
         grad = jnp.dot(gated_ref[...], held[:, cols], preferred_element_type=F32)
         for i in range(2 * each):
             total[i % 2, n * each + i // 2] = grad[:, width * i : width * (i + 1)].astype(BF)
         for c in out_copies(n):
             c.start()
-        return carry
-
-    lax.fori_loop(0, stripes, stripe, 0)
     for c in weights:
         c.wait()
     span = 4 * TAPS
@@ -253,11 +255,27 @@
     return small[:, :TAPS] + small[:, TAPS:]
 
 
-def pair_kernel(order_ref, mine_ref, other_ref, *outs):
-    for i, out in enumerate(outs):
-        for d in range(2):
-            to = order_ref[i] * 2 + d
-            out[d] = mine_ref[to] + other_ref[to]
+def pair_kernel(order_ref, mine_ref, other_ref, *refs):
+    outs = refs[:4]
+    mine, other, lines, sems, out_sems = refs[4:]
+    ins = []
+    for i in range(4):
+        part = pl.ds(order_ref[i] * 2, 2)
+        ins.append([
+            pltpu.make_async_copy(ref.at[part], held.at[i], sems.at[i, j])
+            for j, (ref, held) in enumerate(((mine_ref, mine), (other_ref, other)))
+        ])
+        for c in ins[-1]:
+            c.start()
+    backs = []
+    for i in range(4):
+        for c in ins[i]:
+            c.wait()
+        lines[i] = mine[i] + other[i]
+        backs.append(pltpu.make_async_copy(lines.at[i], outs[i], out_sems.at[i]))
+        backs[-1].start()
+    for c in backs:
+        c.wait()
 
 
 def line_kernel(source_ref, zh_ref, *refs):
@@ -382,13 +400,20 @@
     other = lax.ppermute(other, "core", ring(2, 1))
     grads = lax.all_to_all(grads, SEQ, split_axis=0, concat_axis=0, tiled=True)
 
+    part = (2, panel, outs_here)
     lines = call(
-        pair_kernel, [shape((2, panel, outs_here))] * 4, [SMEM] + [VMEM] * 2, [VMEM] * 4
+        pair_kernel,
+        [shape(part)] * 4,
+        [SMEM] + [ANY] * 2,
+        [ANY] * 4,
+        scratch=[pltpu.VMEM((4, *part), BF)] * 3
+        + [pltpu.SemaphoreType.DMA((4, 2)), pltpu.SemaphoreType.DMA((4,))],
     )(order, mine, other)
     gm = after(gm, lines[0])
     sums = call(filter_kernel, shape((SMALL, TAPS), F32), [VMEM, VMEM], VMEM)(gm, pq)
     lines = [lines[0]] + [lax.ppermute(lines[i], "x", ring(4, i)) for i in (1, 2, 3)]
     sums = sums + lax.ppermute(sums, "core", ring(2, 1))
+    sums = after(sums, lines[1])
     sums = [sums] + [lax.ppermute(sums, "x", ring(4, i)) for i in (1, 2, 3)]
     grad_query, grad_key, grad_value = call(
         finish_kernel, [shape((rows, width))] * 3, [VMEM] * 3, [VMEM] * 3

time: 179 us -> 175 us (0.978)
  waiting for transfers between devices: 48.7 us -> 42.6 us
  starting transfers between devices: 52.4 us -> 56.1 us
    ppermute x3, waiting for transfers between devices: 15.3 us -> 0.47 us  [shards(): sums = [sums] + [lax.ppermute(sums, 'x', ring(4, i)) for i in (1, 2, 3)]]
    ppermute x3, waiting for transfers between devices: 0.01 us -> 7.98 us  [shards(): lax.ppermute(lines[i], 'x', ring(4, i))]
    ppermute x3, starting transfers between devices: 2.07 us -> 5.45 us  [shards(): sums = [sums] + [lax.ppermute(sums, 'x', ring(4, i)) for i in (1, 2, 3)]]
  transfers between devices with their start and end apart: 21 -> 21, of which waited for: 8 -> 10; matrix products, arithmetic and copies ran while one was open for 2% -> 2% of each run, Pallas kernels for 18% -> 19%
where the time goes in v5:
time: 175 us
  starting transfers between devices  56.1 us (32%)
  Pallas kernels  53.4 us (31%)
  waiting for transfers between devices  42.6 us (24%)
  between operations  14.1 us (8%)
  local copies, waits for them, and re-layouts  6.39 us (4%)
  other arithmetic  1.94 us (1%)
    ppermute x1, starting transfers between devices, shards(): far_a = lax.ppermute(up[:half], 'y', ring(4, 1))  18.6 us
    ppermute x1, waiting for transfers between devices, shards(): up = lax.ppermute(own, 'y', ring(4, 1))  17.4 us
    pallas_call x1, Pallas kernels, shards(): call(product_kernel, [shape(by_core), shape(by_core), shape((BLOCKS, pane...  16.8 us
    ppermute x1, waiting for transfers between devices, shards(): far_a = lax.ppermute(up[:half], 'y', ring(4, 1))  9.12 us
    ppermute x3, waiting for transfers between devices, shards(): lax.ppermute(lines[i], 'x', ring(4, i))  7.98 us
    pallas_call x1, Pallas kernels, shards(): call(filter_kernel, shape((SMALL, TAPS), F32), [VMEM, VMEM], VMEM)(gm, pq)  6.19 us
    all_to_all x1, starting transfers between devices, shards(): grads = lax.all_to_all(grads, SEQ, split_axis=0, concat_axis=0, tiled=True)  6.08 us
    ppermute x3, starting transfers between devices, shards(): lax.ppermute(lines[i], 'x', ring(4, i))  5.91 us
  transfers between devices with their start and end apart: 21, of which 10 were waited for; matrix products, arithmetic and copies ran while one was open for 2% of the time, Pallas kernels for 19%

profile of v5, /device:TPU:8, one launch (start us, length us, event | category | flops | bytes accessed | tf_op | source)
XLA Modules:
  0.0 174.6 jit_solution(8543776566054136692)
XLA Ops:
  7.2 1.8 %shard_map.121 = bf16[512,256]{1,0:T(8,128)(2,1)} custom-call(bf16[256,512]{1,0:T(8,128)(2,1)} %w_ref.1), custom_call_target="tpu_custom_call" | custom-call | flops 1 | bytes 1 | tf_op jit(solution)/shard_map/pallas_call | solution.py:346
  11.1 1.9 %collective-permute-start.2 = (bf16[128,4096]{1,0:T(8,128)(2,1)}, bf16[128,4096]{1,0:T(8,128)(2,1)}, u32[]{:S(2)}, u32[]{:S(2)}) collective-permute-start(bf16[128,4096]{1,0:T(8,128)(2,1)} %bitcast.40), channel_id=1, source_target_pairs={{0,4},{4,0},{1,5},{5,1},{2,6},{6,2},{3,7},{7,3},{8,12},{12,8},{9,1... | collective-permute-start | bytes 3145736 | tf_op jit(solution)/shard_map/ppermute | solution.py:350
  13.0 3.9 %shard_map.119 = bf16[8,2,512,128]{3,2,1,0:T(8,128)(2,1)} custom-call(bf16[128,4096]{1,0:T(8,128)(2,1)} %bitcast.37, bf16[128,4096]{1,0:T(8,128)(2,1)} %bitcast.33, bf16[128,4096]{1,0:T(8,128)(2,1)} %bitcast.35), custom_call_target="tpu_custom_call" | custom-call | flops 1 | bytes 1 | tf_op jit(solution)/shard_map/pallas_call | solution.py:354
  16.9 5.2 %all-to-all-start = ((bf16[8,2,512,128]{3,2,1,0:T(8,128)(2,1)}), bf16[8,2,512,128]{3,2,1,0:T(8,128)(2,1)S(1)}, u32[]{:S(2)}, u32[]{:S(2)}) async-start(bf16[8,2,512,128]{3,2,1,0:T(8,128)(2,1)} %shard_map.119), calls=%async_computation | async-start | bytes 4194304 | tf_op jit(solution)/shard_map/all_to_all | solution.py:369
  22.1 5.9 %shard_map.118 = (bf16[32,128,256]{2,1,0:T(8,128)(2,1)}, f32[512,128]{1,0:T(8,128)}) custom-call(s32[1]{0:T(128)} %bitcast.12.panel_ref, bf16[256,128]{1,0:T(8,128)(2,1)} %filters_ref.1, f32[8,4,128]{2,1,0:T(4,128)} %bitcast.42), custom_call_target="tpu_custom_call" | custom-call | flops 1 | bytes 1 | tf_op jit(solution)/shard_map/pallas_call | solution.py:355
  28.0 17.4 %collective-permute-done.refs_1_ = bf16[128,4096]{1,0:T(8,128)(2,1)S(1)} collective-permute-done((bf16[128,4096]{1,0:T(8,128)(2,1)}, bf16[128,4096]{1,0:T(8,128)(2,1)S(1)}, u32[]{:S(2)}, u32[]{:S(2)}) %collective-permute-start) | collective-permute-done | bytes 1048608 | tf_op jit(solution)/shard_map/ppermute | solution.py:351
  45.4 18.6 %collective-permute-start.3 = (bf16[64,4096]{1,0:T(8,128)(2,1)S(1)}, bf16[64,4096]{1,0:T(8,128)(2,1)}, u32[]{:S(2)}, u32[]{:S(2)}) collective-permute-start(bf16[64,4096]{1,0:T(8,128)(2,1)S(1)} %slice.6), channel_id=1, source_target_pairs={{0,1},{1,2},{2,3},{3,0},{4,5},{5,6},{6,7},{7,4},{8,9},{9,10},{10,1... | collective-permute-start | bytes 1572872 | tf_op jit(solution)/shard_map/ppermute | solution.py:362
  65.2 2.0 %collective-permute-start.5 = (bf16[128,4096]{1,0:T(8,128)(2,1)}, bf16[128,4096]{1,0:T(8,128)(2,1)}, u32[]{:S(2)}, u32[]{:S(2)}) collective-permute-start(bf16[128,4096]{1,0:T(8,128)(2,1)} %collective-permute-done.2.refs_5_), channel_id=1, source_target_pairs={{0,1},{1,2},{2,3},{3,0},{4,5},{5,6},{6,7},{7,4},{8,9},{9,10},{10,1... | collective-permute-start | bytes 3145736 | tf_op jit(solution)/shard_map/ppermute | solution.py:364
  67.3 9.1 %collective-permute-done.3.refs_3_ = bf16[64,4096]{1,0:T(8,128)(2,1)} collective-permute-done((bf16[64,4096]{1,0:T(8,128)(2,1)S(1)}, bf16[64,4096]{1,0:T(8,128)(2,1)}, u32[]{:S(2)}, u32[]{:S(2)}) %collective-permute-start.3) | collective-permute-done | bytes 524320 | tf_op jit(solution)/shard_map/ppermute | solution.py:362
  76.4 2.5 %collective-permute-start.7 = (bf16[64,4096]{1,0:T(8,128)(2,1)}, bf16[64,4096]{1,0:T(8,128)(2,1)}, u32[]{:S(2)}, u32[]{:S(2)}) collective-permute-start(bf16[64,4096]{1,0:T(8,128)(2,1)} %collective-permute-done.3.refs_3_), channel_id=1, source_target_pairs={{0,4},{4,0},{1,5},{5,1},{2,6},{6,2},{3,7},{7,3},{8,12},{12,8},{9,1... | collective-permute-start | bytes 1572872 | tf_op jit(solution)/shard_map/ppermute | solution.py:366
  80.1 2.5 %collective-permute-start.8 = (bf16[64,4096]{1,0:T(8,128)(2,1)}, bf16[64,4096]{1,0:T(8,128)(2,1)}, u32[]{:S(2)}, u32[]{:S(2)}) collective-permute-start(bf16[64,4096]{1,0:T(8,128)(2,1)} %collective-permute-done.4.refs_4_), channel_id=1, source_target_pairs={{0,4},{4,0},{1,5},{5,1},{2,6},{6,2},{3,7},{7,3},{8,12},{12,8},{9,1... | collective-permute-start | bytes 1572872 | tf_op jit(solution)/shard_map/ppermute | solution.py:367
  85.2 5.7 %shard_map.120 = (f32[8,512,128]{2,1,0:T(8,128)}, bf16[512,1024]{1,0:T(8,128)(2,1)}) custom-call(s32[8]{0:T(128)} %stack.87.slot_ref, bf16[8,2,512,128]{3,2,1,0:T(8,128)(2,1)} %copy-done, bf16[32,128,256]{2,1,0:T(8,128)(2,1)} %get-tuple-element.36.table_ref.refs_14_, f32[512,128]{1,0:T(8,128)} %get-tuple-element.37.gain_ref.refs_15_), custom_call_target="tpu_custom_call" | custom-call | flops 1 | bytes 1 | tf_op jit(solution)/shard_map/pallas_call | solution.py:371
  91.0 4.0 %collective-permute-done.8.refs_9_ = bf16[64,4096]{1,0:T(8,128)(2,1)} collective-permute-done((bf16[64,4096]{1,0:T(8,128)(2,1)}, bf16[64,4096]{1,0:T(8,128)(2,1)}, u32[]{:S(2)}, u32[]{:S(2)}) %collective-permute-start.8) | collective-permute-done | bytes 524320 | tf_op jit(solution)/shard_map/ppermute | solution.py:367
  95.0 16.8 %shard_map.122 = (bf16[8,512,256]{2,1,0:T(8,128)(2,1)}, bf16[8,512,256]{2,1,0:T(8,128)(2,1)}, bf16[8,512,128]{2,1,0:T(8,128)(2,1)}, bf16[8,2,512,128]{3,2,1,0:T(8,128)(2,1)}) custom-call(s32[1]{0:T(128)} %bitcast.2.core_ref, s32[8]{0:T(128)} %stack.82.place_ref, bf16[128,4096]{1,0:T(8,128)(2,1)} %bitcast.41, bf16[128,4096]{1,0:T(8,128)(2,1)} %copy-done.2, ...), custom_call_target="tpu_custom_call" | custom-call | flops 1 | bytes 300000000 | tf_op jit(solution)/shard_map/pallas_call | solution.py:379
  111.9 6.1 %all-to-all-start.1 = ((bf16[8,2,512,128]{3,2,1,0:T(8,128)(2,1)}), bf16[8,2,512,128]{3,2,1,0:T(8,128)(2,1)S(1)}, u32[]{:S(2)}, u32[]{:S(2)}) async-start(bf16[8,2,512,128]{3,2,1,0:T(8,128)(2,1)} %get-tuple-element.40), calls=%async_computation.1 | async-start | bytes 4194304 | tf_op jit(solution)/shard_map/all_to_all | solution.py:401
  118.6 3.8 %shard_map.124 = (bf16[2,512,256]{2,1,0:T(8,128)(2,1)}, bf16[2,512,256]{2,1,0:T(8,128)(2,1)}, bf16[2,512,256]{2,1,0:T(8,128)(2,1)}, bf16[2,512,256]{2,1,0:T(8,128)(2,1)}) custom-call(s32[4]{0:T(128)} %pad_add_fusion.1.order_ref, bf16[8,512,256]{2,1,0:T(8,128)(2,1)} %get-tuple-element.44.mine_ref, bf16[8,512,256]{2,1,0:T(8,128)(2,1)} %collective-permute-done.9.other_ref), custom_call_target="tpu_custom_call" | custom-call | flops 1 | bytes 1 | tf_op jit(solution)/shard_map/pallas_call | solution.py:404
  124.1 2.7 %collective-permute-start.11 = (bf16[2,512,256]{2,1,0:T(8,128)(2,1)}, bf16[2,512,256]{2,1,0:T(8,128)(2,1)S(1)}, u32[]{:S(2)}, u32[]{:S(2)}) collective-permute-start(bf16[2,512,256]{2,1,0:T(8,128)(2,1)} %get-tuple-element.48), channel_id=1, source_target_pairs={{0,64},{32,96},{64,0},{96,32},{1,65},{33,97},{65,1},{97,33},{2,66}... | collective-permute-start | bytes 1572872 | tf_op jit(solution)/shard_map/ppermute | solution.py:414
  128.3 6.2 %shard_map.125 = f32[48,128]{1,0:T(8,128)} custom-call(bf16[8,512,128]{2,1,0:T(8,128)(2,1)} %get-tuple-element.51.gm_ref, bf16[8,2,512,128]{3,2,1,0:T(8,128)(2,1)} %copy-done), custom_call_target="tpu_custom_call" | custom-call | flops 1 | bytes 1 | tf_op jit(solution)/shard_map/pallas_call | solution.py:413
  139.1 2.7 %collective-permute-start.15 = (f32[48,128]{1,0:T(8,128)S(1)}, f32[48,128]{1,0:T(8,128)S(1)}, u32[]{:S(2)}, u32[]{:S(2)}) collective-permute-start(f32[48,128]{1,0:T(8,128)S(1)} %add.151.refs_4_), channel_id=1, source_target_pairs={{0,64},{32,96},{64,0},{96,32},{1,65},{33,97},{65,1},{97,33},{2,66}... | collective-permute-start | bytes 73736 | tf_op jit(solution)/shard_map/ppermute | solution.py:417
  143.9 6.7 %collective-permute-done.11.refs_2_ = bf16[2,512,256]{2,1,0:T(8,128)(2,1)S(1)} collective-permute-done((bf16[2,512,256]{2,1,0:T(8,128)(2,1)}, bf16[2,512,256]{2,1,0:T(8,128)(2,1)S(1)}, u32[]{:S(2)}, u32[]{:S(2)}) %collective-permute-start.11) | collective-permute-done | bytes 524320 | tf_op jit(solution)/shard_map/ppermute | solution.py:414
  151.7 2.7 %shard_map.126 = (bf16[560,256]{1,0:T(8,128)(2,1)}, bf16[560,256]{1,0:T(8,128)(2,1)}) custom-call(s32[4]{0:T(128)} %pad_add_fusion.source_ref, s32[1]{0:T(128)} %bitcast.27.zh_ref, bf16[2,512,256]{2,1,0:T(8,128)(2,1)} %get-tuple-element.46.refs_0_, bf16[2,512,256]{2,1,0:T(8,128)(2,1)} %copy-done.3, bf16[2,512,256]{2,1,0:T(8,128)(2,1)} %copy-done.4, ...), custom_call_target="tpu_custom_call" | custom-call | flops 1 | bytes 1 | tf_op jit(solution)/shard_map/pallas_call | solution.py:421
  154.4 3.6 %collective-permute-start.17 = (bf16[560,256]{1,0:T(8,128)(2,1)}, bf16[560,256]{1,0:T(8,128)(2,1)S(1)}, u32[]{:S(2)}, u32[]{:S(2)}) collective-permute-start(bf16[560,256]{1,0:T(8,128)(2,1)} %get-tuple-element.54), channel_id=1, source_target_pairs={{0,16},{16,0},{1,17},{17,1},{2,18},{18,2},{3,19},{19,3},{4,20},{20... | collective-permute-start | bytes 860168 | tf_op jit(solution)/shard_map/ppermute | solution.py:428
  159.4 4.6 %shard_map.123 = (bf16[128,4096]{1,0:T(8,128)(2,1)}, bf16[128,4096]{1,0:T(8,128)(2,1)}, bf16[128,4096]{1,0:T(8,128)(2,1)}) custom-call(bf16[128,4096]{1,0:T(8,128)(2,1)} %bitcast.34, bf16[128,4096]{1,0:T(8,128)(2,1)} %bitcast.36, bf16[8,2,512,128]{3,2,1,0:T(8,128)(2,1)} %copy-done.1), custom_call_target="tpu_custom_call" | custom-call | flops 1 | bytes 1 | tf_op jit(solution)/shard_map/pallas_call | solution.py:418
  165.7 2.0 %shard_map.127 = (f32[256,512]{1,0:T(8,128)}, f32[32,128]{1,0:T(8,128)}, f32[4,128]{1,0:T(4,128)}) custom-call(bf16[560,256]{1,0:T(8,128)(2,1)} %get-tuple-element.53.mine_ref, bf16[560,256]{1,0:T(8,128)(2,1)} %copy-done.5), custom_call_target="tpu_custom_call" | custom-call | flops 1 | bytes 1 | tf_op jit(solution)/shard_map/pallas_call | solution.py:429
  (56 shorter events, 22.0 us)
Async XLA Ops:
  7.2 87.8 %all-gather.3.cloned.1.call-start = ((), (), s32[]{:S(2)}) async-start(), calls=%async_computation.2 | async-start | bytes 4456448 | tf_op jit(solution)/shard_map/all_gather | solution.py:347
  9.0 36.3 %collective-permute-start = (bf16[128,4096]{1,0:T(8,128)(2,1)}, bf16[128,4096]{1,0:T(8,128)(2,1)S(1)}, u32[]{:S(2)}, u32[]{:S(2)}) collective-permute-start(bf16[128,4096]{1,0:T(8,128)(2,1)} %bitcast.38), channel_id=1, source_target_pairs={{0,1},{1,2},{2,3},{3,0},{4,5},{5,6},{6,7},{7,4},{8,9},{9,10},{10,1... | collective-permute-start | bytes 3145736 | tf_op jit(solution)/shard_map/ppermute | solution.py:351
  10.7 34.7 %collective-permute-start.1 = (bf16[128,4096]{1,0:T(8,128)(2,1)}, bf16[128,4096]{1,0:T(8,128)(2,1)}, u32[]{:S(2)}, u32[]{:S(2)}) collective-permute-start(bf16[128,4096]{1,0:T(8,128)(2,1)} %bitcast.39), channel_id=1, source_target_pairs={{0,3},{1,0},{2,1},{3,2},{4,7},{5,4},{6,5},{7,6},{8,11},{9,8},{10,9... | collective-permute-start | bytes 3145736 | tf_op jit(solution)/shard_map/ppermute | solution.py:352
  11.1 34.2 %collective-permute-start.2 = (bf16[128,4096]{1,0:T(8,128)(2,1)}, bf16[128,4096]{1,0:T(8,128)(2,1)}, u32[]{:S(2)}, u32[]{:S(2)}) collective-permute-start(bf16[128,4096]{1,0:T(8,128)(2,1)} %bitcast.40), channel_id=1, source_target_pairs={{0,4},{4,0},{1,5},{5,1},{2,6},{6,2},{3,7},{7,3},{8,12},{12,8},{9,1... | collective-permute-start | bytes 3145736 | tf_op jit(solution)/shard_map/ppermute | solution.py:350
  16.9 66.9 %all-to-all-start = ((bf16[8,2,512,128]{3,2,1,0:T(8,128)(2,1)}), bf16[8,2,512,128]{3,2,1,0:T(8,128)(2,1)S(1)}, u32[]{:S(2)}, u32[]{:S(2)}) async-start(bf16[8,2,512,128]{3,2,1,0:T(8,128)(2,1)} %shard_map.119), calls=%async_computation | async-start | bytes 4194304 | tf_op jit(solution)/shard_map/all_to_all | solution.py:369
  45.4 45.6 %copy-start.2 = (bf16[128,4096]{1,0:T(8,128)(2,1)}, bf16[128,4096]{1,0:T(8,128)(2,1)S(1)}, u32[]{:S(2)}) copy-start(bf16[128,4096]{1,0:T(8,128)(2,1)S(1)} %collective-permute-done.refs_1_) | copy-start | bytes 3145732
  45.4 31.0 %collective-permute-start.3 = (bf16[64,4096]{1,0:T(8,128)(2,1)S(1)}, bf16[64,4096]{1,0:T(8,128)(2,1)}, u32[]{:S(2)}, u32[]{:S(2)}) collective-permute-start(bf16[64,4096]{1,0:T(8,128)(2,1)S(1)} %slice.6), channel_id=1, source_target_pairs={{0,1},{1,2},{2,3},{3,0},{4,5},{5,6},{6,7},{7,4},{8,9},{9,10},{10,1... | collective-permute-start | bytes 1572872 | tf_op jit(solution)/shard_map/ppermute | solution.py:362
  65.1 15.0 %collective-permute-start.4 = (bf16[64,4096]{1,0:T(8,128)(2,1)S(1)}, bf16[64,4096]{1,0:T(8,128)(2,1)}, u32[]{:S(2)}, u32[]{:S(2)}) collective-permute-start(bf16[64,4096]{1,0:T(8,128)(2,1)S(1)} %slice.7), channel_id=1, source_target_pairs={{0,3},{1,0},{2,1},{3,2},{4,7},{5,4},{6,5},{7,6},{8,11},{9,8},{10,9... | collective-permute-start | bytes 1572872 | tf_op jit(solution)/shard_map/ppermute | solution.py:363
  65.2 29.8 %collective-permute-start.5 = (bf16[128,4096]{1,0:T(8,128)(2,1)}, bf16[128,4096]{1,0:T(8,128)(2,1)}, u32[]{:S(2)}, u32[]{:S(2)}) collective-permute-start(bf16[128,4096]{1,0:T(8,128)(2,1)} %collective-permute-done.2.refs_5_), channel_id=1, source_target_pairs={{0,1},{1,2},{2,3},{3,0},{4,5},{5,6},{6,7},{7,4},{8,9},{9,10},{10,1... | collective-permute-start | bytes 3145736 | tf_op jit(solution)/shard_map/ppermute | solution.py:364
  67.2 27.8 %collective-permute-start.6 = (bf16[128,4096]{1,0:T(8,128)(2,1)}, bf16[128,4096]{1,0:T(8,128)(2,1)}, u32[]{:S(2)}, u32[]{:S(2)}) collective-permute-start(bf16[128,4096]{1,0:T(8,128)(2,1)} %collective-permute-done.2.refs_5_), channel_id=1, source_target_pairs={{0,3},{1,0},{2,1},{3,2},{4,7},{5,4},{6,5},{7,6},{8,11},{9,8},{10,9... | collective-permute-start | bytes 3145736 | tf_op jit(solution)/shard_map/ppermute | solution.py:365
  76.4 14.6 %collective-permute-start.7 = (bf16[64,4096]{1,0:T(8,128)(2,1)}, bf16[64,4096]{1,0:T(8,128)(2,1)}, u32[]{:S(2)}, u32[]{:S(2)}) collective-permute-start(bf16[64,4096]{1,0:T(8,128)(2,1)} %collective-permute-done.3.refs_3_), channel_id=1, source_target_pairs={{0,4},{4,0},{1,5},{5,1},{2,6},{6,2},{3,7},{7,3},{8,12},{12,8},{9,1... | collective-permute-start | bytes 1572872 | tf_op jit(solution)/shard_map/ppermute | solution.py:366
  80.1 14.8 %collective-permute-start.8 = (bf16[64,4096]{1,0:T(8,128)(2,1)}, bf16[64,4096]{1,0:T(8,128)(2,1)}, u32[]{:S(2)}, u32[]{:S(2)}) collective-permute-start(bf16[64,4096]{1,0:T(8,128)(2,1)} %collective-permute-done.4.refs_4_), channel_id=1, source_target_pairs={{0,4},{4,0},{1,5},{5,1},{2,6},{6,2},{3,7},{7,3},{8,12},{12,8},{9,1... | collective-permute-start | bytes 1572872 | tf_op jit(solution)/shard_map/ppermute | solution.py:367
  111.8 6.8 %collective-permute-start.9 = (bf16[8,512,256]{2,1,0:T(8,128)(2,1)}, bf16[8,512,256]{2,1,0:T(8,128)(2,1)}, u32[]{:S(2)}, u32[]{:S(2)}) collective-permute-start(bf16[8,512,256]{2,1,0:T(8,128)(2,1)} %get-tuple-element.45), channel_id=1, source_target_pairs={{0,8},{8,0},{1,9},{9,1},{2,10},{10,2},{3,11},{11,3},{4,12},{12,4},... | collective-permute-start | bytes 6291464 | tf_op jit(solution)/shard_map/ppermute | solution.py:400
  111.9 46.1 %all-to-all-start.1 = ((bf16[8,2,512,128]{3,2,1,0:T(8,128)(2,1)}), bf16[8,2,512,128]{3,2,1,0:T(8,128)(2,1)S(1)}, u32[]{:S(2)}, u32[]{:S(2)}) async-start(bf16[8,2,512,128]{3,2,1,0:T(8,128)(2,1)} %get-tuple-element.40), calls=%async_computation.1 | async-start | bytes 4194304 | tf_op jit(solution)/shard_map/all_to_all | solution.py:401
  122.4 15.5 %collective-permute-start.10 = (bf16[2,512,256]{2,1,0:T(8,128)(2,1)}, bf16[2,512,256]{2,1,0:T(8,128)(2,1)S(1)}, u32[]{:S(2)}, u32[]{:S(2)}) collective-permute-start(bf16[2,512,256]{2,1,0:T(8,128)(2,1)} %get-tuple-element.47), channel_id=1, source_target_pairs={{0,32},{32,64},{64,96},{96,0},{1,33},{33,65},{65,97},{97,1},{2,34}... | collective-permute-start | bytes 1572872 | tf_op jit(solution)/shard_map/ppermute | solution.py:414
  124.1 26.5 %collective-permute-start.11 = (bf16[2,512,256]{2,1,0:T(8,128)(2,1)}, bf16[2,512,256]{2,1,0:T(8,128)(2,1)S(1)}, u32[]{:S(2)}, u32[]{:S(2)}) collective-permute-start(bf16[2,512,256]{2,1,0:T(8,128)(2,1)} %get-tuple-element.48), channel_id=1, source_target_pairs={{0,64},{32,96},{64,0},{96,32},{1,65},{33,97},{65,1},{97,33},{2,66}... | collective-permute-start | bytes 1572872 | tf_op jit(solution)/shard_map/ppermute | solution.py:414
  126.8 23.8 %collective-permute-start.12 = (bf16[2,512,256]{2,1,0:T(8,128)(2,1)}, bf16[2,512,256]{2,1,0:T(8,128)(2,1)}, u32[]{:S(2)}, u32[]{:S(2)}) collective-permute-start(bf16[2,512,256]{2,1,0:T(8,128)(2,1)} %get-tuple-element.49), channel_id=1, source_target_pairs={{0,96},{32,0},{64,32},{96,64},{1,97},{33,1},{65,33},{97,65},{2,98}... | collective-permute-start | bytes 1572872 | tf_op jit(solution)/shard_map/ppermute | solution.py:414
  134.5 1.4 collective-permute-start.13
  136.6 14.5 %copy-start.6 = (f32[48,128]{1,0:T(8,128)}, f32[48,128]{1,0:T(8,128)S(1)}, u32[]{:S(2)}) copy-start(f32[48,128]{1,0:T(8,128)S(1)} %add.151.refs_4_) | copy-start | bytes 73732
  137.8 13.3 %copy-start.3 = (bf16[2,512,256]{2,1,0:T(8,128)(2,1)}, bf16[2,512,256]{2,1,0:T(8,128)(2,1)S(1)}, u32[]{:S(2)}) copy-start(bf16[2,512,256]{2,1,0:T(8,128)(2,1)S(1)} %collective-permute-done.10.refs_1_) | copy-start | bytes 1572868
  137.8 12.9 %collective-permute-start.14 = (f32[48,128]{1,0:T(8,128)S(1)}, f32[48,128]{1,0:T(8,128)S(1)}, u32[]{:S(2)}, u32[]{:S(2)}) collective-permute-start(f32[48,128]{1,0:T(8,128)S(1)} %add.151.refs_4_), channel_id=1, source_target_pairs={{0,32},{32,64},{64,96},{96,0},{1,33},{33,65},{65,97},{97,1},{2,34}... | collective-permute-start | bytes 73736 | tf_op jit(solution)/shard_map/ppermute | solution.py:417
  139.1 12.0 %collective-permute-start.15 = (f32[48,128]{1,0:T(8,128)S(1)}, f32[48,128]{1,0:T(8,128)S(1)}, u32[]{:S(2)}, u32[]{:S(2)}) collective-permute-start(f32[48,128]{1,0:T(8,128)S(1)} %add.151.refs_4_), channel_id=1, source_target_pairs={{0,64},{32,96},{64,0},{96,32},{1,65},{33,97},{65,1},{97,33},{2,66}... | collective-permute-start | bytes 73736 | tf_op jit(solution)/shard_map/ppermute | solution.py:417
  141.8 9.3 %collective-permute-start.16 = (f32[48,128]{1,0:T(8,128)S(1)}, f32[48,128]{1,0:T(8,128)S(1)}, u32[]{:S(2)}, u32[]{:S(2)}) collective-permute-start(f32[48,128]{1,0:T(8,128)S(1)} %add.151.refs_4_), channel_id=1, source_target_pairs={{0,96},{32,0},{64,32},{96,64},{1,97},{33,1},{65,33},{97,65},{2,98}... | collective-permute-start | bytes 73736 | tf_op jit(solution)/shard_map/ppermute | solution.py:417
  154.4 10.5 %collective-permute-start.17 = (bf16[560,256]{1,0:T(8,128)(2,1)}, bf16[560,256]{1,0:T(8,128)(2,1)S(1)}, u32[]{:S(2)}, u32[]{:S(2)}) collective-permute-start(bf16[560,256]{1,0:T(8,128)(2,1)} %get-tuple-element.54), channel_id=1, source_target_pairs={{0,16},{16,0},{1,17},{17,1},{2,18},{18,2},{3,19},{19,3},{4,20},{20... | collective-permute-start | bytes 860168 | tf_op jit(solution)/shard_map/ppermute | solution.py:428
  (7 other events, 6.1 us)
Sparse Core Ops, SparseCore 0:
  11.0 75.9 all-gather.2

commit v6 on v5

--- a/solution.py
+++ b/solution.py
@@ -118,13 +118,13 @@
     return copies
 
 
-def product_kernel(core_ref, place_ref, *refs):
+def product_kernel(core_ref, w_place_ref, place_ref, *refs):
     cot = refs[:10]
-    gated_ref, w_ref, streams = refs[10], refs[11], refs[12:16]
-    mine_ref, other_ref, gm_ref, out_ref = refs[16:20]
-    held, w_held, total, grad_ref = refs[20:24]
-    stream_held = refs[24:28]
-    sems, w_sems, out_sems, stream_sems = refs[28:]
+    gated_ref, w_refs, streams = refs[10], refs[11:19], refs[19:23]
+    mine_ref, other_ref, gm_ref, out_ref = refs[23:27]
+    held, w_held, total, grad_ref = refs[27:31]
+    stream_held = refs[31:35]
+    sems, w_sems, out_sems, stream_sems = refs[35:]
     mixed_ref, pq_ref, table_ref, gain_ref = stream_held
     blocks, channels, width = mine_ref.shape
     stripes = sems.shape[0]
@@ -138,8 +138,9 @@
     stripe_start(1)
     weights = []
     for d in range(2 * blocks):
+        cols = pl.ds(pl.multiple_of(w_place_ref[d] * width, width), width)
         weights.append(
-            pltpu.make_async_copy(w_ref.at[d], w_held.at[:, width * d : width * (d + 1)], w_sems.at[d])
+            pltpu.make_async_copy(w_refs[d // 2].at[d % 2], w_held.at[:, cols], w_sems.at[d])
         )
     ins = [
         pltpu.make_async_copy(ref, dst, stream_sems.at[i])
@@ -341,17 +342,25 @@
     slot_of = numbers([(zl ^ (p // 4)) * 4 + (y - p) % 4 for p in range(BLOCKS)])
     order = numbers([(x + i) % 4 for i in range(4)])
     source = numbers([(x - i) % 4 for i in range(4)])
+    w_place = numbers(
+        [((x - i) % 4 * 2 + (zh ^ d)) * 2 + (core ^ c) for c in range(2) for i in range(4) for d in range(2)]
+    )
     stream = shape((8, 2, panel, rows))
 
     w_t = call(transpose_kernel, shape((panel, outs_here)), [VMEM], VMEM)(out_weight)
-    w_all = lax.all_gather(w_t, DP, axis=0)
+    pq = call(prepare_kernel, stream, [VMEM] * 3, VMEM)(q, k, v)
+    w_other = after(lax.ppermute(w_t, "zh", ring(2, 1)), pq)
+    w_t = jnp.stack([w_t, w_other])
+    w_up, w_down = lax.ppermute(w_t, "x", ring(4, 1)), lax.ppermute(w_t, "x", ring(4, 3))
+    w_far = lax.ppermute(after(w_t, w_up, w_down), "x", ring(4, 2))
+    w_all = [w_t, w_up, w_far, w_down]
+    w_all = w_all + [lax.ppermute(w, "core", ring(2, 1)) for w in w_all]
 
     own = cot
-    own_z = lax.ppermute(own, "zl", ring(2, 1))
+    own_z = lax.ppermute(after(own, pq), "zl", ring(2, 1))
     up = lax.ppermute(own, "y", ring(4, 1))
     down = lax.ppermute(own, "y", ring(4, -1))
 
-    pq = call(prepare_kernel, stream, [VMEM] * 3, VMEM)(q, k, v)
     table, gain = call(
         table_kernel,
         [shape((groups, TAPS, 2 * TAPS)), shape((panel, TAPS), F32)],
@@ -379,7 +388,7 @@
     mine, other, gm, grads = call(
         product_kernel,
         [shape(by_core), shape(by_core), shape((BLOCKS, panel, rows)), stream],
-        [SMEM] * 2 + [ANY] * 10 + [VMEM] + [ANY] * 5,
+        [SMEM] * 3 + [ANY] * 10 + [VMEM] + [ANY] * 12,
         [ANY, ANY, VMEM, VMEM],
         scratch=[
             pltpu.VMEM((length, width), BF),
@@ -396,7 +405,7 @@
             pltpu.SemaphoreType.DMA((4,)),
         ],
         micros=100,
-    )(core.astype(jnp.int32).reshape(1), place, *cots, gated, w_all, mixed, pq, table, gain)
+    )(core.astype(jnp.int32).reshape(1), w_place, place, *cots, gated, *w_all, mixed, pq, table, gain)
     other = lax.ppermute(other, "core", ring(2, 1))
     grads = lax.all_to_all(grads, SEQ, split_axis=0, concat_axis=0, tiled=True)
 

time: 175 us -> 166 us (0.949)
  between operations: 14.1 us -> 0.8 us
  waiting for transfers between devices: 42.6 us -> 53.2 us
  starting transfers between devices: 56.1 us -> 48.5 us
    ppermute x1, waiting for transfers between devices: 17.4 us -> 0.01 us  [shards(): up = lax.ppermute(own, 'y', ring(4, 1))]
    ppermute x1 -> x9, waiting for transfers between devices: 0.01 us -> 14.1 us  [the longest x1 7.12 us: shards(): own_z = lax.ppermute(after(own, pq), 'zl', ring(2, 1))]
    ppermute x1, starting transfers between devices: 18.6 us -> 5.37 us  [shards(): far_a = lax.ppermute(up[:half], 'y', ring(4, 1))]
    ppermute x1, waiting for transfers between devices: 1.25 us -> 9.66 us  [shards(): far_b = lax.ppermute(down[half:], 'y', ring(4, -1))]
    ppermute x1, starting transfers between devices: 0.08 us -> 7.6 us  [shards(): far_b = lax.ppermute(down[half:], 'y', ring(4, -1))]
    ppermute x1, waiting for transfers between devices: 9.12 us -> 2.08 us  [shards(): far_a = lax.ppermute(up[:half], 'y', ring(4, 1))]
    ppermute x1 -> x9, starting transfers between devices: 1.92 us -> 8.34 us  [the longest x1 3.96 us: shards(): w_other = after(lax.ppermute(w_t, 'zh', ring(2, 1)), pq)]
    ppermute x1, waiting for transfers between devices: 0.01 us -> 5.62 us  [shards(): far_a_z = lax.ppermute(far_a, 'zl', ring(2, 1))]
  transfers between devices with their start and end apart: 21 -> 28, of which waited for: 10 -> 15; matrix products, arithmetic and copies ran while one was open for 2% -> 4% of each run, Pallas kernels for 19% -> 21%
where the time goes in v6:
time: 166 us
  Pallas kernels  53.4 us (32%)
  waiting for transfers between devices  53.2 us (32%)
  starting transfers between devices  48.5 us (29%)
  local copies, waits for them, and re-layouts  7.01 us (4%)
  other arithmetic  2.83 us (2%)
    pallas_call x1, Pallas kernels, shards(): call(product_kernel, [shape(by_core), shape(by_core), shape((BLOCKS, pane...  16.8 us
    ppermute x3, waiting for transfers between devices, shards(): lax.ppermute(lines[i], 'x', ring(4, i))  9.85 us
    ppermute x1, waiting for transfers between devices, shards(): far_b = lax.ppermute(down[half:], 'y', ring(4, -1))  9.66 us
    ppermute x1, starting transfers between devices, shards(): far_b = lax.ppermute(down[half:], 'y', ring(4, -1))  7.6 us
    ppermute x1, waiting for transfers between devices, shards(): own_z = lax.ppermute(after(own, pq), 'zl', ring(2, 1))  7.12 us
    all_to_all x1, starting transfers between devices, shards(): pq = lax.all_to_all(pq, SEQ, split_axis=0, concat_axis=0, tiled=True)  6.79 us
    pallas_call x1, Pallas kernels, shards(): call(filter_kernel, shape((SMALL, TAPS), F32), [VMEM, VMEM], VMEM)(gm, pq)  6.19 us
    pallas_call x1, Pallas kernels, shards(): call(table_kernel, [shape((groups, TAPS, 2 * TAPS)), shape((panel, TAPS),...  5.95 us
  transfers between devices with their start and end apart: 28, of which 15 were waited for; matrix products, arithmetic and copies ran while one was open for 4% of the time, Pallas kernels for 21%

profile of v6, /device:TPU:8, one launch (start us, length us, event | category | flops | bytes accessed | tf_op | source)
XLA Modules:
  0.0 165.8 jit_solution(4746194331018040616)
XLA Ops:
  2.9 4.0 %collective-permute-start.9 = (bf16[512,256]{1,0:T(8,128)(2,1)}, bf16[512,256]{1,0:T(8,128)(2,1)S(1)}, u32[]{:S(2)}, u32[]{:S(2)}) collective-permute-start(bf16[512,256]{1,0:T(8,128)(2,1)} %shard_map.121), channel_id=1, source_target_pairs={{0,16},{16,0},{1,17},{17,1},{2,18},{18,2},{3,19},{19,3},{4,20},{20... | collective-permute-start | bytes 786440 | tf_op jit(solution)/shard_map/ppermute | solution.py:352
  8.4 3.9 %shard_map.118 = bf16[8,2,512,128]{3,2,1,0:T(8,128)(2,1)} custom-call(bf16[128,4096]{1,0:T(8,128)(2,1)} %bitcast.53, bf16[128,4096]{1,0:T(8,128)(2,1)} %bitcast.49, bf16[128,4096]{1,0:T(8,128)(2,1)} %bitcast.51), custom_call_target="tpu_custom_call" | custom-call | flops 1 | bytes 1 | tf_op jit(solution)/shard_map/pallas_call | solution.py:351
  14.1 2.8 %collective-permute-start.11 = (bf16[2,512,256]{2,1,0:T(8,128)(2,1)}, bf16[2,512,256]{2,1,0:T(8,128)(2,1)}, u32[]{:S(2)}, u32[]{:S(2)}) collective-permute-start(bf16[2,512,256]{2,1,0:T(8,128)(2,1)} %pad_maximum_fusion.refs_11_), channel_id=1, source_target_pairs={{0,96},{32,0},{64,32},{96,64},{1,97},{33,1},{65,33},{97,65},{2,98}... | collective-permute-start | bytes 1572872 | tf_op jit(solution)/shard_map/ppermute | solution.py:354
  16.9 6.8 %all-to-all-start = ((bf16[8,2,512,128]{3,2,1,0:T(8,128)(2,1)}), bf16[8,2,512,128]{3,2,1,0:T(8,128)(2,1)S(1)}, u32[]{:S(2)}, u32[]{:S(2)}) async-start(bf16[8,2,512,128]{3,2,1,0:T(8,128)(2,1)} %shard_map.118), calls=%async_computation | async-start | bytes 4194304 | tf_op jit(solution)/shard_map/all_to_all | solution.py:378
  23.7 3.6 %collective-permute-done.11.refs_14_ = bf16[2,512,256]{2,1,0:T(8,128)(2,1)} collective-permute-done((bf16[2,512,256]{2,1,0:T(8,128)(2,1)}, bf16[2,512,256]{2,1,0:T(8,128)(2,1)}, u32[]{:S(2)}, u32[]{:S(2)}) %collective-permute-start.11) | collective-permute-done | bytes 524320 | tf_op jit(solution)/shard_map/ppermute | solution.py:354
  27.3 3.4 %collective-permute-done.10.refs_12_ = bf16[2,512,256]{2,1,0:T(8,128)(2,1)} collective-permute-done((bf16[2,512,256]{2,1,0:T(8,128)(2,1)}, bf16[2,512,256]{2,1,0:T(8,128)(2,1)}, u32[]{:S(2)}, u32[]{:S(2)}) %collective-permute-start.10) | collective-permute-done | bytes 524320 | tf_op jit(solution)/shard_map/ppermute | solution.py:354
  30.8 6.0 %shard_map.119 = (bf16[32,128,256]{2,1,0:T(8,128)(2,1)}, f32[512,128]{1,0:T(8,128)}) custom-call(s32[1]{0:T(128)} %bitcast.29.panel_ref, bf16[256,128]{1,0:T(8,128)(2,1)} %filters_ref.1, f32[8,4,128]{2,1,0:T(4,128)} %bitcast.56), custom_call_target="tpu_custom_call" | custom-call | flops 1 | bytes 1 | tf_op jit(solution)/shard_map/pallas_call | solution.py:364
  37.2 7.1 %collective-permute-done.2.refs_5_ = bf16[128,4096]{1,0:T(8,128)(2,1)} collective-permute-done((bf16[128,4096]{1,0:T(8,128)(2,1)}, bf16[128,4096]{1,0:T(8,128)(2,1)}, u32[]{:S(2)}, u32[]{:S(2)}) %collective-permute-start.2) | collective-permute-done | bytes 1048608 | tf_op jit(solution)/shard_map/ppermute | solution.py:360
  45.4 7.6 %collective-permute-start.4 = (bf16[64,4096]{1,0:T(8,128)(2,1)S(1)}, bf16[64,4096]{1,0:T(8,128)(2,1)}, u32[]{:S(2)}, u32[]{:S(2)}) collective-permute-start(bf16[64,4096]{1,0:T(8,128)(2,1)S(1)} %slice.7), channel_id=1, source_target_pairs={{0,3},{1,0},{2,1},{3,2},{4,7},{5,4},{6,5},{7,6},{8,11},{9,8},{10,9... | collective-permute-start | bytes 1572872 | tf_op jit(solution)/shard_map/ppermute | solution.py:372
  53.0 5.4 %collective-permute-start.3 = (bf16[64,4096]{1,0:T(8,128)(2,1)S(1)}, bf16[64,4096]{1,0:T(8,128)(2,1)}, u32[]{:S(2)}, u32[]{:S(2)}) collective-permute-start(bf16[64,4096]{1,0:T(8,128)(2,1)S(1)} %slice.6), channel_id=1, source_target_pairs={{0,1},{1,2},{2,3},{3,0},{4,5},{5,6},{6,7},{7,4},{8,9},{9,10},{10,1... | collective-permute-start | bytes 1572872 | tf_op jit(solution)/shard_map/ppermute | solution.py:371
  58.4 3.1 %collective-permute-start.6 = (bf16[128,4096]{1,0:T(8,128)(2,1)}, bf16[128,4096]{1,0:T(8,128)(2,1)}, u32[]{:S(2)}, u32[]{:S(2)}) collective-permute-start(bf16[128,4096]{1,0:T(8,128)(2,1)} %collective-permute-done.2.refs_5_), channel_id=1, source_target_pairs={{0,3},{1,0},{2,1},{3,2},{4,7},{5,4},{6,5},{7,6},{8,11},{9,8},{10,9... | collective-permute-start | bytes 3145736 | tf_op jit(solution)/shard_map/ppermute | solution.py:374
  61.6 9.7 %collective-permute-done.4.refs_4_ = bf16[64,4096]{1,0:T(8,128)(2,1)} collective-permute-done((bf16[64,4096]{1,0:T(8,128)(2,1)S(1)}, bf16[64,4096]{1,0:T(8,128)(2,1)}, u32[]{:S(2)}, u32[]{:S(2)}) %collective-permute-start.4) | collective-permute-done | bytes 524320 | tf_op jit(solution)/shard_map/ppermute | solution.py:372
  78.6 5.7 %shard_map.120 = (f32[8,512,128]{2,1,0:T(8,128)}, bf16[512,1024]{1,0:T(8,128)(2,1)}) custom-call(s32[8]{0:T(128)} %stack.164.slot_ref, bf16[8,2,512,128]{3,2,1,0:T(8,128)(2,1)} %copy-done, bf16[32,128,256]{2,1,0:T(8,128)(2,1)} %get-tuple-element.40.table_ref.refs_21_, f32[512,128]{1,0:T(8,128)} %get-tuple-element.41.gain_ref.refs_22_), custom_call_target="tpu_custom_call" | custom-call | flops 1 | bytes 1 | tf_op jit(solution)/shard_map/pallas_call | solution.py:380
  85.7 5.6 %collective-permute-done.7.refs_8_ = bf16[64,4096]{1,0:T(8,128)(2,1)} collective-permute-done((bf16[64,4096]{1,0:T(8,128)(2,1)}, bf16[64,4096]{1,0:T(8,128)(2,1)}, u32[]{:S(2)}, u32[]{:S(2)}) %collective-permute-start.7) | collective-permute-done | bytes 524320 | tf_op jit(solution)/shard_map/ppermute | solution.py:375
  91.4 3.9 %collective-permute-done.5.refs_6_ = bf16[128,4096]{1,0:T(8,128)(2,1)} collective-permute-done((bf16[128,4096]{1,0:T(8,128)(2,1)}, bf16[128,4096]{1,0:T(8,128)(2,1)}, u32[]{:S(2)}, u32[]{:S(2)}) %collective-permute-start.5) | collective-permute-done | bytes 1048608 | tf_op jit(solution)/shard_map/ppermute | solution.py:373
  95.2 16.8 %shard_map.122 = (bf16[8,512,256]{2,1,0:T(8,128)(2,1)}, bf16[8,512,256]{2,1,0:T(8,128)(2,1)}, bf16[8,512,128]{2,1,0:T(8,128)(2,1)}, bf16[8,2,512,128]{3,2,1,0:T(8,128)(2,1)}) custom-call(s32[1]{0:T(128)} %bitcast.2.core_ref, s32[16]{0:T(128)} %stack.150.w_place_ref, s32[8]{0:T(128)} %stack.159.place_ref, bf16[128,4096]{1,0:T(8,128)(2,1)} %bitcast.27.refs_0_, ...), custom_call_target="tpu_custom_call" | custom-call | flops 1 | bytes 300000000 | tf_op jit(solution)/shard_map/pallas_call | solution.py:388
  112.1 3.6 %all-to-all-start.1 = ((bf16[8,2,512,128]{3,2,1,0:T(8,128)(2,1)}), bf16[8,2,512,128]{3,2,1,0:T(8,128)(2,1)S(1)}, u32[]{:S(2)}, u32[]{:S(2)}) async-start(bf16[8,2,512,128]{3,2,1,0:T(8,128)(2,1)} %get-tuple-element.46), calls=%async_computation.1 | async-start | bytes 4194304 | tf_op jit(solution)/shard_map/all_to_all | solution.py:410
  116.6 3.8 %shard_map.124 = (bf16[2,512,256]{2,1,0:T(8,128)(2,1)}, bf16[2,512,256]{2,1,0:T(8,128)(2,1)}, bf16[2,512,256]{2,1,0:T(8,128)(2,1)}, bf16[2,512,256]{2,1,0:T(8,128)(2,1)}) custom-call(s32[4]{0:T(128)} %pad_add_fusion.1.order_ref, bf16[8,512,256]{2,1,0:T(8,128)(2,1)} %get-tuple-element.50.mine_ref, bf16[8,512,256]{2,1,0:T(8,128)(2,1)} %collective-permute-done.17.other_ref), custom_call_target="tpu_custom_call" | custom-call | flops 1 | bytes 1 | tf_op jit(solution)/shard_map/pallas_call | solution.py:413
  122.0 2.8 %collective-permute-start.19 = (bf16[2,512,256]{2,1,0:T(8,128)(2,1)}, bf16[2,512,256]{2,1,0:T(8,128)(2,1)S(1)}, u32[]{:S(2)}, u32[]{:S(2)}) collective-permute-start(bf16[2,512,256]{2,1,0:T(8,128)(2,1)} %get-tuple-element.54), channel_id=1, source_target_pairs={{0,64},{32,96},{64,0},{96,32},{1,65},{33,97},{65,1},{97,33},{2,66}... | collective-permute-start | bytes 1572872 | tf_op jit(solution)/shard_map/ppermute | solution.py:423
  126.1 6.2 %shard_map.125 = f32[48,128]{1,0:T(8,128)} custom-call(bf16[8,512,128]{2,1,0:T(8,128)(2,1)} %get-tuple-element.57.gm_ref, bf16[8,2,512,128]{3,2,1,0:T(8,128)(2,1)} %copy-done), custom_call_target="tpu_custom_call" | custom-call | flops 1 | bytes 1 | tf_op jit(solution)/shard_map/pallas_call | solution.py:422
  140.5 8.3 %collective-permute-done.19.refs_2_ = bf16[2,512,256]{2,1,0:T(8,128)(2,1)S(1)} collective-permute-done((bf16[2,512,256]{2,1,0:T(8,128)(2,1)}, bf16[2,512,256]{2,1,0:T(8,128)(2,1)S(1)}, u32[]{:S(2)}, u32[]{:S(2)}) %collective-permute-start.19) | collective-permute-done | bytes 524320 | tf_op jit(solution)/shard_map/ppermute | solution.py:423
  149.9 2.7 %shard_map.126 = (bf16[560,256]{1,0:T(8,128)(2,1)}, bf16[560,256]{1,0:T(8,128)(2,1)}) custom-call(s32[4]{0:T(128)} %pad_add_fusion.source_ref, s32[1]{0:T(128)} %bitcast.44.zh_ref, bf16[2,512,256]{2,1,0:T(8,128)(2,1)} %get-tuple-element.52.refs_0_, bf16[2,512,256]{2,1,0:T(8,128)(2,1)} %copy-done.4, bf16[2,512,256]{2,1,0:T(8,128)(2,1)} %copy-done.5, ...), custom_call_target="tpu_custom_call" | custom-call | flops 1 | bytes 1 | tf_op jit(solution)/shard_map/pallas_call | solution.py:430
  153.9 4.6 %shard_map.123 = (bf16[128,4096]{1,0:T(8,128)(2,1)}, bf16[128,4096]{1,0:T(8,128)(2,1)}, bf16[128,4096]{1,0:T(8,128)(2,1)}) custom-call(bf16[128,4096]{1,0:T(8,128)(2,1)} %bitcast.50, bf16[128,4096]{1,0:T(8,128)(2,1)} %bitcast.52, bf16[8,2,512,128]{3,2,1,0:T(8,128)(2,1)} %copy-done.1), custom_call_target="tpu_custom_call" | custom-call | flops 1 | bytes 1 | tf_op jit(solution)/shard_map/pallas_call | solution.py:427
  158.6 4.5 %collective-permute-done.25.other_ref = bf16[560,256]{1,0:T(8,128)(2,1)S(1)} collective-permute-done((bf16[560,256]{1,0:T(8,128)(2,1)}, bf16[560,256]{1,0:T(8,128)(2,1)S(1)}, u32[]{:S(2)}, u32[]{:S(2)}) %collective-permute-start.25) | collective-permute-done | bytes 286752 | tf_op jit(solution)/shard_map/ppermute | solution.py:437
  (75 shorter events, 33.4 us)
Async XLA Ops:
  0.6 30.1 %collective-permute-start.1 = (bf16[128,4096]{1,0:T(8,128)(2,1)}, bf16[128,4096]{1,0:T(8,128)(2,1)S(1)}, u32[]{:S(2)}, u32[]{:S(2)}) collective-permute-start(bf16[128,4096]{1,0:T(8,128)(2,1)} %bitcast.27.refs_0_), channel_id=1, source_target_pairs={{0,3},{1,0},{2,1},{3,2},{4,7},{5,4},{6,5},{7,6},{8,11},{9,8},{10,9... | collective-permute-start | bytes 3145736 | tf_op jit(solution)/shard_map/ppermute | solution.py:362
  6.8 30.0 %collective-permute-start = (bf16[128,4096]{1,0:T(8,128)(2,1)}, bf16[128,4096]{1,0:T(8,128)(2,1)}, u32[]{:S(2)}, u32[]{:S(2)}) collective-permute-start(bf16[128,4096]{1,0:T(8,128)(2,1)} %bitcast.27.refs_0_), channel_id=1, source_target_pairs={{0,1},{1,2},{2,3},{3,0},{4,5},{5,6},{6,7},{7,4},{8,9},{9,10},{10,1... | collective-permute-start | bytes 3145736 | tf_op jit(solution)/shard_map/ppermute | solution.py:361
  12.3 32.0 %collective-permute-start.2 = (bf16[128,4096]{1,0:T(8,128)(2,1)}, bf16[128,4096]{1,0:T(8,128)(2,1)}, u32[]{:S(2)}, u32[]{:S(2)}) collective-permute-start(bf16[128,4096]{1,0:T(8,128)(2,1)} %bitcast.27.refs_0_), channel_id=1, source_target_pairs={{0,4},{4,0},{1,5},{5,1},{2,6},{6,2},{3,7},{7,3},{8,12},{12,8},{9,1... | collective-permute-start | bytes 3145736 | tf_op jit(solution)/shard_map/ppermute | solution.py:360
  14.1 13.1 %collective-permute-start.11 = (bf16[2,512,256]{2,1,0:T(8,128)(2,1)}, bf16[2,512,256]{2,1,0:T(8,128)(2,1)}, u32[]{:S(2)}, u32[]{:S(2)}) collective-permute-start(bf16[2,512,256]{2,1,0:T(8,128)(2,1)} %pad_maximum_fusion.refs_11_), channel_id=1, source_target_pairs={{0,96},{32,0},{64,32},{96,64},{1,97},{33,1},{65,33},{97,65},{2,98}... | collective-permute-start | bytes 1572872 | tf_op jit(solution)/shard_map/ppermute | solution.py:354
  16.9 13.8 %collective-permute-start.10 = (bf16[2,512,256]{2,1,0:T(8,128)(2,1)}, bf16[2,512,256]{2,1,0:T(8,128)(2,1)}, u32[]{:S(2)}, u32[]{:S(2)}) collective-permute-start(bf16[2,512,256]{2,1,0:T(8,128)(2,1)} %pad_maximum_fusion.refs_11_), channel_id=1, source_target_pairs={{0,32},{32,64},{64,96},{96,0},{1,33},{33,65},{65,97},{97,1},{2,34}... | collective-permute-start | bytes 1572872 | tf_op jit(solution)/shard_map/ppermute | solution.py:354
  16.9 60.3 %all-to-all-start = ((bf16[8,2,512,128]{3,2,1,0:T(8,128)(2,1)}), bf16[8,2,512,128]{3,2,1,0:T(8,128)(2,1)S(1)}, u32[]{:S(2)}, u32[]{:S(2)}) async-start(bf16[8,2,512,128]{3,2,1,0:T(8,128)(2,1)} %shard_map.118), calls=%async_computation | async-start | bytes 4194304 | tf_op jit(solution)/shard_map/all_to_all | solution.py:378
  27.3 25.8 %collective-permute-start.13 = (bf16[2,512,256]{2,1,0:T(8,128)(2,1)}, bf16[2,512,256]{2,1,0:T(8,128)(2,1)}, u32[]{:S(2)}, u32[]{:S(2)}) collective-permute-start(bf16[2,512,256]{2,1,0:T(8,128)(2,1)} %pad_maximum_fusion.refs_11_), channel_id=1, source_target_pairs={{0,8},{8,0},{1,9},{9,1},{2,10},{10,2},{3,11},{11,3},{4,12},{12,4},... | collective-permute-start | bytes 1572872 | tf_op jit(solution)/shard_map/ppermute | solution.py:357
  30.7 27.7 %collective-permute-start.16 = (bf16[2,512,256]{2,1,0:T(8,128)(2,1)}, bf16[2,512,256]{2,1,0:T(8,128)(2,1)}, u32[]{:S(2)}, u32[]{:S(2)}) collective-permute-start(bf16[2,512,256]{2,1,0:T(8,128)(2,1)} %collective-permute-done.11.refs_14_), channel_id=1, source_target_pairs={{0,8},{8,0},{1,9},{9,1},{2,10},{10,2},{3,11},{11,3},{4,12},{12,4},... | collective-permute-start | bytes 1572872 | tf_op jit(solution)/shard_map/ppermute | solution.py:357
  30.7 30.8 %collective-permute-start.12 = (bf16[2,512,256]{2,1,0:T(8,128)(2,1)}, bf16[2,512,256]{2,1,0:T(8,128)(2,1)}, u32[]{:S(2)}, u32[]{:S(2)}) collective-permute-start(bf16[2,512,256]{2,1,0:T(8,128)(2,1)} %pad_maximum_fusion.refs_11_), channel_id=1, source_target_pairs={{0,64},{32,96},{64,0},{96,32},{1,65},{33,97},{65,1},{97,33},{2,66}... | collective-permute-start | bytes 1572872 | tf_op jit(solution)/shard_map/ppermute | solution.py:355
  36.8 24.7 %collective-permute-start.14 = (bf16[2,512,256]{2,1,0:T(8,128)(2,1)}, bf16[2,512,256]{2,1,0:T(8,128)(2,1)}, u32[]{:S(2)}, u32[]{:S(2)}) collective-permute-start(bf16[2,512,256]{2,1,0:T(8,128)(2,1)} %collective-permute-done.10.refs_12_), channel_id=1, source_target_pairs={{0,8},{8,0},{1,9},{9,1},{2,10},{10,2},{3,11},{11,3},{4,12},{12,4},... | collective-permute-start | bytes 1572872 | tf_op jit(solution)/shard_map/ppermute | solution.py:357
  45.4 25.8 %collective-permute-start.4 = (bf16[64,4096]{1,0:T(8,128)(2,1)S(1)}, bf16[64,4096]{1,0:T(8,128)(2,1)}, u32[]{:S(2)}, u32[]{:S(2)}) collective-permute-start(bf16[64,4096]{1,0:T(8,128)(2,1)S(1)} %slice.7), channel_id=1, source_target_pairs={{0,3},{1,0},{2,1},{3,2},{4,7},{5,4},{6,5},{7,6},{8,11},{9,8},{10,9... | collective-permute-start | bytes 1572872 | tf_op jit(solution)/shard_map/ppermute | solution.py:372
  53.0 21.3 %collective-permute-start.3 = (bf16[64,4096]{1,0:T(8,128)(2,1)S(1)}, bf16[64,4096]{1,0:T(8,128)(2,1)}, u32[]{:S(2)}, u32[]{:S(2)}) collective-permute-start(bf16[64,4096]{1,0:T(8,128)(2,1)S(1)} %slice.6), channel_id=1, source_target_pairs={{0,1},{1,2},{2,3},{3,0},{4,5},{5,6},{6,7},{7,4},{8,9},{9,10},{10,1... | collective-permute-start | bytes 1572872 | tf_op jit(solution)/shard_map/ppermute | solution.py:371
  58.4 33.0 %collective-permute-start.6 = (bf16[128,4096]{1,0:T(8,128)(2,1)}, bf16[128,4096]{1,0:T(8,128)(2,1)}, u32[]{:S(2)}, u32[]{:S(2)}) collective-permute-start(bf16[128,4096]{1,0:T(8,128)(2,1)} %collective-permute-done.2.refs_5_), channel_id=1, source_target_pairs={{0,3},{1,0},{2,1},{3,2},{4,7},{5,4},{6,5},{7,6},{8,11},{9,8},{10,9... | collective-permute-start | bytes 3145736 | tf_op jit(solution)/shard_map/ppermute | solution.py:374
  61.5 33.8 %collective-permute-start.5 = (bf16[128,4096]{1,0:T(8,128)(2,1)}, bf16[128,4096]{1,0:T(8,128)(2,1)}, u32[]{:S(2)}, u32[]{:S(2)}) collective-permute-start(bf16[128,4096]{1,0:T(8,128)(2,1)} %collective-permute-done.2.refs_5_), channel_id=1, source_target_pairs={{0,1},{1,2},{2,3},{3,0},{4,5},{5,6},{6,7},{7,4},{8,9},{9,10},{10,1... | collective-permute-start | bytes 3145736 | tf_op jit(solution)/shard_map/ppermute | solution.py:373
  61.5 22.8 %collective-permute-start.15 = (bf16[2,512,256]{2,1,0:T(8,128)(2,1)}, bf16[2,512,256]{2,1,0:T(8,128)(2,1)}, u32[]{:S(2)}, u32[]{:S(2)}) collective-permute-start(bf16[2,512,256]{2,1,0:T(8,128)(2,1)} %collective-permute-done.12.refs_13_), channel_id=1, source_target_pairs={{0,8},{8,0},{1,9},{9,1},{2,10},{10,2},{3,11},{11,3},{4,12},{12,4},... | collective-permute-start | bytes 1572872 | tf_op jit(solution)/shard_map/ppermute | solution.py:357
  71.3 14.5 %collective-permute-start.8 = (bf16[64,4096]{1,0:T(8,128)(2,1)}, bf16[64,4096]{1,0:T(8,128)(2,1)}, u32[]{:S(2)}, u32[]{:S(2)}) collective-permute-start(bf16[64,4096]{1,0:T(8,128)(2,1)} %collective-permute-done.4.refs_4_), channel_id=1, source_target_pairs={{0,4},{4,0},{1,5},{5,1},{2,6},{6,2},{3,7},{7,3},{8,12},{12,8},{9,1... | collective-permute-start | bytes 1572872 | tf_op jit(solution)/shard_map/ppermute | solution.py:376
  74.4 17.0 %collective-permute-start.7 = (bf16[64,4096]{1,0:T(8,128)(2,1)}, bf16[64,4096]{1,0:T(8,128)(2,1)}, u32[]{:S(2)}, u32[]{:S(2)}) collective-permute-start(bf16[64,4096]{1,0:T(8,128)(2,1)} %collective-permute-done.3.refs_3_), channel_id=1, source_target_pairs={{0,4},{4,0},{1,5},{5,1},{2,6},{6,2},{3,7},{7,3},{8,12},{12,8},{9,1... | collective-permute-start | bytes 1572872 | tf_op jit(solution)/shard_map/ppermute | solution.py:375
  112.1 40.5 %all-to-all-start.1 = ((bf16[8,2,512,128]{3,2,1,0:T(8,128)(2,1)}), bf16[8,2,512,128]{3,2,1,0:T(8,128)(2,1)S(1)}, u32[]{:S(2)}, u32[]{:S(2)}) async-start(bf16[8,2,512,128]{3,2,1,0:T(8,128)(2,1)} %get-tuple-element.46), calls=%async_computation.1 | async-start | bytes 4194304 | tf_op jit(solution)/shard_map/all_to_all | solution.py:410
  120.4 15.6 %collective-permute-start.18 = (bf16[2,512,256]{2,1,0:T(8,128)(2,1)}, bf16[2,512,256]{2,1,0:T(8,128)(2,1)S(1)}, u32[]{:S(2)}, u32[]{:S(2)}) collective-permute-start(bf16[2,512,256]{2,1,0:T(8,128)(2,1)} %get-tuple-element.53), channel_id=1, source_target_pairs={{0,32},{32,64},{64,96},{96,0},{1,33},{33,65},{65,97},{97,1},{2,34}... | collective-permute-start | bytes 1572872 | tf_op jit(solution)/shard_map/ppermute | solution.py:423
  122.0 26.9 %collective-permute-start.19 = (bf16[2,512,256]{2,1,0:T(8,128)(2,1)}, bf16[2,512,256]{2,1,0:T(8,128)(2,1)S(1)}, u32[]{:S(2)}, u32[]{:S(2)}) collective-permute-start(bf16[2,512,256]{2,1,0:T(8,128)(2,1)} %get-tuple-element.54), channel_id=1, source_target_pairs={{0,64},{32,96},{64,0},{96,32},{1,65},{33,97},{65,1},{97,33},{2,66}... | collective-permute-start | bytes 1572872 | tf_op jit(solution)/shard_map/ppermute | solution.py:423
  124.7 24.1 %collective-permute-start.20 = (bf16[2,512,256]{2,1,0:T(8,128)(2,1)}, bf16[2,512,256]{2,1,0:T(8,128)(2,1)S(1)}, u32[]{:S(2)}, u32[]{:S(2)}) collective-permute-start(bf16[2,512,256]{2,1,0:T(8,128)(2,1)} %get-tuple-element.55), channel_id=1, source_target_pairs={{0,96},{32,0},{64,32},{96,64},{1,97},{33,1},{65,33},{97,65},{2,98}... | collective-permute-start | bytes 1572872 | tf_op jit(solution)/shard_map/ppermute | solution.py:423
  136.0 12.8 %collective-permute-start.24 = (f32[48,128]{1,0:T(8,128)S(1)}, f32[48,128]{1,0:T(8,128)S(1)}, u32[]{:S(2)}, u32[]{:S(2)}) collective-permute-start(f32[48,128]{1,0:T(8,128)S(1)} %add.271.refs_4_), channel_id=1, source_target_pairs={{0,96},{32,0},{64,32},{96,64},{1,97},{33,1},{65,33},{97,65},{2,98}... | collective-permute-start | bytes 73736 | tf_op jit(solution)/shard_map/ppermute | solution.py:426
  138.2 10.9 %collective-permute-start.23 = (f32[48,128]{1,0:T(8,128)S(1)}, f32[48,128]{1,0:T(8,128)S(1)}, u32[]{:S(2)}, u32[]{:S(2)}) collective-permute-start(f32[48,128]{1,0:T(8,128)S(1)} %add.271.refs_4_), channel_id=1, source_target_pairs={{0,64},{32,96},{64,0},{96,32},{1,65},{33,97},{65,1},{97,33},{2,66}... | collective-permute-start | bytes 73736 | tf_op jit(solution)/shard_map/ppermute | solution.py:426
  152.6 10.5 %collective-permute-start.25 = (bf16[560,256]{1,0:T(8,128)(2,1)}, bf16[560,256]{1,0:T(8,128)(2,1)S(1)}, u32[]{:S(2)}, u32[]{:S(2)}) collective-permute-start(bf16[560,256]{1,0:T(8,128)(2,1)} %get-tuple-element.60), channel_id=1, source_target_pairs={{0,16},{16,0},{1,17},{17,1},{2,18},{18,2},{3,19},{19,3},{4,20},{20... | collective-permute-start | bytes 860168 | tf_op jit(solution)/shard_map/ppermute | solution.py:437
  (16 other events, 120.8 us)

commit v7 on v6

--- a/solution.py
+++ b/solution.py
@@ -63,8 +63,9 @@
         ).T
 
 
-def transpose_kernel(w_ref, out_ref):
-    out_ref[...] = w_ref[...].astype(F32).T.astype(BF)
+def transpose_kernel(own_ref, other_ref, out_ref):
+    for i, ref in enumerate((own_ref, other_ref)):
+        out_ref[i] = ref[...].astype(F32).T.astype(BF)
 
 
 def prepare_kernel(q_ref, k_ref, v_ref, out_ref):
@@ -120,11 +121,12 @@
 
 def product_kernel(core_ref, w_place_ref, place_ref, *refs):
     cot = refs[:10]
-    gated_ref, w_refs, streams = refs[10], refs[11:19], refs[19:23]
-    mine_ref, other_ref, gm_ref, out_ref = refs[23:27]
+    gated_in_ref, w_refs, streams = refs[10], refs[11:19], refs[19:23]
+    mine_ref, other_ref, gm_out_ref, out_out_ref = refs[23:27]
     held, w_held, total, grad_ref = refs[27:31]
     stream_held = refs[31:35]
-    sems, w_sems, out_sems, stream_sems = refs[35:]
+    gated_ref, gm_ref, out_ref = refs[35:38]
+    sems, w_sems, out_sems, stream_sems, back_sems = refs[38:]
     mixed_ref, pq_ref, table_ref, gain_ref = stream_held
     blocks, channels, width = mine_ref.shape
     stripes = sems.shape[0]
@@ -134,6 +136,8 @@
         for c in cot_copies(cot, held, lambda slot: sems.at[n], slice(span * n, span * (n + 1))):
             c.start()
 
+    gated_in = pltpu.make_async_copy(gated_in_ref, gated_ref, back_sems.at[0, 0])
+    gated_in.start()
     stripe_start(0)
     stripe_start(1)
     weights = []
@@ -154,6 +158,7 @@
             for i, ref in enumerate((mine_ref, other_ref))
         ]
 
+    gated_in.wait()
     for n in range(stripes):
         cols = slice(span * n, span * (n + 1))
         pltpu.make_async_copy(held.at[:, cols], held.at[:, cols], sems.at[n]).wait()
@@ -203,7 +208,19 @@
             out_ref[b, 1, rows, :] = result.astype(BF)
         return carry
 
-    lax.fori_loop(0, table_ref.shape[0], one_group, 0, unroll=4)
+    backs = []
+    quarter = table_ref.shape[0] // 4
+    for n in range(4):
+        lax.fori_loop(quarter * n, quarter * (n + 1), one_group, 0, unroll=4)
+        rows = slice(quarter * n * GROUP, quarter * (n + 1) * GROUP)
+        backs.append(pltpu.make_async_copy(gm_ref.at[:, rows], gm_out_ref.at[:, rows], back_sems.at[1, n]))
+        backs.append(
+            pltpu.make_async_copy(out_ref.at[:, :, rows], out_out_ref.at[:, :, rows], back_sems.at[2, n])
+        )
+        for c in backs[-2:]:
+            c.start()
+    for c in backs:
+        c.wait()
     for n in range(stripes):
         for c in out_copies(n):
             c.wait()
@@ -347,10 +364,9 @@
     )
     stream = shape((8, 2, panel, rows))
 
-    w_t = call(transpose_kernel, shape((panel, outs_here)), [VMEM], VMEM)(out_weight)
     pq = call(prepare_kernel, stream, [VMEM] * 3, VMEM)(q, k, v)
-    w_other = after(lax.ppermute(w_t, "zh", ring(2, 1)), pq)
-    w_t = jnp.stack([w_t, w_other])
+    w_other = after(lax.ppermute(out_weight, "zh", ring(2, 1)), pq)
+    w_t = call(transpose_kernel, shape((2, panel, outs_here)), [VMEM] * 2, VMEM)(out_weight, w_other)
     w_up, w_down = lax.ppermute(w_t, "x", ring(4, 1)), lax.ppermute(w_t, "x", ring(4, 3))
     w_far = lax.ppermute(after(w_t, w_up, w_down), "x", ring(4, 2))
     w_all = [w_t, w_up, w_far, w_down]
@@ -388,8 +404,8 @@
     mine, other, gm, grads = call(
         product_kernel,
         [shape(by_core), shape(by_core), shape((BLOCKS, panel, rows)), stream],
-        [SMEM] * 3 + [ANY] * 10 + [VMEM] + [ANY] * 12,
-        [ANY, ANY, VMEM, VMEM],
+        [SMEM] * 3 + [ANY] * 23,
+        [ANY] * 4,
         scratch=[
             pltpu.VMEM((length, width), BF),
             pltpu.VMEM((panel, width), BF),
@@ -399,10 +415,14 @@
             pltpu.VMEM(stream.shape, BF),
             pltpu.VMEM(table.shape, BF),
             pltpu.VMEM(gain.shape, F32),
+            pltpu.VMEM((panel, length), BF),
+            pltpu.VMEM((BLOCKS, panel, rows), BF),
+            pltpu.VMEM(stream.shape, BF),
             pltpu.SemaphoreType.DMA((4,)),
             pltpu.SemaphoreType.DMA((16,)),
             pltpu.SemaphoreType.DMA((2, 4)),
             pltpu.SemaphoreType.DMA((4,)),
+            pltpu.SemaphoreType.DMA((3, 4)),
         ],
         micros=100,
     )(core.astype(jnp.int32).reshape(1), w_place, place, *cots, gated, *w_all, mixed, pq, table, gain)

time: 166 us -> 163 us (0.982)
  waiting for transfers between devices: 53.2 us -> 48.7 us
    ppermute x1, waiting for transfers between devices: 3.88 us -> 0.01 us  [shards(): up_z = lax.ppermute(own_z, 'y', ring(4, 1))]
    ppermute x1, waiting for transfers between devices: 7.12 us -> 5.19 us  [shards(): own_z = lax.ppermute(after(own, pq), 'zl', ring(2, 1))]
  transfers between devices with their start and end apart: 28 -> 28, of which waited for: 15 -> 13; matrix products, arithmetic and copies ran while one was open for 4% -> 3% of each run, Pallas kernels for 21% -> 21%
where the time goes in v7:
time: 163 us; the launch traced here: 162 us
  Pallas kernels  53.3 us (33%)
  starting transfers between devices  49.9 us (31%)
  waiting for transfers between devices  48.7 us (30%)
  local copies, waits for them, and re-layouts  7.71 us (5%)
  other arithmetic  1.99 us (1%)
    pallas_call x1, Pallas kernels, shards(): call(product_kernel, [shape(by_core), shape(by_core), shape((BLOCKS, pane...  16.4 us
    ppermute x3, waiting for transfers between devices, shards(): lax.ppermute(lines[i], 'x', ring(4, i))  9.73 us
    ppermute x1, waiting for transfers between devices, shards(): far_b = lax.ppermute(down[half:], 'y', ring(4, -1))  9.66 us
    ppermute x1, starting transfers between devices, shards(): far_b = lax.ppermute(down[half:], 'y', ring(4, -1))  7.73 us
    all_to_all x1, starting transfers between devices, shards(): pq = lax.all_to_all(pq, SEQ, split_axis=0, concat_axis=0, tiled=True)  6.83 us
    ppermute x1, waiting for transfers between devices, shards(): far_a_z = lax.ppermute(far_a, 'zl', ring(2, 1))  6.53 us
    pallas_call x1, Pallas kernels, shards(): call(filter_kernel, shape((SMALL, TAPS), F32), [VMEM, VMEM], VMEM)(gm, pq)  6.19 us
    pallas_call x1, Pallas kernels, shards(): call(table_kernel, [shape((groups, TAPS, 2 * TAPS)), shape((panel, TAPS),...  5.95 us
  transfers between devices with their start and end apart: 28, of which 13 were waited for; matrix products, arithmetic and copies ran while one was open for 3% of the time, Pallas kernels for 21%

profile of v7, /device:TPU:8, one launch (start us, length us, event | category | flops | bytes accessed | tf_op | source)
XLA Modules:
  0.0 162.3 jit_solution(17569845119454820261)
XLA Ops:
  1.1 4.0 %collective-permute-start.9 = (bf16[256,512]{1,0:T(8,128)(2,1)}, bf16[256,512]{1,0:T(8,128)(2,1)S(1)}, u32[]{:S(2)}, u32[]{:S(2)}) collective-permute-start(bf16[256,512]{1,0:T(8,128)(2,1)} %own_ref.1), channel_id=1, source_target_pairs={{0,16},{16,0},{1,17},{17,1},{2,18},{18,2},{3,19},{19,3},{4,20},{20... | collective-permute-start | bytes 786440 | tf_op jit(solution)/shard_map/ppermute | solution.py:368
  6.6 3.8 %shard_map.118 = bf16[8,2,512,128]{3,2,1,0:T(8,128)(2,1)} custom-call(bf16[128,4096]{1,0:T(8,128)(2,1)} %bitcast.51, bf16[128,4096]{1,0:T(8,128)(2,1)} %bitcast.47, bf16[128,4096]{1,0:T(8,128)(2,1)} %bitcast.49), custom_call_target="tpu_custom_call" | custom-call | flops 1 | bytes 1 | tf_op jit(solution)/shard_map/pallas_call | solution.py:367
  14.2 2.8 %collective-permute-start.11 = (bf16[2,512,256]{2,1,0:T(8,128)(2,1)}, bf16[2,512,256]{2,1,0:T(8,128)(2,1)}, u32[]{:S(2)}, u32[]{:S(2)}) collective-permute-start(bf16[2,512,256]{2,1,0:T(8,128)(2,1)} %shard_map.121.refs_11_), channel_id=1, source_target_pairs={{0,96},{32,0},{64,32},{96,64},{1,97},{33,1},{65,33},{97,65},{2,98}... | collective-permute-start | bytes 1572872 | tf_op jit(solution)/shard_map/ppermute | solution.py:370
  17.0 6.8 %all-to-all-start = ((bf16[8,2,512,128]{3,2,1,0:T(8,128)(2,1)}), bf16[8,2,512,128]{3,2,1,0:T(8,128)(2,1)S(1)}, u32[]{:S(2)}, u32[]{:S(2)}) async-start(bf16[8,2,512,128]{3,2,1,0:T(8,128)(2,1)} %shard_map.118), calls=%async_computation | async-start | bytes 4194304 | tf_op jit(solution)/shard_map/all_to_all | solution.py:394
  23.8 3.6 %collective-permute-done.11.refs_14_ = bf16[2,512,256]{2,1,0:T(8,128)(2,1)} collective-permute-done((bf16[2,512,256]{2,1,0:T(8,128)(2,1)}, bf16[2,512,256]{2,1,0:T(8,128)(2,1)}, u32[]{:S(2)}, u32[]{:S(2)}) %collective-permute-start.11) | collective-permute-done | bytes 524320 | tf_op jit(solution)/shard_map/ppermute | solution.py:370
  27.4 3.4 %collective-permute-done.10.refs_12_ = bf16[2,512,256]{2,1,0:T(8,128)(2,1)} collective-permute-done((bf16[2,512,256]{2,1,0:T(8,128)(2,1)}, bf16[2,512,256]{2,1,0:T(8,128)(2,1)}, u32[]{:S(2)}, u32[]{:S(2)}) %collective-permute-start.10) | collective-permute-done | bytes 524320 | tf_op jit(solution)/shard_map/ppermute | solution.py:370
  30.9 6.0 %shard_map.119 = (bf16[32,128,256]{2,1,0:T(8,128)(2,1)}, f32[512,128]{1,0:T(8,128)}) custom-call(s32[1]{0:T(128)} %bitcast.29.panel_ref, bf16[256,128]{1,0:T(8,128)(2,1)} %filters_ref.1, f32[8,4,128]{2,1,0:T(4,128)} %bitcast.52), custom_call_target="tpu_custom_call" | custom-call | flops 1 | bytes 1 | tf_op jit(solution)/shard_map/pallas_call | solution.py:380
  37.3 5.2 %collective-permute-done.2.refs_5_ = bf16[128,4096]{1,0:T(8,128)(2,1)} collective-permute-done((bf16[128,4096]{1,0:T(8,128)(2,1)}, bf16[128,4096]{1,0:T(8,128)(2,1)}, u32[]{:S(2)}, u32[]{:S(2)}) %collective-permute-start.2) | collective-permute-done | bytes 1048608 | tf_op jit(solution)/shard_map/ppermute | solution.py:376
  43.6 7.7 %collective-permute-start.4 = (bf16[64,4096]{1,0:T(8,128)(2,1)S(1)}, bf16[64,4096]{1,0:T(8,128)(2,1)}, u32[]{:S(2)}, u32[]{:S(2)}) collective-permute-start(bf16[64,4096]{1,0:T(8,128)(2,1)S(1)} %slice.7), channel_id=1, source_target_pairs={{0,3},{1,0},{2,1},{3,2},{4,7},{5,4},{6,5},{7,6},{8,11},{9,8},{10,9... | collective-permute-start | bytes 1572872 | tf_op jit(solution)/shard_map/ppermute | solution.py:388
  51.3 5.2 %collective-permute-start.3 = (bf16[64,4096]{1,0:T(8,128)(2,1)S(1)}, bf16[64,4096]{1,0:T(8,128)(2,1)}, u32[]{:S(2)}, u32[]{:S(2)}) collective-permute-start(bf16[64,4096]{1,0:T(8,128)(2,1)S(1)} %slice.6), channel_id=1, source_target_pairs={{0,1},{1,2},{2,3},{3,0},{4,5},{5,6},{6,7},{7,4},{8,9},{9,10},{10,1... | collective-permute-start | bytes 1572872 | tf_op jit(solution)/shard_map/ppermute | solution.py:387
  56.6 3.1 %collective-permute-start.6 = (bf16[128,4096]{1,0:T(8,128)(2,1)}, bf16[128,4096]{1,0:T(8,128)(2,1)}, u32[]{:S(2)}, u32[]{:S(2)}) collective-permute-start(bf16[128,4096]{1,0:T(8,128)(2,1)} %collective-permute-done.2.refs_5_), channel_id=1, source_target_pairs={{0,3},{1,0},{2,1},{3,2},{4,7},{5,4},{6,5},{7,6},{8,11},{9,8},{10,9... | collective-permute-start | bytes 3145736 | tf_op jit(solution)/shard_map/ppermute | solution.py:390
  59.8 9.7 %collective-permute-done.4.refs_4_ = bf16[64,4096]{1,0:T(8,128)(2,1)} collective-permute-done((bf16[64,4096]{1,0:T(8,128)(2,1)S(1)}, bf16[64,4096]{1,0:T(8,128)(2,1)}, u32[]{:S(2)}, u32[]{:S(2)}) %collective-permute-start.4) | collective-permute-done | bytes 524320 | tf_op jit(solution)/shard_map/ppermute | solution.py:388
  76.8 5.7 %shard_map.120 = (f32[8,512,128]{2,1,0:T(8,128)}, bf16[512,1024]{1,0:T(8,128)(2,1)}) custom-call(s32[8]{0:T(128)} %stack.155.slot_ref, bf16[8,2,512,128]{3,2,1,0:T(8,128)(2,1)} %copy-done, bf16[32,128,256]{2,1,0:T(8,128)(2,1)} %get-tuple-element.40.table_ref.refs_21_, f32[512,128]{1,0:T(8,128)} %get-tuple-element.41.gain_ref.refs_22_), custom_call_target="tpu_custom_call" | custom-call | flops 1 | bytes 1 | tf_op jit(solution)/shard_map/pallas_call | solution.py:396
  84.6 6.5 %collective-permute-done.7.refs_8_ = bf16[64,4096]{1,0:T(8,128)(2,1)} collective-permute-done((bf16[64,4096]{1,0:T(8,128)(2,1)}, bf16[64,4096]{1,0:T(8,128)(2,1)}, u32[]{:S(2)}, u32[]{:S(2)}) %collective-permute-start.7) | collective-permute-done | bytes 524320 | tf_op jit(solution)/shard_map/ppermute | solution.py:391
  91.1 16.4 %shard_map.122 = (bf16[8,512,256]{2,1,0:T(8,128)(2,1)}, bf16[8,512,256]{2,1,0:T(8,128)(2,1)}, bf16[8,512,128]{2,1,0:T(8,128)(2,1)}, bf16[8,2,512,128]{3,2,1,0:T(8,128)(2,1)}) custom-call(s32[1]{0:T(128)} %bitcast.2.core_ref, s32[16]{0:T(128)} %stack.141.w_place_ref, s32[8]{0:T(128)} %stack.150.place_ref, bf16[128,4096]{1,0:T(8,128)(2,1)} %bitcast.27.refs_0_, ...), custom_call_target="tpu_custom_call" | custom-call | flops 1 | bytes 300000000 | tf_op jit(solution)/shard_map/pallas_call | solution.py:404
  107.7 4.9 %all-to-all-start.1 = ((bf16[8,2,512,128]{3,2,1,0:T(8,128)(2,1)}), bf16[8,2,512,128]{3,2,1,0:T(8,128)(2,1)S(1)}, u32[]{:S(2)}, u32[]{:S(2)}) async-start(bf16[8,2,512,128]{3,2,1,0:T(8,128)(2,1)} %get-tuple-element.46), calls=%async_computation.1 | async-start | bytes 4194304 | tf_op jit(solution)/shard_map/all_to_all | solution.py:430
  113.2 3.8 %shard_map.124 = (bf16[2,512,256]{2,1,0:T(8,128)(2,1)}, bf16[2,512,256]{2,1,0:T(8,128)(2,1)}, bf16[2,512,256]{2,1,0:T(8,128)(2,1)}, bf16[2,512,256]{2,1,0:T(8,128)(2,1)}) custom-call(s32[4]{0:T(128)} %pad_add_fusion.1.order_ref, bf16[8,512,256]{2,1,0:T(8,128)(2,1)} %get-tuple-element.50.mine_ref, bf16[8,512,256]{2,1,0:T(8,128)(2,1)} %collective-permute-done.17.other_ref), custom_call_target="tpu_custom_call" | custom-call | flops 1 | bytes 1 | tf_op jit(solution)/shard_map/pallas_call | solution.py:433
  118.5 2.8 %collective-permute-start.19 = (bf16[2,512,256]{2,1,0:T(8,128)(2,1)}, bf16[2,512,256]{2,1,0:T(8,128)(2,1)S(1)}, u32[]{:S(2)}, u32[]{:S(2)}) collective-permute-start(bf16[2,512,256]{2,1,0:T(8,128)(2,1)} %get-tuple-element.54), channel_id=1, source_target_pairs={{0,64},{32,96},{64,0},{96,32},{1,65},{33,97},{65,1},{97,33},{2,66}... | collective-permute-start | bytes 1572872 | tf_op jit(solution)/shard_map/ppermute | solution.py:443
  122.7 6.2 %shard_map.125 = f32[48,128]{1,0:T(8,128)} custom-call(bf16[8,512,128]{2,1,0:T(8,128)(2,1)} %get-tuple-element.57.gm_ref, bf16[8,2,512,128]{3,2,1,0:T(8,128)(2,1)} %copy-done), custom_call_target="tpu_custom_call" | custom-call | flops 1 | bytes 1 | tf_op jit(solution)/shard_map/pallas_call | solution.py:442
  132.5 2.3 %collective-permute-start.24 = (f32[48,128]{1,0:T(8,128)S(1)}, f32[48,128]{1,0:T(8,128)S(1)}, u32[]{:S(2)}, u32[]{:S(2)}) collective-permute-start(f32[48,128]{1,0:T(8,128)S(1)} %add.271.refs_4_), channel_id=1, source_target_pairs={{0,96},{32,0},{64,32},{96,64},{1,97},{33,1},{65,33},{97,65},{2,98}... | collective-permute-start | bytes 73736 | tf_op jit(solution)/shard_map/ppermute | solution.py:446
  137.1 8.3 %collective-permute-done.19.refs_2_ = bf16[2,512,256]{2,1,0:T(8,128)(2,1)S(1)} collective-permute-done((bf16[2,512,256]{2,1,0:T(8,128)(2,1)}, bf16[2,512,256]{2,1,0:T(8,128)(2,1)S(1)}, u32[]{:S(2)}, u32[]{:S(2)}) %collective-permute-start.19) | collective-permute-done | bytes 524320 | tf_op jit(solution)/shard_map/ppermute | solution.py:443
  146.4 2.7 %shard_map.126 = (bf16[560,256]{1,0:T(8,128)(2,1)}, bf16[560,256]{1,0:T(8,128)(2,1)}) custom-call(s32[4]{0:T(128)} %pad_add_fusion.source_ref, s32[1]{0:T(128)} %bitcast.42.zh_ref, bf16[2,512,256]{2,1,0:T(8,128)(2,1)} %get-tuple-element.52.refs_0_, bf16[2,512,256]{2,1,0:T(8,128)(2,1)} %copy-done.3, bf16[2,512,256]{2,1,0:T(8,128)(2,1)} %copy-done.4, ...), custom_call_target="tpu_custom_call" | custom-call | flops 1 | bytes 1 | tf_op jit(solution)/shard_map/pallas_call | solution.py:450
  150.5 4.6 %shard_map.123 = (bf16[128,4096]{1,0:T(8,128)(2,1)}, bf16[128,4096]{1,0:T(8,128)(2,1)}, bf16[128,4096]{1,0:T(8,128)(2,1)}) custom-call(bf16[128,4096]{1,0:T(8,128)(2,1)} %bitcast.48, bf16[128,4096]{1,0:T(8,128)(2,1)} %bitcast.50, bf16[8,2,512,128]{3,2,1,0:T(8,128)(2,1)} %copy-done.1), custom_call_target="tpu_custom_call" | custom-call | flops 1 | bytes 1 | tf_op jit(solution)/shard_map/pallas_call | solution.py:447
  155.1 4.5 %collective-permute-done.25.other_ref = bf16[560,256]{1,0:T(8,128)(2,1)S(1)} collective-permute-done((bf16[560,256]{1,0:T(8,128)(2,1)}, bf16[560,256]{1,0:T(8,128)(2,1)S(1)}, u32[]{:S(2)}, u32[]{:S(2)}) %collective-permute-start.25) | collective-permute-done | bytes 286752 | tf_op jit(solution)/shard_map/ppermute | solution.py:457
  (74 shorter events, 31.7 us)
Async XLA Ops:
  0.6 30.2 %collective-permute-start.1 = (bf16[128,4096]{1,0:T(8,128)(2,1)}, bf16[128,4096]{1,0:T(8,128)(2,1)S(1)}, u32[]{:S(2)}, u32[]{:S(2)}) collective-permute-start(bf16[128,4096]{1,0:T(8,128)(2,1)} %bitcast.27.refs_0_), channel_id=1, source_target_pairs={{0,3},{1,0},{2,1},{3,2},{4,7},{5,4},{6,5},{7,6},{8,11},{9,8},{10,9... | collective-permute-start | bytes 3145736 | tf_op jit(solution)/shard_map/ppermute | solution.py:378
  5.0 31.8 %collective-permute-start = (bf16[128,4096]{1,0:T(8,128)(2,1)}, bf16[128,4096]{1,0:T(8,128)(2,1)}, u32[]{:S(2)}, u32[]{:S(2)}) collective-permute-start(bf16[128,4096]{1,0:T(8,128)(2,1)} %bitcast.27.refs_0_), channel_id=1, source_target_pairs={{0,1},{1,2},{2,3},{3,0},{4,5},{5,6},{6,7},{7,4},{8,9},{9,10},{10,1... | collective-permute-start | bytes 3145736 | tf_op jit(solution)/shard_map/ppermute | solution.py:377
  10.4 32.0 %collective-permute-start.2 = (bf16[128,4096]{1,0:T(8,128)(2,1)}, bf16[128,4096]{1,0:T(8,128)(2,1)}, u32[]{:S(2)}, u32[]{:S(2)}) collective-permute-start(bf16[128,4096]{1,0:T(8,128)(2,1)} %bitcast.27.refs_0_), channel_id=1, source_target_pairs={{0,4},{4,0},{1,5},{5,1},{2,6},{6,2},{3,7},{7,3},{8,12},{12,8},{9,1... | collective-permute-start | bytes 3145736 | tf_op jit(solution)/shard_map/ppermute | solution.py:376
  14.2 13.2 %collective-permute-start.11 = (bf16[2,512,256]{2,1,0:T(8,128)(2,1)}, bf16[2,512,256]{2,1,0:T(8,128)(2,1)}, u32[]{:S(2)}, u32[]{:S(2)}) collective-permute-start(bf16[2,512,256]{2,1,0:T(8,128)(2,1)} %shard_map.121.refs_11_), channel_id=1, source_target_pairs={{0,96},{32,0},{64,32},{96,64},{1,97},{33,1},{65,33},{97,65},{2,98}... | collective-permute-start | bytes 1572872 | tf_op jit(solution)/shard_map/ppermute | solution.py:370
  17.0 13.8 %collective-permute-start.10 = (bf16[2,512,256]{2,1,0:T(8,128)(2,1)}, bf16[2,512,256]{2,1,0:T(8,128)(2,1)}, u32[]{:S(2)}, u32[]{:S(2)}) collective-permute-start(bf16[2,512,256]{2,1,0:T(8,128)(2,1)} %shard_map.121.refs_11_), channel_id=1, source_target_pairs={{0,32},{32,64},{64,96},{96,0},{1,33},{33,65},{65,97},{97,1},{2,34}... | collective-permute-start | bytes 1572872 | tf_op jit(solution)/shard_map/ppermute | solution.py:370
  17.0 58.5 %all-to-all-start = ((bf16[8,2,512,128]{3,2,1,0:T(8,128)(2,1)}), bf16[8,2,512,128]{3,2,1,0:T(8,128)(2,1)S(1)}, u32[]{:S(2)}, u32[]{:S(2)}) async-start(bf16[8,2,512,128]{3,2,1,0:T(8,128)(2,1)} %shard_map.118), calls=%async_computation | async-start | bytes 4194304 | tf_op jit(solution)/shard_map/all_to_all | solution.py:394
  27.4 24.0 %collective-permute-start.13 = (bf16[2,512,256]{2,1,0:T(8,128)(2,1)}, bf16[2,512,256]{2,1,0:T(8,128)(2,1)}, u32[]{:S(2)}, u32[]{:S(2)}) collective-permute-start(bf16[2,512,256]{2,1,0:T(8,128)(2,1)} %shard_map.121.refs_11_), channel_id=1, source_target_pairs={{0,8},{8,0},{1,9},{9,1},{2,10},{10,2},{3,11},{11,3},{4,12},{12,4},... | collective-permute-start | bytes 1572872 | tf_op jit(solution)/shard_map/ppermute | solution.py:373
  30.8 25.8 %collective-permute-start.16 = (bf16[2,512,256]{2,1,0:T(8,128)(2,1)}, bf16[2,512,256]{2,1,0:T(8,128)(2,1)}, u32[]{:S(2)}, u32[]{:S(2)}) collective-permute-start(bf16[2,512,256]{2,1,0:T(8,128)(2,1)} %collective-permute-done.11.refs_14_), channel_id=1, source_target_pairs={{0,8},{8,0},{1,9},{9,1},{2,10},{10,2},{3,11},{11,3},{4,12},{12,4},... | collective-permute-start | bytes 1572872 | tf_op jit(solution)/shard_map/ppermute | solution.py:373
  30.8 28.9 %collective-permute-start.12 = (bf16[2,512,256]{2,1,0:T(8,128)(2,1)}, bf16[2,512,256]{2,1,0:T(8,128)(2,1)}, u32[]{:S(2)}, u32[]{:S(2)}) collective-permute-start(bf16[2,512,256]{2,1,0:T(8,128)(2,1)} %shard_map.121.refs_11_), channel_id=1, source_target_pairs={{0,64},{32,96},{64,0},{96,32},{1,65},{33,97},{65,1},{97,33},{2,66}... | collective-permute-start | bytes 1572872 | tf_op jit(solution)/shard_map/ppermute | solution.py:371
  36.9 22.8 %collective-permute-start.14 = (bf16[2,512,256]{2,1,0:T(8,128)(2,1)}, bf16[2,512,256]{2,1,0:T(8,128)(2,1)}, u32[]{:S(2)}, u32[]{:S(2)}) collective-permute-start(bf16[2,512,256]{2,1,0:T(8,128)(2,1)} %collective-permute-done.10.refs_12_), channel_id=1, source_target_pairs={{0,8},{8,0},{1,9},{9,1},{2,10},{10,2},{3,11},{11,3},{4,12},{12,4},... | collective-permute-start | bytes 1572872 | tf_op jit(solution)/shard_map/ppermute | solution.py:373
  43.6 25.8 %collective-permute-start.4 = (bf16[64,4096]{1,0:T(8,128)(2,1)S(1)}, bf16[64,4096]{1,0:T(8,128)(2,1)}, u32[]{:S(2)}, u32[]{:S(2)}) collective-permute-start(bf16[64,4096]{1,0:T(8,128)(2,1)S(1)} %slice.7), channel_id=1, source_target_pairs={{0,3},{1,0},{2,1},{3,2},{4,7},{5,4},{6,5},{7,6},{8,11},{9,8},{10,9... | collective-permute-start | bytes 1572872 | tf_op jit(solution)/shard_map/ppermute | solution.py:388
  51.3 21.2 %collective-permute-start.3 = (bf16[64,4096]{1,0:T(8,128)(2,1)S(1)}, bf16[64,4096]{1,0:T(8,128)(2,1)}, u32[]{:S(2)}, u32[]{:S(2)}) collective-permute-start(bf16[64,4096]{1,0:T(8,128)(2,1)S(1)} %slice.6), channel_id=1, source_target_pairs={{0,1},{1,2},{2,3},{3,0},{4,5},{5,6},{6,7},{7,4},{8,9},{9,10},{10,1... | collective-permute-start | bytes 1572872 | tf_op jit(solution)/shard_map/ppermute | solution.py:387
  56.6 34.6 %collective-permute-start.6 = (bf16[128,4096]{1,0:T(8,128)(2,1)}, bf16[128,4096]{1,0:T(8,128)(2,1)}, u32[]{:S(2)}, u32[]{:S(2)}) collective-permute-start(bf16[128,4096]{1,0:T(8,128)(2,1)} %collective-permute-done.2.refs_5_), channel_id=1, source_target_pairs={{0,3},{1,0},{2,1},{3,2},{4,7},{5,4},{6,5},{7,6},{8,11},{9,8},{10,9... | collective-permute-start | bytes 3145736 | tf_op jit(solution)/shard_map/ppermute | solution.py:390
  59.7 31.5 %collective-permute-start.5 = (bf16[128,4096]{1,0:T(8,128)(2,1)}, bf16[128,4096]{1,0:T(8,128)(2,1)}, u32[]{:S(2)}, u32[]{:S(2)}) collective-permute-start(bf16[128,4096]{1,0:T(8,128)(2,1)} %collective-permute-done.2.refs_5_), channel_id=1, source_target_pairs={{0,1},{1,2},{2,3},{3,0},{4,5},{5,6},{6,7},{7,4},{8,9},{9,10},{10,1... | collective-permute-start | bytes 3145736 | tf_op jit(solution)/shard_map/ppermute | solution.py:389
  59.7 22.8 %collective-permute-start.15 = (bf16[2,512,256]{2,1,0:T(8,128)(2,1)}, bf16[2,512,256]{2,1,0:T(8,128)(2,1)}, u32[]{:S(2)}, u32[]{:S(2)}) collective-permute-start(bf16[2,512,256]{2,1,0:T(8,128)(2,1)} %collective-permute-done.12.refs_13_), channel_id=1, source_target_pairs={{0,8},{8,0},{1,9},{9,1},{2,10},{10,2},{3,11},{11,3},{4,12},{12,4},... | collective-permute-start | bytes 1572872 | tf_op jit(solution)/shard_map/ppermute | solution.py:373
  69.4 15.2 %collective-permute-start.8 = (bf16[64,4096]{1,0:T(8,128)(2,1)}, bf16[64,4096]{1,0:T(8,128)(2,1)}, u32[]{:S(2)}, u32[]{:S(2)}) collective-permute-start(bf16[64,4096]{1,0:T(8,128)(2,1)} %collective-permute-done.4.refs_4_), channel_id=1, source_target_pairs={{0,4},{4,0},{1,5},{5,1},{2,6},{6,2},{3,7},{7,3},{8,12},{12,8},{9,1... | collective-permute-start | bytes 1572872 | tf_op jit(solution)/shard_map/ppermute | solution.py:392
  72.5 18.6 %collective-permute-start.7 = (bf16[64,4096]{1,0:T(8,128)(2,1)}, bf16[64,4096]{1,0:T(8,128)(2,1)}, u32[]{:S(2)}, u32[]{:S(2)}) collective-permute-start(bf16[64,4096]{1,0:T(8,128)(2,1)} %collective-permute-done.3.refs_3_), channel_id=1, source_target_pairs={{0,4},{4,0},{1,5},{5,1},{2,6},{6,2},{3,7},{7,3},{8,12},{12,8},{9,1... | collective-permute-start | bytes 1572872 | tf_op jit(solution)/shard_map/ppermute | solution.py:391
  107.7 41.4 %all-to-all-start.1 = ((bf16[8,2,512,128]{3,2,1,0:T(8,128)(2,1)}), bf16[8,2,512,128]{3,2,1,0:T(8,128)(2,1)S(1)}, u32[]{:S(2)}, u32[]{:S(2)}) async-start(bf16[8,2,512,128]{3,2,1,0:T(8,128)(2,1)} %get-tuple-element.46), calls=%async_computation.1 | async-start | bytes 4194304 | tf_op jit(solution)/shard_map/all_to_all | solution.py:430
  117.0 15.5 %collective-permute-start.18 = (bf16[2,512,256]{2,1,0:T(8,128)(2,1)}, bf16[2,512,256]{2,1,0:T(8,128)(2,1)S(1)}, u32[]{:S(2)}, u32[]{:S(2)}) collective-permute-start(bf16[2,512,256]{2,1,0:T(8,128)(2,1)} %get-tuple-element.53), channel_id=1, source_target_pairs={{0,32},{32,64},{64,96},{96,0},{1,33},{33,65},{65,97},{97,1},{2,34}... | collective-permute-start | bytes 1572872 | tf_op jit(solution)/shard_map/ppermute | solution.py:443
  118.5 26.8 %collective-permute-start.19 = (bf16[2,512,256]{2,1,0:T(8,128)(2,1)}, bf16[2,512,256]{2,1,0:T(8,128)(2,1)S(1)}, u32[]{:S(2)}, u32[]{:S(2)}) collective-permute-start(bf16[2,512,256]{2,1,0:T(8,128)(2,1)} %get-tuple-element.54), channel_id=1, source_target_pairs={{0,64},{32,96},{64,0},{96,32},{1,65},{33,97},{65,1},{97,33},{2,66}... | collective-permute-start | bytes 1572872 | tf_op jit(solution)/shard_map/ppermute | solution.py:443
  121.3 24.0 %collective-permute-start.20 = (bf16[2,512,256]{2,1,0:T(8,128)(2,1)}, bf16[2,512,256]{2,1,0:T(8,128)(2,1)S(1)}, u32[]{:S(2)}, u32[]{:S(2)}) collective-permute-start(bf16[2,512,256]{2,1,0:T(8,128)(2,1)} %get-tuple-element.55), channel_id=1, source_target_pairs={{0,96},{32,0},{64,32},{96,64},{1,97},{33,1},{65,33},{97,65},{2,98}... | collective-permute-start | bytes 1572872 | tf_op jit(solution)/shard_map/ppermute | solution.py:443
  132.5 12.8 %collective-permute-start.24 = (f32[48,128]{1,0:T(8,128)S(1)}, f32[48,128]{1,0:T(8,128)S(1)}, u32[]{:S(2)}, u32[]{:S(2)}) collective-permute-start(f32[48,128]{1,0:T(8,128)S(1)} %add.271.refs_4_), channel_id=1, source_target_pairs={{0,96},{32,0},{64,32},{96,64},{1,97},{33,1},{65,33},{97,65},{2,98}... | collective-permute-start | bytes 73736 | tf_op jit(solution)/shard_map/ppermute | solution.py:446
  134.8 10.8 %collective-permute-start.23 = (f32[48,128]{1,0:T(8,128)S(1)}, f32[48,128]{1,0:T(8,128)S(1)}, u32[]{:S(2)}, u32[]{:S(2)}) collective-permute-start(f32[48,128]{1,0:T(8,128)S(1)} %add.271.refs_4_), channel_id=1, source_target_pairs={{0,64},{32,96},{64,0},{96,32},{1,65},{33,97},{65,1},{97,33},{2,66}... | collective-permute-start | bytes 73736 | tf_op jit(solution)/shard_map/ppermute | solution.py:446
  149.1 10.5 %collective-permute-start.25 = (bf16[560,256]{1,0:T(8,128)(2,1)}, bf16[560,256]{1,0:T(8,128)(2,1)S(1)}, u32[]{:S(2)}, u32[]{:S(2)}) collective-permute-start(bf16[560,256]{1,0:T(8,128)(2,1)} %get-tuple-element.60), channel_id=1, source_target_pairs={{0,16},{16,0},{1,17},{17,1},{2,18},{18,2},{3,19},{19,3},{4,20},{20... | collective-permute-start | bytes 860168 | tf_op jit(solution)/shard_map/ppermute | solution.py:457
  (16 other events, 115.5 us)

commit v8 on v7

--- a/solution.py
+++ b/solution.py
@@ -68,13 +68,29 @@
         out_ref[i] = ref[...].astype(F32).T.astype(BF)
 
 
-def prepare_kernel(q_ref, k_ref, v_ref, out_ref):
-    width = out_ref.shape[2]
-    for j in range(out_ref.shape[0]):
+def prepare_kernel(q_ref, k_ref, v_ref, out_ref, held, result, sems, out_sems):
+    blocks, _, width, _ = out_ref.shape
+    ins = []
+    for j in range(blocks):
         cols = slice(j * width, (j + 1) * width)
-        product = k_ref[:, cols].astype(F32) * v_ref[:, cols].astype(F32)
-        out_ref[j, 0] = product.T.astype(BF)
-        out_ref[j, 1] = q_ref[:, cols].astype(F32).T.astype(BF)
+        ins.append([
+            pltpu.make_async_copy(ref.at[:, cols], held.at[i, :, cols], sems.at[j, i])
+            for i, ref in enumerate((q_ref, k_ref, v_ref))
+        ])
+        for c in ins[-1]:
+            c.start()
+    backs = []
+    for j in range(blocks):
+        cols = slice(j * width, (j + 1) * width)
+        for c in ins[j]:
+            c.wait()
+        product = held[1, :, cols].astype(F32) * held[2, :, cols].astype(F32)
+        result[j, 0] = product.T.astype(BF)
+        result[j, 1] = held[0, :, cols].astype(F32).T.astype(BF)
+        backs.append(pltpu.make_async_copy(result.at[j], out_ref.at[j], out_sems.at[j]))
+        backs[-1].start()
+    for c in backs:
+        c.wait()
 
 
 def forward_kernel(slot_ref, pq_ref, table_ref, gain_ref, mixed_ref, gated_ref):
@@ -364,7 +380,18 @@
     )
     stream = shape((8, 2, panel, rows))
 
-    pq = call(prepare_kernel, stream, [VMEM] * 3, VMEM)(q, k, v)
+    pq = call(
+        prepare_kernel,
+        stream,
+        [ANY] * 3,
+        ANY,
+        scratch=[
+            pltpu.VMEM((3, rows, width), BF),
+            pltpu.VMEM(stream.shape, BF),
+            pltpu.SemaphoreType.DMA((8, 3)),
+            pltpu.SemaphoreType.DMA((8,)),
+        ],
+    )(q, k, v)
     w_other = after(lax.ppermute(out_weight, "zh", ring(2, 1)), pq)
     w_t = call(transpose_kernel, shape((2, panel, outs_here)), [VMEM] * 2, VMEM)(out_weight, w_other)
     w_up, w_down = lax.ppermute(w_t, "x", ring(4, 1)), lax.ppermute(w_t, "x", ring(4, 3))

time: 163 us -> 163 us (level)
  transfers between devices with their start and end apart: 28 -> 28, of which waited for: 13 -> 15; matrix products, arithmetic and copies ran while one was open for 3% -> 3% of each run, Pallas kernels for 21% -> 21%
where the time goes in v8:
time: 163 us; the launch traced here: 162 us
  Pallas kernels  52.7 us (32%)
  waiting for transfers between devices  50.3 us (31%)
  starting transfers between devices  48.8 us (30%)
  local copies, waits for them, and re-layouts  7.7 us (5%)
  other arithmetic  1.99 us (1%)
    pallas_call x1, Pallas kernels, shards(): call(product_kernel, [shape(by_core), shape(by_core), shape((BLOCKS, pane...  16.4 us
    ppermute x3, waiting for transfers between devices, shards(): lax.ppermute(lines[i], 'x', ring(4, i))  10.5 us
    ppermute x1, waiting for transfers between devices, shards(): far_b = lax.ppermute(down[half:], 'y', ring(4, -1))  9.8 us
    ppermute x1, starting transfers between devices, shards(): far_b = lax.ppermute(down[half:], 'y', ring(4, -1))  9.26 us
    ppermute x1, waiting for transfers between devices, shards(): far_a_z = lax.ppermute(far_a, 'zl', ring(2, 1))  7.38 us
    all_to_all x1, starting transfers between devices, shards(): pq = lax.all_to_all(pq, SEQ, split_axis=0, concat_axis=0, tiled=True)  7.35 us
    pallas_call x1, Pallas kernels, shards(): call(filter_kernel, shape((SMALL, TAPS), F32), [VMEM, VMEM], VMEM)(gm, pq)  6.19 us
    pallas_call x1, Pallas kernels, shards(): call(table_kernel, [shape((groups, TAPS, 2 * TAPS)), shape((panel, TAPS),...  5.95 us
  transfers between devices with their start and end apart: 28, of which 15 were waited for; matrix products, arithmetic and copies ran while one was open for 3% of the time, Pallas kernels for 21%

profile of v8, /device:TPU:8, one launch (start us, length us, event | category | flops | bytes accessed | tf_op | source)
XLA Modules:
  0.0 162.3 jit_solution(4467617942686119773)
XLA Ops:
  1.1 4.0 %collective-permute-start.9 = (bf16[256,512]{1,0:T(8,128)(2,1)}, bf16[256,512]{1,0:T(8,128)(2,1)S(1)}, u32[]{:S(2)}, u32[]{:S(2)}) collective-permute-start(bf16[256,512]{1,0:T(8,128)(2,1)} %own_ref.1), channel_id=1, source_target_pairs={{0,16},{16,0},{1,17},{17,1},{2,18},{18,2},{3,19},{19,3},{4,20},{20... | collective-permute-start | bytes 786440 | tf_op jit(solution)/shard_map/ppermute | solution.py:395
  6.6 3.2 %shard_map.118 = bf16[8,2,512,128]{3,2,1,0:T(8,128)(2,1)} custom-call(bf16[128,4096]{1,0:T(8,128)(2,1)} %bitcast.51, bf16[128,4096]{1,0:T(8,128)(2,1)} %bitcast.47, bf16[128,4096]{1,0:T(8,128)(2,1)} %bitcast.49), custom_call_target="tpu_custom_call" | custom-call | flops 1 | bytes 1 | tf_op jit(solution)/shard_map/pallas_call | solution.py:383
  14.0 2.8 %collective-permute-start.11 = (bf16[2,512,256]{2,1,0:T(8,128)(2,1)}, bf16[2,512,256]{2,1,0:T(8,128)(2,1)}, u32[]{:S(2)}, u32[]{:S(2)}) collective-permute-start(bf16[2,512,256]{2,1,0:T(8,128)(2,1)} %shard_map.121.refs_11_), channel_id=1, source_target_pairs={{0,96},{32,0},{64,32},{96,64},{1,97},{33,1},{65,33},{97,65},{2,98}... | collective-permute-start | bytes 1572872 | tf_op jit(solution)/shard_map/ppermute | solution.py:397
  16.8 7.3 %all-to-all-start = ((bf16[8,2,512,128]{3,2,1,0:T(8,128)(2,1)}), bf16[8,2,512,128]{3,2,1,0:T(8,128)(2,1)S(1)}, u32[]{:S(2)}, u32[]{:S(2)}) async-start(bf16[8,2,512,128]{3,2,1,0:T(8,128)(2,1)} %shard_map.118), calls=%async_computation | async-start | bytes 4194304 | tf_op jit(solution)/shard_map/all_to_all | solution.py:421
  24.1 3.3 %collective-permute-done.11.refs_14_ = bf16[2,512,256]{2,1,0:T(8,128)(2,1)} collective-permute-done((bf16[2,512,256]{2,1,0:T(8,128)(2,1)}, bf16[2,512,256]{2,1,0:T(8,128)(2,1)}, u32[]{:S(2)}, u32[]{:S(2)}) %collective-permute-start.11) | collective-permute-done | bytes 524320 | tf_op jit(solution)/shard_map/ppermute | solution.py:397
  27.4 3.4 %collective-permute-done.10.refs_12_ = bf16[2,512,256]{2,1,0:T(8,128)(2,1)} collective-permute-done((bf16[2,512,256]{2,1,0:T(8,128)(2,1)}, bf16[2,512,256]{2,1,0:T(8,128)(2,1)}, u32[]{:S(2)}, u32[]{:S(2)}) %collective-permute-start.10) | collective-permute-done | bytes 524320 | tf_op jit(solution)/shard_map/ppermute | solution.py:397
  30.9 6.0 %shard_map.119 = (bf16[32,128,256]{2,1,0:T(8,128)(2,1)}, f32[512,128]{1,0:T(8,128)}) custom-call(s32[1]{0:T(128)} %bitcast.29.panel_ref, bf16[256,128]{1,0:T(8,128)(2,1)} %filters_ref.1, f32[8,4,128]{2,1,0:T(4,128)} %bitcast.52), custom_call_target="tpu_custom_call" | custom-call | flops 1 | bytes 1 | tf_op jit(solution)/shard_map/pallas_call | solution.py:407
  37.3 4.6 %collective-permute-done.2.refs_5_ = bf16[128,4096]{1,0:T(8,128)(2,1)} collective-permute-done((bf16[128,4096]{1,0:T(8,128)(2,1)}, bf16[128,4096]{1,0:T(8,128)(2,1)}, u32[]{:S(2)}, u32[]{:S(2)}) %collective-permute-start.2) | collective-permute-done | bytes 1048608 | tf_op jit(solution)/shard_map/ppermute | solution.py:403
  43.0 9.3 %collective-permute-start.4 = (bf16[64,4096]{1,0:T(8,128)(2,1)S(1)}, bf16[64,4096]{1,0:T(8,128)(2,1)}, u32[]{:S(2)}, u32[]{:S(2)}) collective-permute-start(bf16[64,4096]{1,0:T(8,128)(2,1)S(1)} %slice.7), channel_id=1, source_target_pairs={{0,3},{1,0},{2,1},{3,2},{4,7},{5,4},{6,5},{7,6},{8,11},{9,8},{10,9... | collective-permute-start | bytes 1572872 | tf_op jit(solution)/shard_map/ppermute | solution.py:415
  52.3 3.7 %collective-permute-start.3 = (bf16[64,4096]{1,0:T(8,128)(2,1)S(1)}, bf16[64,4096]{1,0:T(8,128)(2,1)}, u32[]{:S(2)}, u32[]{:S(2)}) collective-permute-start(bf16[64,4096]{1,0:T(8,128)(2,1)S(1)} %slice.6), channel_id=1, source_target_pairs={{0,1},{1,2},{2,3},{3,0},{4,5},{5,6},{6,7},{7,4},{8,9},{9,10},{10,1... | collective-permute-start | bytes 1572872 | tf_op jit(solution)/shard_map/ppermute | solution.py:414
  56.0 3.1 %collective-permute-start.6 = (bf16[128,4096]{1,0:T(8,128)(2,1)}, bf16[128,4096]{1,0:T(8,128)(2,1)}, u32[]{:S(2)}, u32[]{:S(2)}) collective-permute-start(bf16[128,4096]{1,0:T(8,128)(2,1)} %collective-permute-done.2.refs_5_), channel_id=1, source_target_pairs={{0,3},{1,0},{2,1},{3,2},{4,7},{5,4},{6,5},{7,6},{8,11},{9,8},{10,9... | collective-permute-start | bytes 3145736 | tf_op jit(solution)/shard_map/ppermute | solution.py:417
  59.2 9.8 %collective-permute-done.4.refs_4_ = bf16[64,4096]{1,0:T(8,128)(2,1)} collective-permute-done((bf16[64,4096]{1,0:T(8,128)(2,1)S(1)}, bf16[64,4096]{1,0:T(8,128)(2,1)}, u32[]{:S(2)}, u32[]{:S(2)}) %collective-permute-start.4) | collective-permute-done | bytes 524320 | tf_op jit(solution)/shard_map/ppermute | solution.py:415
  76.2 5.7 %shard_map.120 = (f32[8,512,128]{2,1,0:T(8,128)}, bf16[512,1024]{1,0:T(8,128)(2,1)}) custom-call(s32[8]{0:T(128)} %stack.155.slot_ref, bf16[8,2,512,128]{3,2,1,0:T(8,128)(2,1)} %copy-done, bf16[32,128,256]{2,1,0:T(8,128)(2,1)} %get-tuple-element.40.table_ref.refs_21_, f32[512,128]{1,0:T(8,128)} %get-tuple-element.41.gain_ref.refs_22_), custom_call_target="tpu_custom_call" | custom-call | flops 1 | bytes 1 | tf_op jit(solution)/shard_map/pallas_call | solution.py:423
  84.2 7.4 %collective-permute-done.7.refs_8_ = bf16[64,4096]{1,0:T(8,128)(2,1)} collective-permute-done((bf16[64,4096]{1,0:T(8,128)(2,1)}, bf16[64,4096]{1,0:T(8,128)(2,1)}, u32[]{:S(2)}, u32[]{:S(2)}) %collective-permute-start.7) | collective-permute-done | bytes 524320 | tf_op jit(solution)/shard_map/ppermute | solution.py:418
  91.6 16.4 %shard_map.122 = (bf16[8,512,256]{2,1,0:T(8,128)(2,1)}, bf16[8,512,256]{2,1,0:T(8,128)(2,1)}, bf16[8,512,128]{2,1,0:T(8,128)(2,1)}, bf16[8,2,512,128]{3,2,1,0:T(8,128)(2,1)}) custom-call(s32[1]{0:T(128)} %bitcast.2.core_ref, s32[16]{0:T(128)} %stack.141.w_place_ref, s32[8]{0:T(128)} %stack.150.place_ref, bf16[128,4096]{1,0:T(8,128)(2,1)} %bitcast.27.refs_0_, ...), custom_call_target="tpu_custom_call" | custom-call | flops 1 | bytes 300000000 | tf_op jit(solution)/shard_map/pallas_call | solution.py:431
  108.1 3.6 %all-to-all-start.1 = ((bf16[8,2,512,128]{3,2,1,0:T(8,128)(2,1)}), bf16[8,2,512,128]{3,2,1,0:T(8,128)(2,1)S(1)}, u32[]{:S(2)}, u32[]{:S(2)}) async-start(bf16[8,2,512,128]{3,2,1,0:T(8,128)(2,1)} %get-tuple-element.46), calls=%async_computation.1 | async-start | bytes 4194304 | tf_op jit(solution)/shard_map/all_to_all | solution.py:457
  112.6 3.8 %shard_map.124 = (bf16[2,512,256]{2,1,0:T(8,128)(2,1)}, bf16[2,512,256]{2,1,0:T(8,128)(2,1)}, bf16[2,512,256]{2,1,0:T(8,128)(2,1)}, bf16[2,512,256]{2,1,0:T(8,128)(2,1)}) custom-call(s32[4]{0:T(128)} %pad_add_fusion.1.order_ref, bf16[8,512,256]{2,1,0:T(8,128)(2,1)} %get-tuple-element.50.mine_ref, bf16[8,512,256]{2,1,0:T(8,128)(2,1)} %collective-permute-done.17.other_ref), custom_call_target="tpu_custom_call" | custom-call | flops 1 | bytes 1 | tf_op jit(solution)/shard_map/pallas_call | solution.py:460
  118.0 3.2 %collective-permute-start.19 = (bf16[2,512,256]{2,1,0:T(8,128)(2,1)}, bf16[2,512,256]{2,1,0:T(8,128)(2,1)S(1)}, u32[]{:S(2)}, u32[]{:S(2)}) collective-permute-start(bf16[2,512,256]{2,1,0:T(8,128)(2,1)} %get-tuple-element.54), channel_id=1, source_target_pairs={{0,64},{32,96},{64,0},{96,32},{1,65},{33,97},{65,1},{97,33},{2,66}... | collective-permute-start | bytes 1572872 | tf_op jit(solution)/shard_map/ppermute | solution.py:470
  122.1 6.2 %shard_map.125 = f32[48,128]{1,0:T(8,128)} custom-call(bf16[8,512,128]{2,1,0:T(8,128)(2,1)} %get-tuple-element.57.gm_ref, bf16[8,2,512,128]{3,2,1,0:T(8,128)(2,1)} %copy-done), custom_call_target="tpu_custom_call" | custom-call | flops 1 | bytes 1 | tf_op jit(solution)/shard_map/pallas_call | solution.py:469
  132.3 2.4 %collective-permute-start.24 = (f32[48,128]{1,0:T(8,128)S(1)}, f32[48,128]{1,0:T(8,128)S(1)}, u32[]{:S(2)}, u32[]{:S(2)}) collective-permute-start(f32[48,128]{1,0:T(8,128)S(1)} %add.271.refs_4_), channel_id=1, source_target_pairs={{0,96},{32,0},{64,32},{96,64},{1,97},{33,1},{65,33},{97,65},{2,98}... | collective-permute-start | bytes 73736 | tf_op jit(solution)/shard_map/ppermute | solution.py:473
  136.5 8.8 %collective-permute-done.19.refs_2_ = bf16[2,512,256]{2,1,0:T(8,128)(2,1)S(1)} collective-permute-done((bf16[2,512,256]{2,1,0:T(8,128)(2,1)}, bf16[2,512,256]{2,1,0:T(8,128)(2,1)S(1)}, u32[]{:S(2)}, u32[]{:S(2)}) %collective-permute-start.19) | collective-permute-done | bytes 524320 | tf_op jit(solution)/shard_map/ppermute | solution.py:470
  146.3 2.7 %shard_map.126 = (bf16[560,256]{1,0:T(8,128)(2,1)}, bf16[560,256]{1,0:T(8,128)(2,1)}) custom-call(s32[4]{0:T(128)} %pad_add_fusion.source_ref, s32[1]{0:T(128)} %bitcast.42.zh_ref, bf16[2,512,256]{2,1,0:T(8,128)(2,1)} %get-tuple-element.52.refs_0_, bf16[2,512,256]{2,1,0:T(8,128)(2,1)} %copy-done.3, bf16[2,512,256]{2,1,0:T(8,128)(2,1)} %copy-done.4, ...), custom_call_target="tpu_custom_call" | custom-call | flops 1 | bytes 1 | tf_op jit(solution)/shard_map/pallas_call | solution.py:477
  150.4 4.6 %shard_map.123 = (bf16[128,4096]{1,0:T(8,128)(2,1)}, bf16[128,4096]{1,0:T(8,128)(2,1)}, bf16[128,4096]{1,0:T(8,128)(2,1)}) custom-call(bf16[128,4096]{1,0:T(8,128)(2,1)} %bitcast.48, bf16[128,4096]{1,0:T(8,128)(2,1)} %bitcast.50, bf16[8,2,512,128]{3,2,1,0:T(8,128)(2,1)} %copy-done.1), custom_call_target="tpu_custom_call" | custom-call | flops 1 | bytes 1 | tf_op jit(solution)/shard_map/pallas_call | solution.py:474
  155.0 4.5 %collective-permute-done.25.other_ref = bf16[560,256]{1,0:T(8,128)(2,1)S(1)} collective-permute-done((bf16[560,256]{1,0:T(8,128)(2,1)}, bf16[560,256]{1,0:T(8,128)(2,1)S(1)}, u32[]{:S(2)}, u32[]{:S(2)}) %collective-permute-start.25) | collective-permute-done | bytes 286752 | tf_op jit(solution)/shard_map/ppermute | solution.py:484
  (74 shorter events, 31.8 us)
Async XLA Ops:
  0.6 30.2 %collective-permute-start.1 = (bf16[128,4096]{1,0:T(8,128)(2,1)}, bf16[128,4096]{1,0:T(8,128)(2,1)S(1)}, u32[]{:S(2)}, u32[]{:S(2)}) collective-permute-start(bf16[128,4096]{1,0:T(8,128)(2,1)} %bitcast.27.refs_0_), channel_id=1, source_target_pairs={{0,3},{1,0},{2,1},{3,2},{4,7},{5,4},{6,5},{7,6},{8,11},{9,8},{10,9... | collective-permute-start | bytes 3145736 | tf_op jit(solution)/shard_map/ppermute | solution.py:405
  5.0 31.8 %collective-permute-start = (bf16[128,4096]{1,0:T(8,128)(2,1)}, bf16[128,4096]{1,0:T(8,128)(2,1)}, u32[]{:S(2)}, u32[]{:S(2)}) collective-permute-start(bf16[128,4096]{1,0:T(8,128)(2,1)} %bitcast.27.refs_0_), channel_id=1, source_target_pairs={{0,1},{1,2},{2,3},{3,0},{4,5},{5,6},{6,7},{7,4},{8,9},{9,10},{10,1... | collective-permute-start | bytes 3145736 | tf_op jit(solution)/shard_map/ppermute | solution.py:404
  9.8 32.1 %collective-permute-start.2 = (bf16[128,4096]{1,0:T(8,128)(2,1)}, bf16[128,4096]{1,0:T(8,128)(2,1)}, u32[]{:S(2)}, u32[]{:S(2)}) collective-permute-start(bf16[128,4096]{1,0:T(8,128)(2,1)} %bitcast.27.refs_0_), channel_id=1, source_target_pairs={{0,4},{4,0},{1,5},{5,1},{2,6},{6,2},{3,7},{7,3},{8,12},{12,8},{9,1... | collective-permute-start | bytes 3145736 | tf_op jit(solution)/shard_map/ppermute | solution.py:403
  14.0 13.4 %collective-permute-start.11 = (bf16[2,512,256]{2,1,0:T(8,128)(2,1)}, bf16[2,512,256]{2,1,0:T(8,128)(2,1)}, u32[]{:S(2)}, u32[]{:S(2)}) collective-permute-start(bf16[2,512,256]{2,1,0:T(8,128)(2,1)} %shard_map.121.refs_11_), channel_id=1, source_target_pairs={{0,96},{32,0},{64,32},{96,64},{1,97},{33,1},{65,33},{97,65},{2,98}... | collective-permute-start | bytes 1572872 | tf_op jit(solution)/shard_map/ppermute | solution.py:397
  16.8 14.0 %collective-permute-start.10 = (bf16[2,512,256]{2,1,0:T(8,128)(2,1)}, bf16[2,512,256]{2,1,0:T(8,128)(2,1)}, u32[]{:S(2)}, u32[]{:S(2)}) collective-permute-start(bf16[2,512,256]{2,1,0:T(8,128)(2,1)} %shard_map.121.refs_11_), channel_id=1, source_target_pairs={{0,32},{32,64},{64,96},{96,0},{1,33},{33,65},{65,97},{97,1},{2,34}... | collective-permute-start | bytes 1572872 | tf_op jit(solution)/shard_map/ppermute | solution.py:397
  16.8 58.1 %all-to-all-start = ((bf16[8,2,512,128]{3,2,1,0:T(8,128)(2,1)}), bf16[8,2,512,128]{3,2,1,0:T(8,128)(2,1)S(1)}, u32[]{:S(2)}, u32[]{:S(2)}) async-start(bf16[8,2,512,128]{3,2,1,0:T(8,128)(2,1)} %shard_map.118), calls=%async_computation | async-start | bytes 4194304 | tf_op jit(solution)/shard_map/all_to_all | solution.py:421
  27.4 24.9 %collective-permute-start.13 = (bf16[2,512,256]{2,1,0:T(8,128)(2,1)}, bf16[2,512,256]{2,1,0:T(8,128)(2,1)}, u32[]{:S(2)}, u32[]{:S(2)}) collective-permute-start(bf16[2,512,256]{2,1,0:T(8,128)(2,1)} %shard_map.121.refs_11_), channel_id=1, source_target_pairs={{0,8},{8,0},{1,9},{9,1},{2,10},{10,2},{3,11},{11,3},{4,12},{12,4},... | collective-permute-start | bytes 1572872 | tf_op jit(solution)/shard_map/ppermute | solution.py:400
  30.8 25.2 %collective-permute-start.16 = (bf16[2,512,256]{2,1,0:T(8,128)(2,1)}, bf16[2,512,256]{2,1,0:T(8,128)(2,1)}, u32[]{:S(2)}, u32[]{:S(2)}) collective-permute-start(bf16[2,512,256]{2,1,0:T(8,128)(2,1)} %collective-permute-done.11.refs_14_), channel_id=1, source_target_pairs={{0,8},{8,0},{1,9},{9,1},{2,10},{10,2},{3,11},{11,3},{4,12},{12,4},... | collective-permute-start | bytes 1572872 | tf_op jit(solution)/shard_map/ppermute | solution.py:400
  30.8 28.3 %collective-permute-start.12 = (bf16[2,512,256]{2,1,0:T(8,128)(2,1)}, bf16[2,512,256]{2,1,0:T(8,128)(2,1)}, u32[]{:S(2)}, u32[]{:S(2)}) collective-permute-start(bf16[2,512,256]{2,1,0:T(8,128)(2,1)} %shard_map.121.refs_11_), channel_id=1, source_target_pairs={{0,64},{32,96},{64,0},{96,32},{1,65},{33,97},{65,1},{97,33},{2,66}... | collective-permute-start | bytes 1572872 | tf_op jit(solution)/shard_map/ppermute | solution.py:398
  36.9 22.3 %collective-permute-start.14 = (bf16[2,512,256]{2,1,0:T(8,128)(2,1)}, bf16[2,512,256]{2,1,0:T(8,128)(2,1)}, u32[]{:S(2)}, u32[]{:S(2)}) collective-permute-start(bf16[2,512,256]{2,1,0:T(8,128)(2,1)} %collective-permute-done.10.refs_12_), channel_id=1, source_target_pairs={{0,8},{8,0},{1,9},{9,1},{2,10},{10,2},{3,11},{11,3},{4,12},{12,4},... | collective-permute-start | bytes 1572872 | tf_op jit(solution)/shard_map/ppermute | solution.py:400
  43.0 26.0 %collective-permute-start.4 = (bf16[64,4096]{1,0:T(8,128)(2,1)S(1)}, bf16[64,4096]{1,0:T(8,128)(2,1)}, u32[]{:S(2)}, u32[]{:S(2)}) collective-permute-start(bf16[64,4096]{1,0:T(8,128)(2,1)S(1)} %slice.7), channel_id=1, source_target_pairs={{0,3},{1,0},{2,1},{3,2},{4,7},{5,4},{6,5},{7,6},{8,11},{9,8},{10,9... | collective-permute-start | bytes 1572872 | tf_op jit(solution)/shard_map/ppermute | solution.py:415
  52.3 19.7 %collective-permute-start.3 = (bf16[64,4096]{1,0:T(8,128)(2,1)S(1)}, bf16[64,4096]{1,0:T(8,128)(2,1)}, u32[]{:S(2)}, u32[]{:S(2)}) collective-permute-start(bf16[64,4096]{1,0:T(8,128)(2,1)S(1)} %slice.6), channel_id=1, source_target_pairs={{0,1},{1,2},{2,3},{3,0},{4,5},{5,6},{6,7},{7,4},{8,9},{9,10},{10,1... | collective-permute-start | bytes 1572872 | tf_op jit(solution)/shard_map/ppermute | solution.py:414
  56.0 35.6 %collective-permute-start.6 = (bf16[128,4096]{1,0:T(8,128)(2,1)}, bf16[128,4096]{1,0:T(8,128)(2,1)}, u32[]{:S(2)}, u32[]{:S(2)}) collective-permute-start(bf16[128,4096]{1,0:T(8,128)(2,1)} %collective-permute-done.2.refs_5_), channel_id=1, source_target_pairs={{0,3},{1,0},{2,1},{3,2},{4,7},{5,4},{6,5},{7,6},{8,11},{9,8},{10,9... | collective-permute-start | bytes 3145736 | tf_op jit(solution)/shard_map/ppermute | solution.py:417
  59.1 32.5 %collective-permute-start.5 = (bf16[128,4096]{1,0:T(8,128)(2,1)}, bf16[128,4096]{1,0:T(8,128)(2,1)}, u32[]{:S(2)}, u32[]{:S(2)}) collective-permute-start(bf16[128,4096]{1,0:T(8,128)(2,1)} %collective-permute-done.2.refs_5_), channel_id=1, source_target_pairs={{0,1},{1,2},{2,3},{3,0},{4,5},{5,6},{6,7},{7,4},{8,9},{9,10},{10,1... | collective-permute-start | bytes 3145736 | tf_op jit(solution)/shard_map/ppermute | solution.py:416
  59.1 22.8 %collective-permute-start.15 = (bf16[2,512,256]{2,1,0:T(8,128)(2,1)}, bf16[2,512,256]{2,1,0:T(8,128)(2,1)}, u32[]{:S(2)}, u32[]{:S(2)}) collective-permute-start(bf16[2,512,256]{2,1,0:T(8,128)(2,1)} %collective-permute-done.12.refs_13_), channel_id=1, source_target_pairs={{0,8},{8,0},{1,9},{9,1},{2,10},{10,2},{3,11},{11,3},{4,12},{12,4},... | collective-permute-start | bytes 1572872 | tf_op jit(solution)/shard_map/ppermute | solution.py:400
  69.0 15.2 %collective-permute-start.8 = (bf16[64,4096]{1,0:T(8,128)(2,1)}, bf16[64,4096]{1,0:T(8,128)(2,1)}, u32[]{:S(2)}, u32[]{:S(2)}) collective-permute-start(bf16[64,4096]{1,0:T(8,128)(2,1)} %collective-permute-done.4.refs_4_), channel_id=1, source_target_pairs={{0,4},{4,0},{1,5},{5,1},{2,6},{6,2},{3,7},{7,3},{8,12},{12,8},{9,1... | collective-permute-start | bytes 1572872 | tf_op jit(solution)/shard_map/ppermute | solution.py:419
  72.0 19.6 %collective-permute-start.7 = (bf16[64,4096]{1,0:T(8,128)(2,1)}, bf16[64,4096]{1,0:T(8,128)(2,1)}, u32[]{:S(2)}, u32[]{:S(2)}) collective-permute-start(bf16[64,4096]{1,0:T(8,128)(2,1)} %collective-permute-done.3.refs_3_), channel_id=1, source_target_pairs={{0,4},{4,0},{1,5},{5,1},{2,6},{6,2},{3,7},{7,3},{8,12},{12,8},{9,1... | collective-permute-start | bytes 1572872 | tf_op jit(solution)/shard_map/ppermute | solution.py:418
  108.1 40.9 %all-to-all-start.1 = ((bf16[8,2,512,128]{3,2,1,0:T(8,128)(2,1)}), bf16[8,2,512,128]{3,2,1,0:T(8,128)(2,1)S(1)}, u32[]{:S(2)}, u32[]{:S(2)}) async-start(bf16[8,2,512,128]{3,2,1,0:T(8,128)(2,1)} %get-tuple-element.46), calls=%async_computation.1 | async-start | bytes 4194304 | tf_op jit(solution)/shard_map/all_to_all | solution.py:457
  116.4 15.9 %collective-permute-start.18 = (bf16[2,512,256]{2,1,0:T(8,128)(2,1)}, bf16[2,512,256]{2,1,0:T(8,128)(2,1)S(1)}, u32[]{:S(2)}, u32[]{:S(2)}) collective-permute-start(bf16[2,512,256]{2,1,0:T(8,128)(2,1)} %get-tuple-element.53), channel_id=1, source_target_pairs={{0,32},{32,64},{64,96},{96,0},{1,33},{33,65},{65,97},{97,1},{2,34}... | collective-permute-start | bytes 1572872 | tf_op jit(solution)/shard_map/ppermute | solution.py:470
  118.0 27.3 %collective-permute-start.19 = (bf16[2,512,256]{2,1,0:T(8,128)(2,1)}, bf16[2,512,256]{2,1,0:T(8,128)(2,1)S(1)}, u32[]{:S(2)}, u32[]{:S(2)}) collective-permute-start(bf16[2,512,256]{2,1,0:T(8,128)(2,1)} %get-tuple-element.54), channel_id=1, source_target_pairs={{0,64},{32,96},{64,0},{96,32},{1,65},{33,97},{65,1},{97,33},{2,66}... | collective-permute-start | bytes 1572872 | tf_op jit(solution)/shard_map/ppermute | solution.py:470
  121.2 24.1 %collective-permute-start.20 = (bf16[2,512,256]{2,1,0:T(8,128)(2,1)}, bf16[2,512,256]{2,1,0:T(8,128)(2,1)S(1)}, u32[]{:S(2)}, u32[]{:S(2)}) collective-permute-start(bf16[2,512,256]{2,1,0:T(8,128)(2,1)} %get-tuple-element.55), channel_id=1, source_target_pairs={{0,96},{32,0},{64,32},{96,64},{1,97},{33,1},{65,33},{97,65},{2,98}... | collective-permute-start | bytes 1572872 | tf_op jit(solution)/shard_map/ppermute | solution.py:470
  132.3 13.0 %collective-permute-start.24 = (f32[48,128]{1,0:T(8,128)S(1)}, f32[48,128]{1,0:T(8,128)S(1)}, u32[]{:S(2)}, u32[]{:S(2)}) collective-permute-start(f32[48,128]{1,0:T(8,128)S(1)} %add.271.refs_4_), channel_id=1, source_target_pairs={{0,96},{32,0},{64,32},{96,64},{1,97},{33,1},{65,33},{97,65},{2,98}... | collective-permute-start | bytes 73736 | tf_op jit(solution)/shard_map/ppermute | solution.py:473
  134.7 10.9 %collective-permute-start.23 = (f32[48,128]{1,0:T(8,128)S(1)}, f32[48,128]{1,0:T(8,128)S(1)}, u32[]{:S(2)}, u32[]{:S(2)}) collective-permute-start(f32[48,128]{1,0:T(8,128)S(1)} %add.271.refs_4_), channel_id=1, source_target_pairs={{0,64},{32,96},{64,0},{96,32},{1,65},{33,97},{65,1},{97,33},{2,66}... | collective-permute-start | bytes 73736 | tf_op jit(solution)/shard_map/ppermute | solution.py:473
  135.0 10.7 %collective-permute-start.22 = (f32[48,128]{1,0:T(8,128)S(1)}, f32[48,128]{1,0:T(8,128)S(1)}, u32[]{:S(2)}, u32[]{:S(2)}) collective-permute-start(f32[48,128]{1,0:T(8,128)S(1)} %add.271.refs_4_), channel_id=1, source_target_pairs={{0,32},{32,64},{64,96},{96,0},{1,33},{33,65},{65,97},{97,1},{2,34}... | collective-permute-start | bytes 73736 | tf_op jit(solution)/shard_map/ppermute | solution.py:473
  (16 other events, 114.6 us)
